TPU v7x, 32 devices: a whole 2x2x4 slice. The times are simulated.
32 devices in a mesh: parts: 2 (over y), dp: 8 (over z, x), tensor: 2 (over core).
Axes of the slice: x: 2, y: 2, z: 4, core: 2. Of those that a mesh axis runs over, the one named last changes fastest.
Arguments:
- features: bfloat16 [2048, 8192], P(('parts', 'dp'), 'tensor'), parts along dimension 0, may hold values from -6 to 6
- cotangent: bfloat16 [2048, 8192], P(('parts', 'dp'), 'tensor'), parts along dimension 0, may hold values from -6 to 6
- tenant_ids: int32 [2048], P(('parts', 'dp')), parts along dimension 0, may hold values from 0 to 7, as said below
- document_index_per_token: int32 [2048], P(('parts', 'dp')), parts along dimension 0, may hold values from 0 to 1023, as said below
- owner_map: int32 [8], replicated, may hold values from 0 to 7, each once
- adapter_down: bfloat16 [8, 32, 8192], P('dp', None, 'tensor'), may hold values from -0.25 to 0.25
- adapter_up: bfloat16 [8, 32, 8192], P('dp', None, 'tensor'), may hold values from -0.0625 to 0.0625
Outputs:
- input_grad: bfloat16 [2048, 8192], P(('parts', 'dp'), 'tensor'), parts along dimension 0
- grad_down: float32 [16, 32, 8192], P(('parts', 'dp'), None, 'tensor'), parts along dimension 0
- up_adapter_gradient: float32 [16, 32, 8192], P(('parts', 'dp'), None, 'tensor'), parts along dimension 0
There are 2 independent parts, one for each index of `parts`. A program takes and returns all parts, laid end to end along the dimension named above; an argument that names none is the same for every part. Nothing has to cross between parts.
Inputs may be any that keep to these rules, and one draw needn't show every extreme that they name: `tenant_ids`: each tenant's tokens are contiguous within one device's 128 rows, and no tenant has more than 32 of them there; in every draw one tenant has exactly 32 tokens in every device's rows. `document_index_per_token`: never falling; a document's number is the position of its first token; each document lies within one device's rows and within one tenant's tokens; the last token is a document of its own.
All inputs are finite; a program needn't handle non-finite values.
Results may differ from a plain program's by a relative error of at most 0.005.
Values may be sent and summed in bfloat16 or wider, within the bound.
No kernel may reach another device: no remote copies, remote signals or barrier semaphores. Data moves between devices by JAX's collectives and lax.ppermute only.
A program may use at most 64 MiB of HBM per device.

v0:
```python
import jax
import jax.numpy as jnp
from jax import lax
from jax.sharding import PartitionSpec as P

adapter_scale_factor = 2.0


def contract_last(left, right):
    return lax.dot_general(
        left, right, (((1,), (1,)), ((), ())), preferred_element_type=jnp.float32
    )


def contract_first(left, right):
    return lax.dot_general(
        left, right, (((0,), (0,)), ((), ())), preferred_element_type=jnp.float32
    )


def shards(
    features, cotangent, tenant_ids, document_index_per_token, owner_map, adapter_down, adapter_up
):
    ranks = lax.axis_size("dp")
    rows = features.shape[0]
    width = features.shape[1]
    capacity = max(2, 2 * rows // ranks)
    slots = ranks * capacity
    tenant_total = owner_map.shape[0]
    token_row_index = jnp.arange(rows, dtype=jnp.int32)
    match = tenant_ids[:, None] == jnp.arange(tenant_total, dtype=jnp.int32)[None, :]
    target = jnp.sum(jnp.where(match, owner_map[None, :], 0), axis=1)
    same_doc = document_index_per_token[:, None] == document_index_per_token[None, :]
    sequence_length = jnp.sum(same_doc.astype(jnp.float32), axis=1)
    routing_weight = adapter_scale_factor / sequence_length
    earlier = (token_row_index[:, None] > token_row_index[None, :]) & (
        target[:, None] == target[None, :]
    )
    before = jnp.sum(earlier.astype(jnp.int32), axis=1)
    slot_of = target * capacity + before
    placed = slot_of[None, :] == jnp.arange(slots, dtype=jnp.int32)[:, None]
    slot_weight = jnp.sum(
        jnp.where(placed, routing_weight[None, :], jnp.zeros_like(routing_weight)[None, :]), axis=1
    )

    def pack(values):
        return jnp.dot(
            placed.astype(values.dtype), values, preferred_element_type=jnp.float32
        ).astype(values.dtype)

    down_own = adapter_down[0]
    up_own = adapter_up[0]
    got_x, got_g, got_w = (
        lax.all_to_all(
            pack(features).reshape(ranks, capacity, width),
            "dp",
            split_axis=0,
            concat_axis=0,
            tiled=True,
        ),
        lax.all_to_all(
            pack(cotangent).reshape(ranks, capacity, width),
            "dp",
            split_axis=0,
            concat_axis=0,
            tiled=True,
        ),
        lax.all_to_all(
            slot_weight.reshape(ranks, capacity).astype(jnp.bfloat16),
            "dp",
            split_axis=0,
            concat_axis=0,
            tiled=True,
        ).astype(jnp.float32),
    )
    got_x = got_x.reshape(slots, width)
    got_g = got_g.reshape(slots, width)
    low_h, low_u = lax.psum(
        (contract_last(got_x, down_own), contract_last(got_g, up_own)), "tensor"
    )
    got_w = got_w.reshape(slots)
    scaled_h = (low_h * got_w[:, None]).astype(jnp.bfloat16)
    scaled_u = (low_u * got_w[:, None]).astype(jnp.bfloat16)
    up_adapter_gradient = contract_first(scaled_h, got_g)
    grad_down = contract_first(scaled_u, got_x)
    slot_dx = jnp.dot(scaled_u, down_own, preferred_element_type=jnp.float32).astype(jnp.bfloat16)
    returned = lax.all_to_all(
        slot_dx.reshape(ranks, capacity, width), "dp", split_axis=0, concat_axis=0, tiled=True
    ).reshape(slots, width)
    input_grad = contract_first(placed.astype(jnp.bfloat16), returned).astype(jnp.bfloat16)
    return (input_grad, grad_down[None], up_adapter_gradient[None])


def solution(mesh):
    return jax.shard_map(
        shards,
        mesh=mesh,
        in_specs=(
            P(("parts", "dp"), "tensor"),
            P(("parts", "dp"), "tensor"),
            P(("parts", "dp")),
            P(("parts", "dp")),
            P(),
            P("dp", None, "tensor"),
            P("dp", None, "tensor"),
        ),
        out_specs=(
            P(("parts", "dp"), "tensor"),
            P(("parts", "dp"), None, "tensor"),
            P(("parts", "dp"), None, "tensor"),
        ),
        check_vma=False,
    )
```

profile of v0, /device:TPU:0, one launch (start us, length us, event | category | flops | bytes accessed | tf_op | source)
XLA Modules:
  0.0 212.3 jit_solution(8856832212241859197)
XLA Ops:
  7.2 0.0 copy-start
  7.2 0.8 select_reduce_fusion.1
  8.0 0.2 convert_reduce_fusion.1
  8.2 0.2 copy-done
  8.4 2.0 convolution_convert_fusion
  10.5 7.3 %all-to-all-start.3 = ((bf16[8,32,4096]{2,1,0:T(8,128)(2,1)}), bf16[8,32,4096]{2,1,0:T(8,128)(2,1)S(1)}, u32[]{:S(2)}, u32[]{:S(2)}) async-start(bf16[8,32,4096]{2,1,0:T(8,128)(2,1)} %bitcast.29), calls=%async_computation.3 | async-start | bytes 4194304 | tf_op jit(solution)/shard_map/all_to_all | solution.py:54
  17.7 3.2 %convolution_convert_fusion.1 = bf16[256,4096]{1,0:T(8,128)(2,1)} fusion(bf16[128,4096]{1,0:T(8,128)(2,1)} %param.8, s32[128]{0:T(128)S(1)} %multiply_add_fusion), kind=kOutput, calls=%fused_computation.1 | convolution fusion | flops 269516800 | bytes 3146240 | tf_op jit(solution)/shard_map/dot_general | solution.py:47
  21.0 45.0 %all-to-all-done.3 = bf16[8,32,4096]{2,1,0:T(8,128)(2,1)S(1)} async-done(((bf16[8,32,4096]{2,1,0:T(8,128)(2,1)}), bf16[8,32,4096]{2,1,0:T(8,128)(2,1)S(1)}, u32[]{:S(2)}, u32[]{:S(2)}) %all-to-all-start.3) | async-done | bytes 2097184 | tf_op jit(solution)/shard_map/all_to_all | solution.py:54
  66.0 0.0 copy-start.4
  66.0 0.0 copy-start.1
  66.0 4.5 %all-to-all-start = ((bf16[8,32,4096]{2,1,0:T(8,128)(2,1)}), bf16[8,32,4096]{2,1,0:T(8,128)(2,1)}, u32[]{:S(2)}, u32[]{:S(2)}) async-start(bf16[8,32,4096]{2,1,0:T(8,128)(2,1)} %bitcast.27), calls=%async_computation | async-start | bytes 4194304 | tf_op jit(solution)/shard_map/all_to_all | solution.py:61
  70.4 0.0 copy-done.4
  70.5 0.2 convert_reduce_fusion
  70.6 0.1 select_reduce_fusion
  70.8 0.7 convert_element_type.63
  71.5 0.0 copy-done.1
  71.5 1.4 fusion
  72.8 45.5 %all-to-all-done = bf16[8,32,4096]{2,1,0:T(8,128)(2,1)} async-done(((bf16[8,32,4096]{2,1,0:T(8,128)(2,1)}), bf16[8,32,4096]{2,1,0:T(8,128)(2,1)}, u32[]{:S(2)}, u32[]{:S(2)}) %all-to-all-start) | async-done | bytes 2097184 | tf_op jit(solution)/shard_map/all_to_all | solution.py:61
  118.3 3.6 %all-to-all-start.1 = ((bf16[8,1,32]{2,1,0:T(2,128)(2,1)}), bf16[8,1,32]{2,1,0:T(2,128)(2,1)S(1)}, u32[]{:S(2)}, u32[]{:S(2)}) async-start(bf16[8,1,32]{2,1,0:T(2,128)(2,1)} %convert_element_type.63), calls=%async_computation.1 | async-start | bytes 8192 | tf_op jit(solution)/shard_map/all_to_all | solution.py:68
  121.9 0.0 all-reduce.3.cloned.1.call-start
  121.9 2.9 %fusion.3 = f32[256,32]{0,1:T(8,128)} fusion(bf16[256,4096]{1,0:T(8,128)(2,1)} %bitcast.1, bf16[1,32,4096]{2,1,0:T(8,128)(2,1)} %param.13), kind=kOutput, calls=%fused_computation.9 | convolution fusion | flops 67108864 | bytes 2392064 | tf_op jit(solution)/shard_map/dot_general | solution.py:10
  124.9 0.0 all-reduce.3.cloned.1.call-update
  124.9 3.4 %all-to-all-done.1 = bf16[8,1,32]{2,1,0:T(2,128)(2,1)S(1)} async-done(((bf16[8,1,32]{2,1,0:T(2,128)(2,1)}), bf16[8,1,32]{2,1,0:T(2,128)(2,1)S(1)}, u32[]{:S(2)}, u32[]{:S(2)}) %all-to-all-start.1) | async-done | bytes 544 | tf_op jit(solution)/shard_map/all_to_all | solution.py:68
  128.3 0.1 reshape.66
  128.4 16.5 %all-reduce.3.cloned.1.call-done = (f32[256,32]{0,1:T(8,128)}, f32[256,32]{0,1:T(8,128)}) async-done(((f32[256,32]{0,1:T(8,128)}, f32[256,32]{0,1:T(8,128)}), (f32[256,32]{0,1:T(8,128)}, f32[256,32]{0,1:T(8,128)})) %all-reduce.3.cloned.1.call-update) | async-done | bytes 65552 | tf_op jit(solution)/shard_map/psum | solution.py:78
  144.9 2.8 %convolution_convert_fusion.2 = bf16[256,4096]{1,0:T(8,128)(2,1)} fusion(bf16[1,32,4096]{2,1,0:T(8,128)(2,1)S(1)} %copy-done.1, f32[256,32]{0,1:T(8,128)} %get-tuple-element.3, f32[256]{0:T(256)S(1)} %reshape.66), kind=kOutput, calls=%fused_computation.2 | convolution fusion | flops 68173824 | bytes 2393088 | tf_op jit(solution)/shard_map/dot_general | solution.py:86
  147.7 0.0 copy-start.2
  147.7 5.9 %all-to-all-start.2 = ((bf16[8,32,4096]{2,1,0:T(8,128)(2,1)}), bf16[8,32,4096]{2,1,0:T(8,128)(2,1)}, u32[]{:S(2)}, u32[]{:S(2)}) async-start(bf16[8,32,4096]{2,1,0:T(8,128)(2,1)} %bitcast.28), calls=%async_computation.2 | async-start | bytes 4194304 | tf_op jit(solution)/shard_map/all_to_all | solution.py:87
  153.6 0.0 copy-done.2
  153.6 0.0 copy-start.3
  153.6 1.3 convolution_bitcast_fusion.1
  154.9 0.0 copy-done.3
  154.9 2.9 %convolution_bitcast_fusion = f32[1,32,4096]{2,1,0:T(8,128)} fusion(bf16[256,4096]{1,0:T(8,128)(2,1)} %bitcast.1, f32[256,32]{0,1:T(8,128)S(1)} %copy-done.3, f32[256]{0:T(256)S(1)} %reshape.66), kind=kOutput, calls=%fused_computation.4 | convolution fusion | flops 67125248 | bytes 2655232 | tf_op jit(solution)/shard_map/dot_general | solution.py:16
  157.7 44.7 %all-to-all-done.2 = bf16[8,32,4096]{2,1,0:T(8,128)(2,1)} async-done(((bf16[8,32,4096]{2,1,0:T(8,128)(2,1)}), bf16[8,32,4096]{2,1,0:T(8,128)(2,1)}, u32[]{:S(2)}, u32[]{:S(2)}) %all-to-all-start.2) | async-done | bytes 2097184 | tf_op jit(solution)/shard_map/all_to_all | solution.py:87
  202.4 3.1 %convolution_convert_fusion.3 = bf16[128,4096]{1,0:T(8,128)(2,1)} fusion(bf16[256,4096]{1,0:T(8,128)(2,1)} %bitcast.5, s32[128]{0:T(128)S(1)} %multiply_add_fusion), kind=kOutput, calls=%fused_computation.3 | convolution fusion | flops 268992512 | bytes 3146240 | tf_op jit(solution)/shard_map/dot_general | solution.py:16
  (3 shorter events, 0.0 us)
Async XLA Ops:
  7.2 1.3 copy-start
  10.5 55.5 %all-to-all-start.3 = ((bf16[8,32,4096]{2,1,0:T(8,128)(2,1)}), bf16[8,32,4096]{2,1,0:T(8,128)(2,1)S(1)}, u32[]{:S(2)}, u32[]{:S(2)}) async-start(bf16[8,32,4096]{2,1,0:T(8,128)(2,1)} %bitcast.29), calls=%async_computation.3 | async-start | bytes 4194304 | tf_op jit(solution)/shard_map/all_to_all | solution.py:54
  66.0 4.5 %copy-start.4 = (s32[128]{0:T(128)S(1)}, s32[128]{0:T(128)}, u32[]{:S(2)}) copy-start(s32[128]{0:T(128)} %param.10) | copy-start | bytes 1540
  66.0 5.5 %copy-start.1 = (bf16[1,32,4096]{2,1,0:T(8,128)(2,1)S(1)}, bf16[1,32,4096]{2,1,0:T(8,128)(2,1)}, u32[]{:S(2)}) copy-start(bf16[1,32,4096]{2,1,0:T(8,128)(2,1)} %param.12) | copy-start | bytes 786436
  66.0 52.3 %all-to-all-start = ((bf16[8,32,4096]{2,1,0:T(8,128)(2,1)}), bf16[8,32,4096]{2,1,0:T(8,128)(2,1)}, u32[]{:S(2)}, u32[]{:S(2)}) async-start(bf16[8,32,4096]{2,1,0:T(8,128)(2,1)} %bitcast.27), calls=%async_computation | async-start | bytes 4194304 | tf_op jit(solution)/shard_map/all_to_all | solution.py:61
  118.3 10.0 %all-to-all-start.1 = ((bf16[8,1,32]{2,1,0:T(2,128)(2,1)}), bf16[8,1,32]{2,1,0:T(2,128)(2,1)S(1)}, u32[]{:S(2)}, u32[]{:S(2)}) async-start(bf16[8,1,32]{2,1,0:T(2,128)(2,1)} %convert_element_type.63), calls=%async_computation.1 | async-start | bytes 8192 | tf_op jit(solution)/shard_map/all_to_all | solution.py:68
  121.9 23.0 %all-reduce.3.cloned.1.call-start = ((), (), s32[]{:S(2)}) async-start(), calls=%async_computation.4 | async-start | bytes 131072 | tf_op jit(solution)/shard_map/psum | solution.py:78
  147.7 5.9 %copy-start.2 = (f32[256,32]{0,1:T(8,128)S(1)}, f32[256,32]{0,1:T(8,128)}, u32[]{:S(2)}) copy-start(f32[256,32]{0,1:T(8,128)} %get-tuple-element.3) | copy-start | bytes 98308
  147.7 54.7 %all-to-all-start.2 = ((bf16[8,32,4096]{2,1,0:T(8,128)(2,1)}), bf16[8,32,4096]{2,1,0:T(8,128)(2,1)}, u32[]{:S(2)}, u32[]{:S(2)}) async-start(bf16[8,32,4096]{2,1,0:T(8,128)(2,1)} %bitcast.28), calls=%async_computation.2 | async-start | bytes 4194304 | tf_op jit(solution)/shard_map/all_to_all | solution.py:87
  153.6 1.3 copy-start.3
Sparse Core Ops, SparseCore 0:
  125.6 19.1 all-reduce.2
where the time goes:
time: 213 us; the launch traced here: 212 us
  waiting for transfers between devices  155 us (73%)
  starting transfers between devices  21.3 us (10%)
  matrix products  19.5 us (9%)
  between operations  14.1 us (7%)
    all_to_all x1, waiting for transfers between devices, shards(): lax.all_to_all(pack(cotangent).reshape(ranks, capacity, width), 'dp', spl...  45.5 us
    all_to_all x1, waiting for transfers between devices, shards(): lax.all_to_all(pack(features).reshape(ranks, capacity, width), 'dp', spli...  45 us
    all_to_all x1, waiting for transfers between devices, shards(): lax.all_to_all(slot_dx.reshape(ranks, capacity, width), 'dp', split_axis=...  44.7 us
    psum x1, waiting for transfers between devices, shards(): lax.psum((contract_last(got_x, down_own), contract_last(got_g, up_own)),...  16.5 us
    all_to_all x1, starting transfers between devices, shards(): lax.all_to_all(pack(features).reshape(ranks, capacity, width), 'dp', spli...  7.25 us
    dot_general x3, matrix products, contract_first(): lax.dot_general(left, right, (((0,), (0,)), ((), ())), preferred_element_...  7.17 us
    all_to_all x1, starting transfers between devices, shards(): lax.all_to_all(slot_dx.reshape(ranks, capacity, width), 'dp', split_axis=...  5.91 us
    dot_general x2, matrix products, pack(): jnp.dot(placed.astype(values.dtype), values, preferred_element_type=jnp.f...  5.27 us
  transfers between devices with their start and end apart: 5, of which 5 were waited for; matrix products, arithmetic and copies ran while one was open for 6% of the time, Pallas kernels for 0%

commit v1 on v0

v1 whole, which is shorter than its diff:
```python
import jax
import jax.numpy as jnp
from jax import lax
from jax.sharding import PartitionSpec as P

adapter_scale_factor = 2.0


def contract_last(left, right):
    return lax.dot_general(
        left, right, (((1,), (1,)), ((), ())), preferred_element_type=jnp.float32
    )


def contract_first(left, right):
    return lax.dot_general(
        left, right, (((0,), (0,)), ((), ())), preferred_element_type=jnp.float32
    )


def token_owner(tenant_ids, owner_map):
    tenant_total = owner_map.shape[0]
    match = tenant_ids[:, None] == jnp.arange(tenant_total, dtype=jnp.int32)[None, :]
    return jnp.sum(jnp.where(match, owner_map[None, :], 0), axis=1)


def token_weight(document_index_per_token):
    same_doc = document_index_per_token[:, None] == document_index_per_token[None, :]
    sequence_length = jnp.sum(same_doc.astype(jnp.float32), axis=1)
    return adapter_scale_factor / sequence_length


def route_tokens(
    features, cotangent, tenant_ids, document_index_per_token, owner_map, adapter_down, adapter_up
):
    ranks = lax.axis_size("dp")
    rows = features.shape[0]
    width = features.shape[1]
    capacity = max(2, 2 * rows // ranks)
    slots = ranks * capacity
    token_row_index = jnp.arange(rows, dtype=jnp.int32)
    target = token_owner(tenant_ids, owner_map)
    routing_weight = token_weight(document_index_per_token)
    earlier = (token_row_index[:, None] > token_row_index[None, :]) & (
        target[:, None] == target[None, :]
    )
    before = jnp.sum(earlier.astype(jnp.int32), axis=1)
    slot_of = target * capacity + before
    placed = slot_of[None, :] == jnp.arange(slots, dtype=jnp.int32)[:, None]
    slot_weight = jnp.sum(
        jnp.where(placed, routing_weight[None, :], jnp.zeros_like(routing_weight)[None, :]), axis=1
    )

    def pack(values):
        return jnp.dot(
            placed.astype(values.dtype), values, preferred_element_type=jnp.float32
        ).astype(values.dtype)

    def exchange(values):
        return lax.all_to_all(values, "dp", split_axis=0, concat_axis=0, tiled=True)

    down_own = adapter_down[0]
    up_own = adapter_up[0]
    got_x = exchange(pack(features).reshape(ranks, capacity, width)).reshape(slots, width)
    got_g = exchange(pack(cotangent).reshape(ranks, capacity, width)).reshape(slots, width)
    got_w = exchange(slot_weight.reshape(ranks, capacity)).reshape(slots)
    low_h, low_u = lax.psum(
        (contract_last(got_x, down_own), contract_last(got_g, up_own)), "tensor"
    )
    scaled_h = (low_h * got_w[:, None]).astype(jnp.bfloat16)
    scaled_u = (low_u * got_w[:, None]).astype(jnp.bfloat16)
    up_adapter_gradient = contract_first(scaled_h, got_g)
    grad_down = contract_first(scaled_u, got_x)
    slot_dx = jnp.dot(scaled_u, down_own, preferred_element_type=jnp.float32).astype(jnp.bfloat16)
    returned = exchange(slot_dx.reshape(ranks, capacity, width)).reshape(slots, width)
    input_grad = contract_first(placed.astype(jnp.bfloat16), returned).astype(jnp.bfloat16)
    return (input_grad, grad_down[None], up_adapter_gradient[None])


def route_adapters(
    features, cotangent, tenant_ids, document_index_per_token, owner_map, adapter_down, adapter_up
):
    ranks = lax.axis_size("dp")
    columns = ranks // 2
    rows, width = features.shape
    rank = adapter_down.shape[1]
    half = rank // 2
    me = lax.axis_index("dp")
    side, place = me % 2, me // 2
    layer = lax.axis_index("parts")

    def swap_side(value):
        return lax.ppermute(value, "dp", [(i, i ^ 1) for i in range(ranks)])

    def shift(value, by):
        return lax.ppermute(value, "dp", [(i, (i + 2 * by) % ranks) for i in range(ranks)])

    def swap_layer(value):
        return lax.ppermute(value, "parts", [(0, 1), (1, 0)])

    def swap_core(value):
        return lax.ppermute(value, "tensor", [(0, 1), (1, 0)])

    def column_adapters(own):
        mine = lax.dynamic_slice(own, (layer * half, 0), (half, width))
        blocks = [own]
        for step in range(1, columns):
            got = shift(mine, -step)
            other = swap_layer(got)
            blocks.append(
                jnp.where(
                    layer == 0, jnp.concatenate([got, other]), jnp.concatenate([other, got])
                )
            )
        return jnp.concatenate(blocks)

    owner = token_owner(tenant_ids, owner_map)
    weight = token_weight(document_index_per_token)
    facts = jnp.stack([owner.astype(jnp.float32), weight])
    facts = jnp.concatenate([facts, swap_side(facts)], axis=1)
    owner_here = facts[0].astype(jnp.int32)
    weight_here = facts[1]
    steps = jnp.arange(columns, dtype=jnp.int32)
    block_owner = ((place + steps) % columns) * 2 + side
    block_owner_there = block_owner + 1 - 2 * side
    held = (block_owner[:, None] == owner_here[None, :])[:, None, :]
    own_held = (block_owner[:, None] == owner[None, :])[:, None, :]
    own_there = (block_owner_there[:, None] == owner[None, :])[:, None, :]

    def spread(low, mask):
        return jnp.where(mask, low[None], jnp.zeros((), low.dtype)).reshape(
            mask.shape[0] * rank, low.shape[1]
        )

    def project(adapters, own_rows, other_rows):
        low = jnp.concatenate(
            [contract_last(adapters, own_rows), contract_last(adapters, other_rows)], axis=1
        ).reshape(columns, rank, 2 * rows)
        low = jnp.sum(jnp.where(held, low, 0.0), axis=0)
        low = low + swap_core(low)
        return (low * weight_here[None, :]).astype(jnp.bfloat16)

    def gradient(scaled, own_rows, other_rows, pieces):
        left = spread(scaled, held)
        wide = width // pieces
        parts = []
        for piece in range(pieces):
            cut = slice(piece * wide, (piece + 1) * wide)
            total = jnp.dot(
                left[:, :rows], own_rows[:, cut], preferred_element_type=jnp.float32
            ) + jnp.dot(left[:, rows:], other_rows[piece], preferred_element_type=jnp.float32)
            sum_own = total[:rank]
            for step in range(1, columns):
                block = total[step * rank : (step + 1) * rank].astype(jnp.bfloat16)
                sum_own = sum_own + shift(block, step).astype(jnp.float32)
            parts.append(sum_own)
        return jnp.concatenate(parts, axis=1)

    pieces = 2
    wide = width // pieces
    other_x = [swap_side(features[:, i * wide : (i + 1) * wide]) for i in range(pieces)]
    down = column_adapters(adapter_down[0])
    up = column_adapters(adapter_up[0])
    other_g = [swap_side(cotangent[:, i * wide : (i + 1) * wide]) for i in range(pieces)]
    scaled_h = project(down, features, jnp.concatenate(other_x, axis=1))
    up_adapter_gradient = gradient(scaled_h, cotangent, other_g, pieces)
    scaled_u = project(up, cotangent, jnp.concatenate(other_g, axis=1))
    grad_down = gradient(scaled_u, features, other_x, pieces)
    down_there = swap_side(down)
    back = swap_side(scaled_u[:, rows:])
    left = jnp.concatenate([spread(scaled_u[:, :rows], own_held), spread(back, own_there)])
    input_grad = contract_first(left, jnp.concatenate([down, down_there])).astype(jnp.bfloat16)
    return (input_grad, grad_down[None], up_adapter_gradient[None])


def shards(features, *others):
    ranks = lax.axis_size("dp")
    rank = others[-1].shape[1]
    slots = 2 * features.shape[0] // ranks
    if slots >= rank and ranks % 2 == 0 and rank % 32 == 0 and lax.axis_size("parts") == 2:
        return route_adapters(features, *others)
    return route_tokens(features, *others)


def solution(mesh):
    return jax.shard_map(
        shards,
        mesh=mesh,
        in_specs=(
            P(("parts", "dp"), "tensor"),
            P(("parts", "dp"), "tensor"),
            P(("parts", "dp")),
            P(("parts", "dp")),
            P(),
            P("dp", None, "tensor"),
            P("dp", None, "tensor"),
        ),
        out_specs=(
            P(("parts", "dp"), "tensor"),
            P(("parts", "dp"), None, "tensor"),
            P(("parts", "dp"), None, "tensor"),
        ),
        check_vma=False,
    )
```

time: 213 us -> 141 us (0.66)
  waiting for transfers between devices: 155 us -> 69.6 us
  starting transfers between devices: 21.3 us -> 44.3 us
  between operations: 14.1 us -> 1.1 us
  matrix products: 19.5 us -> 9.72 us
  local copies, waits for them, and re-layouts: 1 us -> 8.86 us
  other arithmetic: 1.34 us -> 6.94 us
    all_to_all x4 -> x0, waiting for transfers between devices: 139 us -> none  [the longest x1 45.5 us: shards(): lax.all_to_all(pack(cotangent).reshape(ranks, capacity, width), 'dp', spl...]
    ppermute x0 -> x33, waiting for transfers between devices: none -> 69.6 us  [the longest x7 31.5 us: swap_side(): return lax.ppermute(value, 'dp', [(i, i ^ 1) for i in range(ranks)])]
    ppermute x0 -> x33, starting transfers between devices: none -> 44.3 us  [the longest x18 28.6 us: shift(): lax.ppermute(value, 'dp', [(i, (i + 2 * by) % ranks) for i in range(ranks)])]
    all_to_all x4 -> x0, starting transfers between devices: 21.3 us -> none  [the longest x1 7.25 us: shards(): lax.all_to_all(pack(features).reshape(ranks, capacity, width), 'dp', spli...]
    psum x1 -> x0, waiting for transfers between devices: 16.5 us -> none  [shards(): lax.psum((contract_last(got_x, down_own), contract_last(got_g, up_own)),...]
    dot_general x3 -> x1, matrix products: 7.17 us -> 1.45 us  [contract_first(): lax.dot_general(left, right, (((0,), (0,)), ((), ())), preferred_element_...]
    dot_general x3 -> x8, matrix products: 8.08 us -> 4.36 us  [the longest x4 3.23 us: gradient(): jnp.dot(left[:, rows:], other_rows[piece], preferred_element_type=jnp.flo...]
    slice x0 -> x7, local copies, waits for them, and re-layouts: none -> 3.46 us  [the longest x1 2.27 us: gradient(): own_rows[:, cut]]
  transfers between devices with their start and end apart: 5 -> 33, of which waited for: 5 -> 13; matrix products, arithmetic and copies ran while one was open for 6% -> 14% of each run, Pallas kernels for 0% -> 0%
where the time goes in v1:
time: 141 us
  waiting for transfers between devices  69.6 us (49%)
  starting transfers between devices  44.3 us (31%)
  matrix products  9.72 us (7%)
  local copies, waits for them, and re-layouts  8.86 us (6%)
  other arithmetic  6.94 us (5%)
    ppermute x7, waiting for transfers between devices, swap_side(): return lax.ppermute(value, 'dp', [(i, i ^ 1) for i in range(ranks)])  31.5 us
    ppermute x18, starting transfers between devices, shift(): lax.ppermute(value, 'dp', [(i, (i + 2 * by) % ranks) for i in range(ranks)])  28.6 us
    ppermute x18, waiting for transfers between devices, shift(): lax.ppermute(value, 'dp', [(i, (i + 2 * by) % ranks) for i in range(ranks)])  21.5 us
    ppermute x6, waiting for transfers between devices, swap_layer(): return lax.ppermute(value, 'parts', [(0, 1), (1, 0)])  16.6 us
    ppermute x6, starting transfers between devices, swap_layer(): return lax.ppermute(value, 'parts', [(0, 1), (1, 0)])  9.18 us
    ppermute x7, starting transfers between devices, swap_side(): return lax.ppermute(value, 'dp', [(i, i ^ 1) for i in range(ranks)])  5.94 us
    dot_general x4, matrix products, contract_last(): lax.dot_general(left, right, (((1,), (1,)), ((), ())), preferred_element_...  3.91 us
    dot_general x4, matrix products, gradient(): jnp.dot(left[:, rows:], other_rows[piece], preferred_element_type=jnp.flo...  3.23 us
  transfers between devices with their start and end apart: 33, of which 13 were waited for; matrix products, arithmetic and copies ran while one was open for 14% of the time, Pallas kernels for 0%

profile of v1, /device:TPU:0, one launch (start us, length us, event | category | flops | bytes accessed | tf_op | source)
XLA Modules:
  0.0 140.5 jit_solution(8745453828278170322)
XLA Ops:
  0.6 1.0 dynamic-slice_bitcast_fusion
  1.7 5.1 %collective-permute-start.11 = (bf16[16,4096]{1,0:T(8,128)(2,1)S(1)}, bf16[16,4096]{1,0:T(8,128)(2,1)S(1)}, u32[]{:S(2)}, u32[]{:S(2)}) collective-permute-start(bf16[16,4096]{1,0:T(8,128)(2,1)S(1)} %dynamic-slice_bitcast_fusion), channel_id=1, source_target_pairs={{0,12},{2,14},{4,0},{6,2},{8,4},{10,6},{12,8},{14,10},{1,13},{3,15... | collective-permute-start | bytes 393224 | tf_op jit(solution)/shard_map/ppermute | solution.py:96
  6.8 1.0 collective-permute-start.15
  7.8 0.9 convert_reduce_fusion
  8.7 0.8 select_reduce_fusion.2
  9.5 1.6 %collective-permute-start = (f32[2,128]{1,0:T(2,128)S(1)}, f32[2,128]{1,0:T(2,128)S(1)}, u32[]{:S(2)}, u32[]{:S(2)}) collective-permute-start(f32[2,128]{1,0:T(2,128)S(1)} %pad_maximum_fusion.7), channel_id=1, source_target_pairs={{0,2},{2,0},{4,6},{6,4},{8,10},{10,8},{12,14},{14,12},{1,3},{3,1},... | collective-permute-start | bytes 3080 | tf_op jit(solution)/shard_map/ppermute | solution.py:93
  11.0 1.6 %dynamic-slice_bitcast_fusion.1 = bf16[16,4096]{1,0:T(8,128)(2,1)} fusion(bf16[1,32,4096]{2,1,0:T(8,128)(2,1)} %param.13, s32[]{:T(128)S(6)} %select_n.102), kind=kLoop, calls=%fused_computation.41 | loop fusion | bytes 262148 | tf_op jit(solution)/shard_map/dynamic_slice | solution.py:105
  12.6 2.5 %collective-permute-start.5 = (bf16[16,4096]{1,0:T(8,128)(2,1)}, bf16[16,4096]{1,0:T(8,128)(2,1)S(1)}, u32[]{:S(2)}, u32[]{:S(2)}) collective-permute-start(bf16[16,4096]{1,0:T(8,128)(2,1)} %dynamic-slice_bitcast_fusion.1), channel_id=1, source_target_pairs={{0,4},{2,6},{4,8},{6,10},{8,12},{10,14},{12,0},{14,2},{1,5},{3,7},... | collective-permute-start | bytes 393224 | tf_op jit(solution)/shard_map/ppermute | solution.py:96
  15.1 1.7 %constant_dynamic-update-slice_fusion.4 = bf16[256,4096]{1,0:T(8,128)(2,1)} fusion(bf16[1,32,4096]{2,1,0:T(8,128)(2,1)} %param.12), kind=kLoop, calls=%fused_computation.68 | loop fusion | bytes 524288
  16.7 2.3 %fusion.45 = (bf16[128,2048]{1,0:T(8,128)(2,1)}, bf16[128,2048]{1,0:T(8,128)(2,1)}) fusion(bf16[128,4096]{1,0:T(8,128)(2,1)} %param.7), kind=kLoop, calls=%fused_computation.95 | loop fusion | bytes 2097152 | tf_op jit(solution)/shard_map/slice | solution.py:150
  19.0 1.1 fusion.44
  20.1 1.0 collective-permute-start.3
  21.1 1.6 %collective-permute-start.12 = (bf16[16,4096]{1,0:T(8,128)(2,1)S(1)}, bf16[16,4096]{1,0:T(8,128)(2,1)S(1)}, u32[]{:S(2)}, u32[]{:S(2)}) collective-permute-start(bf16[16,4096]{1,0:T(8,128)(2,1)S(1)} %collective-permute-done.11), channel_id=1, source_target_pairs={{0,16},{16,0},{1,17},{17,1},{2,18},{18,2},{3,19},{19,3},{4,20},{20... | collective-permute-start | bytes 393224 | tf_op jit(solution)/shard_map/ppermute | solution.py:99
  22.8 1.5 %collective-permute-start.1 = (bf16[16,4096]{1,0:T(8,128)(2,1)}, bf16[16,4096]{1,0:T(8,128)(2,1)S(1)}, u32[]{:S(2)}, u32[]{:S(2)}) collective-permute-start(bf16[16,4096]{1,0:T(8,128)(2,1)} %dynamic-slice_bitcast_fusion.1), channel_id=1, source_target_pairs={{0,12},{2,14},{4,0},{6,2},{8,4},{10,6},{12,8},{14,10},{1,13},{3,15... | collective-permute-start | bytes 393224 | tf_op jit(solution)/shard_map/ppermute | solution.py:96
  24.2 2.0 %collective-permute-done.12 = bf16[16,4096]{1,0:T(8,128)(2,1)S(1)} collective-permute-done((bf16[16,4096]{1,0:T(8,128)(2,1)S(1)}, bf16[16,4096]{1,0:T(8,128)(2,1)S(1)}, u32[]{:S(2)}, u32[]{:S(2)}) %collective-permute-start.12) | collective-permute-done | bytes 131104 | tf_op jit(solution)/shard_map/ppermute | solution.py:99
  26.2 1.5 %collective-permute-start.14 = (bf16[16,4096]{1,0:T(8,128)(2,1)S(1)}, bf16[16,4096]{1,0:T(8,128)(2,1)S(1)}, u32[]{:S(2)}, u32[]{:S(2)}) collective-permute-start(bf16[16,4096]{1,0:T(8,128)(2,1)S(1)} %collective-permute-done.13), channel_id=1, source_target_pairs={{0,16},{16,0},{1,17},{17,1},{2,18},{18,2},{3,19},{19,3},{4,20},{20... | collective-permute-start | bytes 393224 | tf_op jit(solution)/shard_map/ppermute | solution.py:99
  27.7 0.7 constant_dynamic-update-slice_fusion.3
  28.5 0.5 collective-permute-start.22
  29.0 3.2 %collective-permute-done.14 = bf16[16,4096]{1,0:T(8,128)(2,1)S(1)} collective-permute-done((bf16[16,4096]{1,0:T(8,128)(2,1)S(1)}, bf16[16,4096]{1,0:T(8,128)(2,1)S(1)}, u32[]{:S(2)}, u32[]{:S(2)}) %collective-permute-start.14) | collective-permute-done | bytes 131104 | tf_op jit(solution)/shard_map/ppermute | solution.py:99
  32.2 1.5 %collective-permute-start.16 = (bf16[16,4096]{1,0:T(8,128)(2,1)S(1)}, bf16[16,4096]{1,0:T(8,128)(2,1)S(1)}, u32[]{:S(2)}, u32[]{:S(2)}) collective-permute-start(bf16[16,4096]{1,0:T(8,128)(2,1)S(1)} %collective-permute-done.15), channel_id=1, source_target_pairs={{0,16},{16,0},{1,17},{17,1},{2,18},{18,2},{3,19},{19,3},{4,20},{20... | collective-permute-start | bytes 393224 | tf_op jit(solution)/shard_map/ppermute | solution.py:99
  33.7 0.7 constant_dynamic-update-slice_fusion.2
  34.5 0.6 collective-permute-start.18
  35.0 3.1 %collective-permute-done.16 = bf16[16,4096]{1,0:T(8,128)(2,1)S(1)} collective-permute-done((bf16[16,4096]{1,0:T(8,128)(2,1)S(1)}, bf16[16,4096]{1,0:T(8,128)(2,1)S(1)}, u32[]{:S(2)}, u32[]{:S(2)}) %collective-permute-start.16) | collective-permute-done | bytes 131104 | tf_op jit(solution)/shard_map/ppermute | solution.py:99
  38.1 1.5 %collective-permute-start.6 = (bf16[16,4096]{1,0:T(8,128)(2,1)S(1)}, bf16[16,4096]{1,0:T(8,128)(2,1)S(1)}, u32[]{:S(2)}, u32[]{:S(2)}) collective-permute-start(bf16[16,4096]{1,0:T(8,128)(2,1)S(1)} %collective-permute-done.5), channel_id=1, source_target_pairs={{0,16},{16,0},{1,17},{17,1},{2,18},{18,2},{3,19},{19,3},{4,20},{20... | collective-permute-start | bytes 393224 | tf_op jit(solution)/shard_map/ppermute | solution.py:99
  39.6 0.7 constant_dynamic-update-slice_fusion.1
  40.5 0.6 collective-permute-start.8
  41.1 2.2 %collective-permute-done.6 = bf16[16,4096]{1,0:T(8,128)(2,1)S(1)} collective-permute-done((bf16[16,4096]{1,0:T(8,128)(2,1)S(1)}, bf16[16,4096]{1,0:T(8,128)(2,1)S(1)}, u32[]{:S(2)}, u32[]{:S(2)}) %collective-permute-start.6) | collective-permute-done | bytes 131104 | tf_op jit(solution)/shard_map/ppermute | solution.py:99
  43.2 1.5 %collective-permute-start.4 = (bf16[16,4096]{1,0:T(8,128)(2,1)S(1)}, bf16[16,4096]{1,0:T(8,128)(2,1)S(1)}, u32[]{:S(2)}, u32[]{:S(2)}) collective-permute-start(bf16[16,4096]{1,0:T(8,128)(2,1)S(1)} %collective-permute-done.3), channel_id=1, source_target_pairs={{0,16},{16,0},{1,17},{17,1},{2,18},{18,2},{3,19},{19,3},{4,20},{20... | collective-permute-start | bytes 393224 | tf_op jit(solution)/shard_map/ppermute | solution.py:99
  44.8 0.6 collective-permute-start.7
  45.4 2.8 %collective-permute-done.4 = bf16[16,4096]{1,0:T(8,128)(2,1)S(1)} collective-permute-done((bf16[16,4096]{1,0:T(8,128)(2,1)S(1)}, bf16[16,4096]{1,0:T(8,128)(2,1)S(1)}, u32[]{:S(2)}, u32[]{:S(2)}) %collective-permute-start.4) | collective-permute-done | bytes 131104 | tf_op jit(solution)/shard_map/ppermute | solution.py:99
  48.2 1.5 %collective-permute-start.2 = (bf16[16,4096]{1,0:T(8,128)(2,1)S(1)}, bf16[16,4096]{1,0:T(8,128)(2,1)S(1)}, u32[]{:S(2)}, u32[]{:S(2)}) collective-permute-start(bf16[16,4096]{1,0:T(8,128)(2,1)S(1)} %collective-permute-done.1), channel_id=1, source_target_pairs={{0,16},{16,0},{1,17},{17,1},{2,18},{18,2},{3,19},{19,3},{4,20},{20... | collective-permute-start | bytes 393224 | tf_op jit(solution)/shard_map/ppermute | solution.py:99
  49.8 3.4 %collective-permute-done.2 = bf16[16,4096]{1,0:T(8,128)(2,1)S(1)} collective-permute-done((bf16[16,4096]{1,0:T(8,128)(2,1)S(1)}, bf16[16,4096]{1,0:T(8,128)(2,1)S(1)}, u32[]{:S(2)}, u32[]{:S(2)}) %collective-permute-start.2) | collective-permute-done | bytes 131104 | tf_op jit(solution)/shard_map/ppermute | solution.py:99
  53.2 0.4 fusion.56
  53.7 1.1 fusion.16
  54.8 0.8 copy-done.4
  55.7 0.4 fusion.4
  56.2 9.9 %collective-permute-done.8 = bf16[128,2048]{1,0:T(8,128)(2,1)} collective-permute-done((bf16[128,2048]{1,0:T(8,128)(2,1)}, bf16[128,2048]{1,0:T(8,128)(2,1)}, u32[]{:S(2)}, u32[]{:S(2)}) %collective-permute-start.8) | collective-permute-done | bytes 524320 | tf_op jit(solution)/shard_map/ppermute | solution.py:93
  66.1 7.1 %collective-permute-done.7 = bf16[128,2048]{1,0:T(8,128)(2,1)} collective-permute-done((bf16[128,2048]{1,0:T(8,128)(2,1)}, bf16[128,2048]{1,0:T(8,128)(2,1)}, u32[]{:S(2)}, u32[]{:S(2)}) %collective-permute-start.7) | collective-permute-done | bytes 524320 | tf_op jit(solution)/shard_map/ppermute | solution.py:93
  73.3 2.0 %fusion = f32[128,128]{0,1:T(8,128)S(1)} fusion(bf16[128,2048]{1,0:T(8,128)(2,1)} %collective-permute-done.8, bf16[128,2048]{1,0:T(8,128)(2,1)} %collective-permute-done.7, bf16[32,4096]{1,0:T(8,128)(2,1)} %copy-done.8, bf16[32,4096]{1,0:T(8,128)(2,1)} %copy-done.9, bf16[32,4096]{1,0:T(8,128)(2,1)} %copy-done.10, bf16[32,4096]{1,0:T(8,128)(2,1)} %bitcast.45), kind=kOutput, calls=%fused_computation.6 | convolution fusion | flops 140509184 | bytes 2162688 | tf_op jit(solution)/shard_map/dot_general | solution.py:10
  75.5 0.5 collective-permute-start.9
  76.0 0.7 broadcast_compare_fusion.2
  76.7 0.5 collective-permute-start.17
  77.3 0.3 fusion.28
  78.5 1.6 %collective-permute-start.10 = (bf16[32,128]{1,0:T(8,128)(2,1)S(1)}, bf16[32,128]{1,0:T(8,128)(2,1)S(1)}, u32[]{:S(2)}, u32[]{:S(2)}) collective-permute-start(bf16[32,128]{1,0:T(8,128)(2,1)S(1)} %get-tuple-element.30), channel_id=1, source_target_pairs={{0,2},{2,0},{4,6},{6,4},{8,10},{10,8},{12,14},{14,12},{1,3},{3,1},... | collective-permute-start | bytes 24584 | tf_op jit(solution)/shard_map/ppermute | solution.py:93
  80.4 1.5 %collective-permute-start.25 = (bf16[32,2048]{1,0:T(8,128)(2,1)S(1)}, bf16[32,2048]{1,0:T(8,128)(2,1)S(1)}, u32[]{:S(2)}, u32[]{:S(2)}) collective-permute-start(bf16[32,2048]{1,0:T(8,128)(2,1)S(1)} %get-tuple-element.27), channel_id=1, source_target_pairs={{0,12},{2,14},{4,0},{6,2},{8,4},{10,6},{12,8},{14,10},{1,13},{3,15... | collective-permute-start | bytes 393224 | tf_op jit(solution)/shard_map/ppermute | solution.py:96
  81.9 0.7 collective-permute-start.24
  82.6 1.9 %collective-permute-start.23 = (bf16[32,2048]{1,0:T(8,128)(2,1)S(1)}, bf16[32,2048]{1,0:T(8,128)(2,1)S(1)}, u32[]{:S(2)}, u32[]{:S(2)}) collective-permute-start(bf16[32,2048]{1,0:T(8,128)(2,1)S(1)} %get-tuple-element.26), channel_id=1, source_target_pairs={{0,4},{2,6},{4,8},{6,10},{8,12},{10,14},{12,0},{14,2},{1,5},{3,7},... | collective-permute-start | bytes 393224 | tf_op jit(solution)/shard_map/ppermute | solution.py:96
  84.8 1.3 fusion.54
  86.2 1.3 fusion.55
  87.6 14.5 %collective-permute-done.10 = bf16[32,128]{1,0:T(8,128)(2,1)S(1)} collective-permute-done((bf16[32,128]{1,0:T(8,128)(2,1)S(1)}, bf16[32,128]{1,0:T(8,128)(2,1)S(1)}, u32[]{:S(2)}, u32[]{:S(2)}) %collective-permute-start.10) | collective-permute-done | bytes 8224 | tf_op jit(solution)/shard_map/ppermute | solution.py:93
  102.0 1.5 %collective-permute-start.21 = (bf16[32,2048]{1,0:T(8,128)(2,1)S(1)}, bf16[32,2048]{1,0:T(8,128)(2,1)S(1)}, u32[]{:S(2)}, u32[]{:S(2)}) collective-permute-start(bf16[32,2048]{1,0:T(8,128)(2,1)S(1)} %get-tuple-element.24), channel_id=1, source_target_pairs={{0,12},{2,14},{4,0},{6,2},{8,4},{10,6},{12,8},{14,10},{1,13},{3,15... | collective-permute-start | bytes 393224 | tf_op jit(solution)/shard_map/ppermute | solution.py:96
  103.5 0.8 collective-permute-start.20
  104.3 1.9 %collective-permute-start.19 = (bf16[32,2048]{1,0:T(8,128)(2,1)S(1)}, bf16[32,2048]{1,0:T(8,128)(2,1)S(1)}, u32[]{:S(2)}, u32[]{:S(2)}) collective-permute-start(bf16[32,2048]{1,0:T(8,128)(2,1)S(1)} %get-tuple-element.23), channel_id=1, source_target_pairs={{0,4},{2,6},{4,8},{6,10},{8,12},{10,14},{12,0},{14,2},{1,5},{3,7},... | collective-permute-start | bytes 393224 | tf_op jit(solution)/shard_map/ppermute | solution.py:96
  106.2 2.0 %collective-permute-start.32 = (bf16[32,2048]{1,0:T(8,128)(2,1)S(1)}, bf16[32,2048]{1,0:T(8,128)(2,1)S(1)}, u32[]{:S(2)}, u32[]{:S(2)}) collective-permute-start(bf16[32,2048]{1,0:T(8,128)(2,1)S(1)} %get-tuple-element.21), channel_id=1, source_target_pairs={{0,12},{2,14},{4,0},{6,2},{8,4},{10,6},{12,8},{14,10},{1,13},{3,15... | collective-permute-start | bytes 393224 | tf_op jit(solution)/shard_map/ppermute | solution.py:96
  108.2 2.3 %collective-permute-start.31 = (bf16[32,2048]{1,0:T(8,128)(2,1)S(1)}, bf16[32,2048]{1,0:T(8,128)(2,1)S(1)}, u32[]{:S(2)}, u32[]{:S(2)}) collective-permute-start(bf16[32,2048]{1,0:T(8,128)(2,1)S(1)} %get-tuple-element.22), channel_id=1, source_target_pairs={{0,8},{2,10},{4,12},{6,14},{8,0},{10,2},{12,4},{14,6},{1,9},{3,11}... | collective-permute-start | bytes 393224 | tf_op jit(solution)/shard_map/ppermute | solution.py:96
  110.5 10.4 %collective-permute-done.20 = bf16[32,2048]{1,0:T(8,128)(2,1)S(1)} collective-permute-done((bf16[32,2048]{1,0:T(8,128)(2,1)S(1)}, bf16[32,2048]{1,0:T(8,128)(2,1)S(1)}, u32[]{:S(2)}, u32[]{:S(2)}) %collective-permute-start.20) | collective-permute-done | bytes 131104 | tf_op jit(solution)/shard_map/ppermute | solution.py:96
  120.9 3.8 %collective-permute-start.29 = (bf16[32,2048]{1,0:T(8,128)(2,1)S(1)}, bf16[32,2048]{1,0:T(8,128)(2,1)S(1)}, u32[]{:S(2)}, u32[]{:S(2)}) collective-permute-start(bf16[32,2048]{1,0:T(8,128)(2,1)S(1)} %get-tuple-element.18), channel_id=1, source_target_pairs={{0,12},{2,14},{4,0},{6,2},{8,4},{10,6},{12,8},{14,10},{1,13},{3,15... | collective-permute-start | bytes 393224 | tf_op jit(solution)/shard_map/ppermute | solution.py:96
  124.9 0.6 collective-permute-done.31
  125.5 1.2 collective-permute-start.27
  126.7 2.1 %collective-permute-done.30 = bf16[32,2048]{1,0:T(8,128)(2,1)S(1)} collective-permute-done((bf16[32,2048]{1,0:T(8,128)(2,1)S(1)}, bf16[32,2048]{1,0:T(8,128)(2,1)S(1)}, u32[]{:S(2)}, u32[]{:S(2)}) %collective-permute-start.30) | collective-permute-done | bytes 131104 | tf_op jit(solution)/shard_map/ppermute | solution.py:96
  129.0 0.8 maximum_bitcast_fusion
  129.8 8.3 %collective-permute-done.28 = bf16[32,2048]{1,0:T(8,128)(2,1)S(1)} collective-permute-done((bf16[32,2048]{1,0:T(8,128)(2,1)S(1)}, bf16[32,2048]{1,0:T(8,128)(2,1)S(1)}, u32[]{:S(2)}, u32[]{:S(2)}) %collective-permute-start.28) | collective-permute-done | bytes 131104 | tf_op jit(solution)/shard_map/ppermute | solution.py:96
  138.2 0.8 maximum_bitcast_fusion.1
  139.1 1.4 %convolution_convert_fusion = bf16[128,4096]{1,0:T(8,128)(2,1)} fusion(bf16[256,4096]{1,0:T(8,128)(2,1)S(1)} %constant_dynamic-update-slice_fusion, bf16[128,128]{1,0:T(8,128)(2,1)S(1)} %bitcast.44, bf16[128,128]{1,0:T(8,128)(2,1)S(1)} %bitcast.43), kind=kOutput, calls=%fused_computation | convolution fusion | flops 269090816 | bytes 3211264 | tf_op jit(solution)/shard_map/dot_general | solution.py:16
  (86 shorter events, 2.7 us)
Async XLA Ops:
  0.6 18.4 %copy-start.1 = (bf16[128,4096]{1,0:T(8,128)(2,1)S(1)}, bf16[128,4096]{1,0:T(8,128)(2,1)}, u32[]{:S(2)}) copy-start(bf16[128,4096]{1,0:T(8,128)(2,1)} %param.8) | copy-start | bytes 3145732
  1.7 19.4 %collective-permute-start.11 = (bf16[16,4096]{1,0:T(8,128)(2,1)S(1)}, bf16[16,4096]{1,0:T(8,128)(2,1)S(1)}, u32[]{:S(2)}, u32[]{:S(2)}) collective-permute-start(bf16[16,4096]{1,0:T(8,128)(2,1)S(1)} %dynamic-slice_bitcast_fusion), channel_id=1, source_target_pairs={{0,12},{2,14},{4,0},{6,2},{8,4},{10,6},{12,8},{14,10},{1,13},{3,15... | collective-permute-start | bytes 393224 | tf_op jit(solution)/shard_map/ppermute | solution.py:96
  6.8 16.0 %collective-permute-start.13 = (bf16[16,4096]{1,0:T(8,128)(2,1)S(1)}, bf16[16,4096]{1,0:T(8,128)(2,1)S(1)}, u32[]{:S(2)}, u32[]{:S(2)}) collective-permute-start(bf16[16,4096]{1,0:T(8,128)(2,1)S(1)} %dynamic-slice_bitcast_fusion), channel_id=1, source_target_pairs={{0,8},{2,10},{4,12},{6,14},{8,0},{10,2},{12,4},{14,6},{1,9},{3,11}... | collective-permute-start | bytes 393224 | tf_op jit(solution)/shard_map/ppermute | solution.py:96
  6.8 21.7 %collective-permute-start.15 = (bf16[16,4096]{1,0:T(8,128)(2,1)S(1)}, bf16[16,4096]{1,0:T(8,128)(2,1)S(1)}, u32[]{:S(2)}, u32[]{:S(2)}) collective-permute-start(bf16[16,4096]{1,0:T(8,128)(2,1)S(1)} %dynamic-slice_bitcast_fusion), channel_id=1, source_target_pairs={{0,4},{2,6},{4,8},{6,10},{8,12},{10,14},{12,0},{14,2},{1,5},{3,7},... | collective-permute-start | bytes 393224 | tf_op jit(solution)/shard_map/ppermute | solution.py:96
  9.4 10.6 %copy-start.13 = (s32[128]{0:T(128)}, s32[128]{0:T(128)S(1)}, u32[]{:S(2)}) copy-start(s32[128]{0:T(128)S(1)} %select_reduce_fusion.2) | copy-start | bytes 1540
  9.5 10.6 %collective-permute-start = (f32[2,128]{1,0:T(2,128)S(1)}, f32[2,128]{1,0:T(2,128)S(1)}, u32[]{:S(2)}, u32[]{:S(2)}) collective-permute-start(f32[2,128]{1,0:T(2,128)S(1)} %pad_maximum_fusion.7), channel_id=1, source_target_pairs={{0,2},{2,0},{4,6},{6,4},{8,10},{10,8},{12,14},{14,12},{1,3},{3,1},... | collective-permute-start | bytes 3080 | tf_op jit(solution)/shard_map/ppermute | solution.py:93
  12.6 21.9 %collective-permute-start.5 = (bf16[16,4096]{1,0:T(8,128)(2,1)}, bf16[16,4096]{1,0:T(8,128)(2,1)S(1)}, u32[]{:S(2)}, u32[]{:S(2)}) collective-permute-start(bf16[16,4096]{1,0:T(8,128)(2,1)} %dynamic-slice_bitcast_fusion.1), channel_id=1, source_target_pairs={{0,4},{2,6},{4,8},{6,10},{8,12},{10,14},{12,0},{14,2},{1,5},{3,7},... | collective-permute-start | bytes 393224 | tf_op jit(solution)/shard_map/ppermute | solution.py:96
  19.0 21.4 %copy-start.3 = (bf16[1,32,4096]{2,1,0:T(8,128)(2,1)S(1)}, bf16[1,32,4096]{2,1,0:T(8,128)(2,1)}, u32[]{:S(2)}) copy-start(bf16[1,32,4096]{2,1,0:T(8,128)(2,1)} %param.12) | copy-start | bytes 786436
  20.1 20.3 %collective-permute-start.3 = (bf16[16,4096]{1,0:T(8,128)(2,1)}, bf16[16,4096]{1,0:T(8,128)(2,1)S(1)}, u32[]{:S(2)}, u32[]{:S(2)}) collective-permute-start(bf16[16,4096]{1,0:T(8,128)(2,1)} %dynamic-slice_bitcast_fusion.1), channel_id=1, source_target_pairs={{0,8},{2,10},{4,12},{6,14},{8,0},{10,2},{12,4},{14,6},{1,9},{3,11}... | collective-permute-start | bytes 393224 | tf_op jit(solution)/shard_map/ppermute | solution.py:96
  21.1 5.1 %collective-permute-start.12 = (bf16[16,4096]{1,0:T(8,128)(2,1)S(1)}, bf16[16,4096]{1,0:T(8,128)(2,1)S(1)}, u32[]{:S(2)}, u32[]{:S(2)}) collective-permute-start(bf16[16,4096]{1,0:T(8,128)(2,1)S(1)} %collective-permute-done.11), channel_id=1, source_target_pairs={{0,16},{16,0},{1,17},{17,1},{2,18},{18,2},{3,19},{19,3},{4,20},{20... | collective-permute-start | bytes 393224 | tf_op jit(solution)/shard_map/ppermute | solution.py:99
  22.8 22.1 %collective-permute-start.1 = (bf16[16,4096]{1,0:T(8,128)(2,1)}, bf16[16,4096]{1,0:T(8,128)(2,1)S(1)}, u32[]{:S(2)}, u32[]{:S(2)}) collective-permute-start(bf16[16,4096]{1,0:T(8,128)(2,1)} %dynamic-slice_bitcast_fusion.1), channel_id=1, source_target_pairs={{0,12},{2,14},{4,0},{6,2},{8,4},{10,6},{12,8},{14,10},{1,13},{3,15... | collective-permute-start | bytes 393224 | tf_op jit(solution)/shard_map/ppermute | solution.py:96
  26.2 6.0 %collective-permute-start.14 = (bf16[16,4096]{1,0:T(8,128)(2,1)S(1)}, bf16[16,4096]{1,0:T(8,128)(2,1)S(1)}, u32[]{:S(2)}, u32[]{:S(2)}) collective-permute-start(bf16[16,4096]{1,0:T(8,128)(2,1)S(1)} %collective-permute-done.13), channel_id=1, source_target_pairs={{0,16},{16,0},{1,17},{17,1},{2,18},{18,2},{3,19},{19,3},{4,20},{20... | collective-permute-start | bytes 393224 | tf_op jit(solution)/shard_map/ppermute | solution.py:99
  28.5 26.3 %collective-permute-start.22 = (bf16[128,2048]{1,0:T(8,128)(2,1)}, bf16[128,2048]{1,0:T(8,128)(2,1)S(1)}, u32[]{:S(2)}, u32[]{:S(2)}) collective-permute-start(bf16[128,2048]{1,0:T(8,128)(2,1)} %get-tuple-element.16), channel_id=1, source_target_pairs={{0,2},{2,0},{4,6},{6,4},{8,10},{10,8},{12,14},{14,12},{1,3},{3,1},... | collective-permute-start | bytes 1572872 | tf_op jit(solution)/shard_map/ppermute | solution.py:93
  32.2 5.9 %collective-permute-start.16 = (bf16[16,4096]{1,0:T(8,128)(2,1)S(1)}, bf16[16,4096]{1,0:T(8,128)(2,1)S(1)}, u32[]{:S(2)}, u32[]{:S(2)}) collective-permute-start(bf16[16,4096]{1,0:T(8,128)(2,1)S(1)} %collective-permute-done.15), channel_id=1, source_target_pairs={{0,16},{16,0},{1,17},{17,1},{2,18},{18,2},{3,19},{19,3},{4,20},{20... | collective-permute-start | bytes 393224 | tf_op jit(solution)/shard_map/ppermute | solution.py:99
  34.5 20.4 %collective-permute-start.18 = (bf16[128,2048]{1,0:T(8,128)(2,1)}, bf16[128,2048]{1,0:T(8,128)(2,1)S(1)}, u32[]{:S(2)}, u32[]{:S(2)}) collective-permute-start(bf16[128,2048]{1,0:T(8,128)(2,1)} %get-tuple-element.15), channel_id=1, source_target_pairs={{0,2},{2,0},{4,6},{6,4},{8,10},{10,8},{12,14},{14,12},{1,3},{3,1},... | collective-permute-start | bytes 1572872 | tf_op jit(solution)/shard_map/ppermute | solution.py:93
  38.1 5.1 %collective-permute-start.6 = (bf16[16,4096]{1,0:T(8,128)(2,1)S(1)}, bf16[16,4096]{1,0:T(8,128)(2,1)S(1)}, u32[]{:S(2)}, u32[]{:S(2)}) collective-permute-start(bf16[16,4096]{1,0:T(8,128)(2,1)S(1)} %collective-permute-done.5), channel_id=1, source_target_pairs={{0,16},{16,0},{1,17},{17,1},{2,18},{18,2},{3,19},{19,3},{4,20},{20... | collective-permute-start | bytes 393224 | tf_op jit(solution)/shard_map/ppermute | solution.py:99
  39.6 13.6 %copy-start = (bf16[128,4096]{1,0:T(8,128)(2,1)S(1)}, bf16[128,4096]{1,0:T(8,128)(2,1)}, u32[]{:S(2)}) copy-start(bf16[128,4096]{1,0:T(8,128)(2,1)} %param.7) | copy-start | bytes 3145732
  40.4 13.3 %copy-start.11 = (bf16[1,32,4096]{2,1,0:T(8,128)(2,1)S(1)}, bf16[1,32,4096]{2,1,0:T(8,128)(2,1)}, u32[]{:S(2)}) copy-start(bf16[1,32,4096]{2,1,0:T(8,128)(2,1)} %param.13) | copy-start | bytes 786436
  40.5 25.7 %collective-permute-start.8 = (bf16[128,2048]{1,0:T(8,128)(2,1)}, bf16[128,2048]{1,0:T(8,128)(2,1)}, u32[]{:S(2)}, u32[]{:S(2)}) collective-permute-start(bf16[128,2048]{1,0:T(8,128)(2,1)} %get-tuple-element.14), channel_id=1, source_target_pairs={{0,2},{2,0},{4,6},{6,4},{8,10},{10,8},{12,14},{14,12},{1,3},{3,1},... | collective-permute-start | bytes 1572872 | tf_op jit(solution)/shard_map/ppermute | solution.py:93
  43.2 5.0 %collective-permute-start.4 = (bf16[16,4096]{1,0:T(8,128)(2,1)S(1)}, bf16[16,4096]{1,0:T(8,128)(2,1)S(1)}, u32[]{:S(2)}, u32[]{:S(2)}) collective-permute-start(bf16[16,4096]{1,0:T(8,128)(2,1)S(1)} %collective-permute-done.3), channel_id=1, source_target_pairs={{0,16},{16,0},{1,17},{17,1},{2,18},{18,2},{3,19},{19,3},{4,20},{20... | collective-permute-start | bytes 393224 | tf_op jit(solution)/shard_map/ppermute | solution.py:99
  44.8 10.0 %copy-start.8 = (bf16[32,4096]{1,0:T(8,128)(2,1)}, bf16[32,4096]{1,0:T(8,128)(2,1)S(1)}, u32[]{:S(2)}) copy-start(bf16[32,4096]{1,0:T(8,128)(2,1)S(1)} %maximum_select_fusion.2) | copy-start | bytes 786436
  44.8 28.4 %collective-permute-start.7 = (bf16[128,2048]{1,0:T(8,128)(2,1)}, bf16[128,2048]{1,0:T(8,128)(2,1)}, u32[]{:S(2)}, u32[]{:S(2)}) collective-permute-start(bf16[128,2048]{1,0:T(8,128)(2,1)} %get-tuple-element.13), channel_id=1, source_target_pairs={{0,2},{2,0},{4,6},{6,4},{8,10},{10,8},{12,14},{14,12},{1,3},{3,1},... | collective-permute-start | bytes 1572872 | tf_op jit(solution)/shard_map/ppermute | solution.py:93
  48.2 5.0 %collective-permute-start.2 = (bf16[16,4096]{1,0:T(8,128)(2,1)S(1)}, bf16[16,4096]{1,0:T(8,128)(2,1)S(1)}, u32[]{:S(2)}, u32[]{:S(2)}) collective-permute-start(bf16[16,4096]{1,0:T(8,128)(2,1)S(1)} %collective-permute-done.1), channel_id=1, source_target_pairs={{0,16},{16,0},{1,17},{17,1},{2,18},{18,2},{3,19},{19,3},{4,20},{20... | collective-permute-start | bytes 393224 | tf_op jit(solution)/shard_map/ppermute | solution.py:99
  49.8 5.0 %copy-start.9 = (bf16[32,4096]{1,0:T(8,128)(2,1)}, bf16[32,4096]{1,0:T(8,128)(2,1)S(1)}, u32[]{:S(2)}) copy-start(bf16[32,4096]{1,0:T(8,128)(2,1)S(1)} %maximum_select_fusion.1) | copy-start | bytes 786436
  53.2 1.6 %copy-start.10 = (bf16[32,4096]{1,0:T(8,128)(2,1)}, bf16[32,4096]{1,0:T(8,128)(2,1)S(1)}, u32[]{:S(2)}) copy-start(bf16[32,4096]{1,0:T(8,128)(2,1)S(1)} %maximum_select_fusion) | copy-start | bytes 786436
  54.8 1.3 copy-start.6
  54.8 0.8 copy-start.4
  56.2 19.0 %copy-start.12 = (f32[128,128]{0,1:T(8,128)S(1)}, f32[128,128]{0,1:T(8,128)}, u32[]{:S(2)}) copy-start(f32[128,128]{0,1:T(8,128)} %fusion.16) | copy-start | bytes 196612
  75.4 1.9 %collective-permute-start.26 = (f32[32,256]{1,0:T(8,128)S(1)}, f32[32,256]{1,0:T(8,128)S(1)}, u32[]{:S(2)}, u32[]{:S(2)}) collective-permute-start(f32[32,256]{1,0:T(8,128)S(1)} %get-tuple-element.3), channel_id=1, source_target_pairs={{0,1},{1,0},{2,3},{3,2},{4,5},{5,4},{6,7},{7,6},{8,9},{9,8},{10,11... | collective-permute-start | bytes 98312 | tf_op jit(solution)/shard_map/ppermute | solution.py:102
  75.5 1.8 %collective-permute-start.9 = (f32[32,256]{1,0:T(8,128)S(1)}, f32[32,256]{1,0:T(8,128)S(1)}, u32[]{:S(2)}, u32[]{:S(2)}) collective-permute-start(f32[32,256]{1,0:T(8,128)S(1)} %get-tuple-element.4), channel_id=1, source_target_pairs={{0,1},{1,0},{2,3},{3,2},{4,5},{5,4},{6,7},{7,6},{8,9},{9,8},{10,11... | collective-permute-start | bytes 98312 | tf_op jit(solution)/shard_map/ppermute | solution.py:102
  76.7 62.3 %collective-permute-start.17 = (bf16[128,4096]{1,0:T(8,128)(2,1)S(1)}, bf16[128,4096]{1,0:T(8,128)(2,1)S(1)}, u32[]{:S(2)}, u32[]{:S(2)}) collective-permute-start(bf16[128,4096]{1,0:T(8,128)(2,1)S(1)} %pad_maximum_fusion.1), channel_id=1, source_target_pairs={{0,2},{2,0},{4,6},{6,4},{8,10},{10,8},{12,14},{14,12},{1,3},{3,1},... | collective-permute-start | bytes 3145736 | tf_op jit(solution)/shard_map/ppermute | solution.py:93
  77.6 2.5 %copy-start.7 = (bf16[128,2048]{1,0:T(8,128)(2,1)S(1)}, bf16[128,2048]{1,0:T(8,128)(2,1)}, u32[]{:S(2)}) copy-start(bf16[128,2048]{1,0:T(8,128)(2,1)} %copy-done.6) | copy-start | bytes 1572868
  78.5 6.0 %copy-start.5 = (bf16[128,2048]{1,0:T(8,128)(2,1)S(1)}, bf16[128,2048]{1,0:T(8,128)(2,1)}, u32[]{:S(2)}) copy-start(bf16[128,2048]{1,0:T(8,128)(2,1)} %copy-done.4) | copy-start | bytes 1572868
  78.5 23.5 %collective-permute-start.10 = (bf16[32,128]{1,0:T(8,128)(2,1)S(1)}, bf16[32,128]{1,0:T(8,128)(2,1)S(1)}, u32[]{:S(2)}, u32[]{:S(2)}) collective-permute-start(bf16[32,128]{1,0:T(8,128)(2,1)S(1)} %get-tuple-element.30), channel_id=1, source_target_pairs={{0,2},{2,0},{4,6},{6,4},{8,10},{10,8},{12,14},{14,12},{1,3},{3,1},... | collective-permute-start | bytes 24584 | tf_op jit(solution)/shard_map/ppermute | solution.py:93
  80.4 23.1 %collective-permute-start.25 = (bf16[32,2048]{1,0:T(8,128)(2,1)S(1)}, bf16[32,2048]{1,0:T(8,128)(2,1)S(1)}, u32[]{:S(2)}, u32[]{:S(2)}) collective-permute-start(bf16[32,2048]{1,0:T(8,128)(2,1)S(1)} %get-tuple-element.27), channel_id=1, source_target_pairs={{0,12},{2,14},{4,0},{6,2},{8,4},{10,6},{12,8},{14,10},{1,13},{3,15... | collective-permute-start | bytes 393224 | tf_op jit(solution)/shard_map/ppermute | solution.py:96
  81.9 22.4 %collective-permute-start.24 = (bf16[32,2048]{1,0:T(8,128)(2,1)S(1)}, bf16[32,2048]{1,0:T(8,128)(2,1)S(1)}, u32[]{:S(2)}, u32[]{:S(2)}) collective-permute-start(bf16[32,2048]{1,0:T(8,128)(2,1)S(1)} %get-tuple-element.28), channel_id=1, source_target_pairs={{0,8},{2,10},{4,12},{6,14},{8,0},{10,2},{12,4},{14,6},{1,9},{3,11}... | collective-permute-start | bytes 393224 | tf_op jit(solution)/shard_map/ppermute | solution.py:96
  82.6 23.6 %collective-permute-start.23 = (bf16[32,2048]{1,0:T(8,128)(2,1)S(1)}, bf16[32,2048]{1,0:T(8,128)(2,1)S(1)}, u32[]{:S(2)}, u32[]{:S(2)}) collective-permute-start(bf16[32,2048]{1,0:T(8,128)(2,1)S(1)} %get-tuple-element.26), channel_id=1, source_target_pairs={{0,4},{2,6},{4,8},{6,10},{8,12},{10,14},{12,0},{14,2},{1,5},{3,7},... | collective-permute-start | bytes 393224 | tf_op jit(solution)/shard_map/ppermute | solution.py:96
  102.0 6.2 %collective-permute-start.21 = (bf16[32,2048]{1,0:T(8,128)(2,1)S(1)}, bf16[32,2048]{1,0:T(8,128)(2,1)S(1)}, u32[]{:S(2)}, u32[]{:S(2)}) collective-permute-start(bf16[32,2048]{1,0:T(8,128)(2,1)S(1)} %get-tuple-element.24), channel_id=1, source_target_pairs={{0,12},{2,14},{4,0},{6,2},{8,4},{10,6},{12,8},{14,10},{1,13},{3,15... | collective-permute-start | bytes 393224 | tf_op jit(solution)/shard_map/ppermute | solution.py:96
  103.5 17.4 %collective-permute-start.20 = (bf16[32,2048]{1,0:T(8,128)(2,1)S(1)}, bf16[32,2048]{1,0:T(8,128)(2,1)S(1)}, u32[]{:S(2)}, u32[]{:S(2)}) collective-permute-start(bf16[32,2048]{1,0:T(8,128)(2,1)S(1)} %get-tuple-element.25), channel_id=1, source_target_pairs={{0,8},{2,10},{4,12},{6,14},{8,0},{10,2},{12,4},{14,6},{1,9},{3,11}... | collective-permute-start | bytes 393224 | tf_op jit(solution)/shard_map/ppermute | solution.py:96
  104.3 16.6 %collective-permute-start.19 = (bf16[32,2048]{1,0:T(8,128)(2,1)S(1)}, bf16[32,2048]{1,0:T(8,128)(2,1)S(1)}, u32[]{:S(2)}, u32[]{:S(2)}) collective-permute-start(bf16[32,2048]{1,0:T(8,128)(2,1)S(1)} %get-tuple-element.23), channel_id=1, source_target_pairs={{0,4},{2,6},{4,8},{6,10},{8,12},{10,14},{12,0},{14,2},{1,5},{3,7},... | collective-permute-start | bytes 393224 | tf_op jit(solution)/shard_map/ppermute | solution.py:96
  106.2 18.7 %collective-permute-start.32 = (bf16[32,2048]{1,0:T(8,128)(2,1)S(1)}, bf16[32,2048]{1,0:T(8,128)(2,1)S(1)}, u32[]{:S(2)}, u32[]{:S(2)}) collective-permute-start(bf16[32,2048]{1,0:T(8,128)(2,1)S(1)} %get-tuple-element.21), channel_id=1, source_target_pairs={{0,12},{2,14},{4,0},{6,2},{8,4},{10,6},{12,8},{14,10},{1,13},{3,15... | collective-permute-start | bytes 393224 | tf_op jit(solution)/shard_map/ppermute | solution.py:96
  108.2 17.3 %collective-permute-start.31 = (bf16[32,2048]{1,0:T(8,128)(2,1)S(1)}, bf16[32,2048]{1,0:T(8,128)(2,1)S(1)}, u32[]{:S(2)}, u32[]{:S(2)}) collective-permute-start(bf16[32,2048]{1,0:T(8,128)(2,1)S(1)} %get-tuple-element.22), channel_id=1, source_target_pairs={{0,8},{2,10},{4,12},{6,14},{8,0},{10,2},{12,4},{14,6},{1,9},{3,11}... | collective-permute-start | bytes 393224 | tf_op jit(solution)/shard_map/ppermute | solution.py:96
  120.9 8.0 %collective-permute-start.30 = (bf16[32,2048]{1,0:T(8,128)(2,1)S(1)}, bf16[32,2048]{1,0:T(8,128)(2,1)S(1)}, u32[]{:S(2)}, u32[]{:S(2)}) collective-permute-start(bf16[32,2048]{1,0:T(8,128)(2,1)S(1)} %get-tuple-element.20), channel_id=1, source_target_pairs={{0,4},{2,6},{4,8},{6,10},{8,12},{10,14},{12,0},{14,2},{1,5},{3,7},... | collective-permute-start | bytes 393224 | tf_op jit(solution)/shard_map/ppermute | solution.py:96
  120.9 8.8 %collective-permute-start.29 = (bf16[32,2048]{1,0:T(8,128)(2,1)S(1)}, bf16[32,2048]{1,0:T(8,128)(2,1)S(1)}, u32[]{:S(2)}, u32[]{:S(2)}) collective-permute-start(bf16[32,2048]{1,0:T(8,128)(2,1)S(1)} %get-tuple-element.18), channel_id=1, source_target_pairs={{0,12},{2,14},{4,0},{6,2},{8,4},{10,6},{12,8},{14,10},{1,13},{3,15... | collective-permute-start | bytes 393224 | tf_op jit(solution)/shard_map/ppermute | solution.py:96
  124.8 14.2 %copy-start.2 = (bf16[256,4096]{1,0:T(8,128)(2,1)S(1)}, bf16[256,4096]{1,0:T(8,128)(2,1)}, u32[]{:S(2)}) copy-start(bf16[256,4096]{1,0:T(8,128)(2,1)} %get-tuple-element.7) | copy-start | bytes 6291460
  124.8 13.2 %collective-permute-start.28 = (bf16[32,2048]{1,0:T(8,128)(2,1)S(1)}, bf16[32,2048]{1,0:T(8,128)(2,1)S(1)}, u32[]{:S(2)}, u32[]{:S(2)}) collective-permute-start(bf16[32,2048]{1,0:T(8,128)(2,1)S(1)} %get-tuple-element.19), channel_id=1, source_target_pairs={{0,8},{2,10},{4,12},{6,14},{8,0},{10,2},{12,4},{14,6},{1,9},{3,11}... | collective-permute-start | bytes 393224 | tf_op jit(solution)/shard_map/ppermute | solution.py:96
  125.5 12.6 %collective-permute-start.27 = (bf16[32,2048]{1,0:T(8,128)(2,1)S(1)}, bf16[32,2048]{1,0:T(8,128)(2,1)S(1)}, u32[]{:S(2)}, u32[]{:S(2)}) collective-permute-start(bf16[32,2048]{1,0:T(8,128)(2,1)S(1)} %get-tuple-element.17), channel_id=1, source_target_pairs={{0,4},{2,6},{4,8},{6,10},{8,12},{10,14},{12,0},{14,2},{1,5},{3,7},... | collective-permute-start | bytes 393224 | tf_op jit(solution)/shard_map/ppermute | solution.py:96

commit v2 on v1

--- a/solution.py
+++ b/solution.py
@@ -1,6 +1,8 @@
 import jax
 import jax.numpy as jnp
 from jax import lax
+from jax.experimental import pallas as pl
+from jax.experimental.pallas import tpu as pltpu
 from jax.sharding import PartitionSpec as P
 
 adapter_scale_factor = 2.0
@@ -28,6 +30,10 @@
     same_doc = document_index_per_token[:, None] == document_index_per_token[None, :]
     sequence_length = jnp.sum(same_doc.astype(jnp.float32), axis=1)
     return adapter_scale_factor / sequence_length
+
+
+def after(value, *others):
+    return lax.optimization_barrier((value,) + others)[0]
 
 
 def route_tokens(
@@ -77,6 +83,125 @@
     return (input_grad, grad_down[None], up_adapter_gradient[None])
 
 
+VMEM_LIMIT = 32 * 1024 * 1024
+
+
+def whole(*shape):
+    return pl.BlockSpec(shape, lambda _: (0,) * len(shape))
+
+
+def column_cut(rows, wide, at):
+    return pl.BlockSpec((rows, wide), lambda _: (0, at))
+
+
+def cost(flops, moved):
+    return pl.CostEstimate(flops=flops, bytes_accessed=moved, transcendentals=0)
+
+
+def join_kernel(layer_ref, own_ref, *refs):
+    *halves, out_ref = refs
+    count = len(halves) // 2
+    rank = own_ref.shape[0]
+    out_ref[:rank, :] = own_ref[...]
+    first = layer_ref[0] == 0
+    for step in range(count):
+        got, other = halves[step][...], halves[count + step][...]
+        low = (step + 1) * rank
+        middle = low + rank // 2
+        out_ref[low:middle, :] = jnp.where(first, got, other)
+        out_ref[middle : low + rank, :] = jnp.where(first, other, got)
+
+
+def join(layer, own, got, other):
+    rank, width = own.shape
+    rows = (len(got) + 1) * rank
+    return pl.pallas_call(
+        join_kernel,
+        grid=(1,),
+        out_shape=jax.ShapeDtypeStruct((rows, width), own.dtype),
+        in_specs=[pl.BlockSpec(memory_space=pltpu.SMEM), whole(rank, width)]
+        + [whole(rank // 2, width)] * (2 * len(got)),
+        out_specs=whole(rows, width),
+        compiler_params=pltpu.CompilerParams(vmem_limit_bytes=VMEM_LIMIT),
+        cost_estimate=cost(0, 4 * rows * width),
+    )(layer, own, *got, *other)
+
+
+def project_kernel(adapter_ref, own_ref, other_ref, held_ref, base_ref, out_ref):
+    columns, tokens = held_ref.shape
+    rows = tokens // 2
+    rank = adapter_ref.shape[0] // columns
+    adapters = adapter_ref[...]
+    for part, rows_ref in enumerate((own_ref, other_ref)):
+        cut = slice(part * rows, (part + 1) * rows)
+        low = contract_last(adapters, rows_ref[...])
+        total = base_ref[:, cut]
+        for step in range(columns):
+            total = total + jnp.where(
+                held_ref[step : step + 1, cut] > 0, low[step * rank : (step + 1) * rank], 0.0
+            )
+        out_ref[:, cut] = total
+
+
+def project(adapters, own_rows, other_rows, held, base, at):
+    rows, wide = other_rows.shape
+    height = adapters.shape[0]
+    return pl.pallas_call(
+        project_kernel,
+        grid=(1,),
+        out_shape=jax.ShapeDtypeStruct(base.shape, jnp.float32),
+        in_specs=[
+            column_cut(height, wide, at),
+            column_cut(rows, wide, at),
+            whole(rows, wide),
+            whole(*held.shape),
+            whole(*base.shape),
+        ],
+        out_specs=whole(*base.shape),
+        compiler_params=pltpu.CompilerParams(vmem_limit_bytes=VMEM_LIMIT),
+        cost_estimate=cost(4 * height * rows * wide, 2 * wide * (height + 2 * rows)),
+    )(adapters, own_rows, other_rows, held, base)
+
+
+def partial_kernel(scaled_ref, held_ref, own_ref, other_ref, sum_ref, *send_refs):
+    columns, tokens = held_ref.shape
+    rows = tokens // 2
+    rank = scaled_ref.shape[0]
+    scaled = scaled_ref[...]
+    left = jnp.concatenate(
+        [
+            jnp.where(held_ref[step : step + 1, :] > 0, scaled, 0.0).astype(jnp.bfloat16)
+            for step in range(columns)
+        ]
+    )
+    total = jnp.dot(left[:, :rows], own_ref[...], preferred_element_type=jnp.float32)
+    total = total + jnp.dot(left[:, rows:], other_ref[...], preferred_element_type=jnp.float32)
+    sum_ref[...] = total[:rank]
+    for step, send_ref in enumerate(send_refs):
+        send_ref[...] = total[(step + 1) * rank : (step + 2) * rank].astype(jnp.bfloat16)
+
+
+def partials(scaled, held, own_rows, other_rows, at):
+    columns, tokens = held.shape
+    rows, wide = other_rows.shape
+    rank = scaled.shape[0]
+    return pl.pallas_call(
+        partial_kernel,
+        grid=(1,),
+        out_shape=[jax.ShapeDtypeStruct((rank, wide), jnp.float32)]
+        + [jax.ShapeDtypeStruct((rank, wide), jnp.bfloat16)] * (columns - 1),
+        in_specs=[
+            whole(*scaled.shape),
+            whole(*held.shape),
+            column_cut(rows, wide, at),
+            whole(rows, wide),
+        ],
+        out_specs=[whole(rank, wide)] * columns,
+        compiler_params=pltpu.CompilerParams(vmem_limit_bytes=VMEM_LIMIT),
+        cost_estimate=cost(2 * columns * rank * tokens * wide, 8 * rows * wide),
+    )(scaled, held, own_rows, other_rows)
+
+
 def route_adapters(
     features, cotangent, tenant_ids, document_index_per_token, owner_map, adapter_down, adapter_up
 ):
@@ -101,75 +226,79 @@
     def swap_core(value):
         return lax.ppermute(value, "tensor", [(0, 1), (1, 0)])
 
-    def column_adapters(own):
-        mine = lax.dynamic_slice(own, (layer * half, 0), (half, width))
-        blocks = [own]
-        for step in range(1, columns):
-            got = shift(mine, -step)
-            other = swap_layer(got)
-            blocks.append(
-                jnp.where(
-                    layer == 0, jnp.concatenate([got, other]), jnp.concatenate([other, got])
-                )
-            )
-        return jnp.concatenate(blocks)
+    def half_rows(own):
+        return lax.dynamic_slice(own, (layer * half, 0), (half, width))
+
+    def fetch(own):
+        return [shift(half_rows(own), -step) for step in range(1, columns)]
+
+    def send(blocks):
+        return [shift(block, step) for step, block in enumerate(blocks, 1)]
+
+    def add(total, got):
+        for block in got:
+            total = total + block.astype(jnp.float32)
+        return total
+
+    pieces = 4
+    wide = width // pieces
+    layer_of = layer.astype(jnp.int32)[None]
+    other_x = swap_side(features)
+    down_got = fetch(adapter_down[0])
+    down_other = [swap_layer(got) for got in down_got]
+    up_own, cotangent, tenant_ids, document_index_per_token = lax.optimization_barrier(
+        (adapter_up[0], cotangent, tenant_ids, document_index_per_token) + tuple(down_got)
+    )[:4]
+    other_g = [swap_side(cotangent[:, i * wide : (i + 1) * wide]) for i in range(pieces)]
+    up_got = fetch(up_own)
+    down = join(layer_of, adapter_down[0], down_got, down_other)
 
     owner = token_owner(tenant_ids, owner_map)
     weight = token_weight(document_index_per_token)
     facts = jnp.stack([owner.astype(jnp.float32), weight])
-    facts = jnp.concatenate([facts, swap_side(facts)], axis=1)
+    facts = jnp.concatenate([facts, swap_side(after(facts, down))], axis=1)
     owner_here = facts[0].astype(jnp.int32)
     weight_here = facts[1]
     steps = jnp.arange(columns, dtype=jnp.int32)
     block_owner = ((place + steps) % columns) * 2 + side
     block_owner_there = block_owner + 1 - 2 * side
-    held = (block_owner[:, None] == owner_here[None, :])[:, None, :]
+    held = (block_owner[:, None] == owner_here[None, :]).astype(jnp.float32)
     own_held = (block_owner[:, None] == owner[None, :])[:, None, :]
     own_there = (block_owner_there[:, None] == owner[None, :])[:, None, :]
 
     def spread(low, mask):
         return jnp.where(mask, low[None], jnp.zeros((), low.dtype)).reshape(
-            mask.shape[0] * rank, low.shape[1]
+            columns * rank, low.shape[1]
         )
 
-    def project(adapters, own_rows, other_rows):
-        low = jnp.concatenate(
-            [contract_last(adapters, own_rows), contract_last(adapters, other_rows)], axis=1
-        ).reshape(columns, rank, 2 * rows)
-        low = jnp.sum(jnp.where(held, low, 0.0), axis=0)
-        low = low + swap_core(low)
-        return (low * weight_here[None, :]).astype(jnp.bfloat16)
-
-    def gradient(scaled, own_rows, other_rows, pieces):
-        left = spread(scaled, held)
-        wide = width // pieces
-        parts = []
-        for piece in range(pieces):
-            cut = slice(piece * wide, (piece + 1) * wide)
-            total = jnp.dot(
-                left[:, :rows], own_rows[:, cut], preferred_element_type=jnp.float32
-            ) + jnp.dot(left[:, rows:], other_rows[piece], preferred_element_type=jnp.float32)
-            sum_own = total[:rank]
-            for step in range(1, columns):
-                block = total[step * rank : (step + 1) * rank].astype(jnp.bfloat16)
-                sum_own = sum_own + shift(block, step).astype(jnp.float32)
-            parts.append(sum_own)
-        return jnp.concatenate(parts, axis=1)
-
-    pieces = 2
-    wide = width // pieces
-    other_x = [swap_side(features[:, i * wide : (i + 1) * wide]) for i in range(pieces)]
-    down = column_adapters(adapter_down[0])
-    up = column_adapters(adapter_up[0])
-    other_g = [swap_side(cotangent[:, i * wide : (i + 1) * wide]) for i in range(pieces)]
-    scaled_h = project(down, features, jnp.concatenate(other_x, axis=1))
-    up_adapter_gradient = gradient(scaled_h, cotangent, other_g, pieces)
-    scaled_u = project(up, cotangent, jnp.concatenate(other_g, axis=1))
-    grad_down = gradient(scaled_u, features, other_x, pieces)
-    down_there = swap_side(down)
-    back = swap_side(scaled_u[:, rows:])
+    def combine(low):
+        return ((low + swap_core(low)) * weight_here[None, :]).astype(jnp.bfloat16)
+
+    nothing = jnp.zeros((rank, 2 * rows), jnp.float32)
+    low_h = project(down, features, other_x, held, nothing, 0)
+    up_got = [after(got, low_h) for got in up_got]
+    up = join(layer_of, up_own, up_got, [swap_layer(got) for got in up_got])
+    scaled_h = combine(low_h)
+    low_u = nothing
+    totals, gots = [], []
+    for i in range(pieces):
+        if i > 1:
+            other_g[i] = after(other_g[i], *gots[i - 2])
+        total, *blocks = partials(scaled_h, held, cotangent, other_g[i], i)
+        other_g[i] = after(other_g[i], total)
+        totals.append(total)
+        gots.append(send(blocks))
+        low_u = project(up, cotangent, other_g[i], held, low_u, i)
+    low_u = after(low_u, *gots[pieces - 2])
+    scaled_u = combine(low_u)
+    total, *blocks = partials(scaled_u, held, features, other_x, 0)
+    got = send(blocks)
+    back = swap_side(after(scaled_u, total)[:, rows:])
+    down_there = swap_side(after(down, other_g[1]))
+    up_adapter_gradient = jnp.concatenate([add(*pair) for pair in zip(totals, gots)], axis=1)
     left = jnp.concatenate([spread(scaled_u[:, :rows], own_held), spread(back, own_there)])
     input_grad = contract_first(left, jnp.concatenate([down, down_there])).astype(jnp.bfloat16)
+    grad_down = add(total, got)
     return (input_grad, grad_down[None], up_adapter_gradient[None])
 
 

time: 141 us -> 106 us (0.75)
  the two profiles are of different devices: /device:TPU:0 before, /device:TPU:13 now
where the time goes in v2:
time: 106 us
  waiting for transfers between devices  57 us (54%)
  starting transfers between devices  37.1 us (35%)
  Pallas kernels  3.89 us (4%)
  other arithmetic  3.74 us (4%)
  local copies, waits for them, and re-layouts  1.98 us (2%)
  matrix products  1.44 us (1%)
    ppermute x21, waiting for transfers between devices, shift(): lax.ppermute(value, 'dp', [(i, (i + 2 * by) % ranks) for i in range(ranks)])  41.2 us
    ppermute x21, starting transfers between devices, shift(): lax.ppermute(value, 'dp', [(i, (i + 2 * by) % ranks) for i in range(ranks)])  19.5 us
    ppermute x6, waiting for transfers between devices, swap_layer(): return lax.ppermute(value, 'parts', [(0, 1), (1, 0)])  8.49 us
    ppermute x8, starting transfers between devices, swap_side(): return lax.ppermute(value, 'dp', [(i, i ^ 1) for i in range(ranks)])  8.47 us
    ppermute x8, waiting for transfers between devices, swap_side(): return lax.ppermute(value, 'dp', [(i, i ^ 1) for i in range(ranks)])  7.28 us
    ppermute x2, starting transfers between devices, swap_core(): return lax.ppermute(value, 'tensor', [(0, 1), (1, 0)])  5.6 us
    ppermute x6, starting transfers between devices, swap_layer(): return lax.ppermute(value, 'parts', [(0, 1), (1, 0)])  3.56 us
  transfers between devices with their start and end apart: 37, of which 16 were waited for; matrix products, arithmetic and copies ran while one was open for 4% of the time, Pallas kernels for 4%

profile of v2, /device:TPU:13, one launch (start us, length us, event | category | flops | bytes accessed | tf_op | source)
XLA Modules:
  0.0 106.0 jit_solution(8798566595358144208)
XLA Ops:
  0.6 0.9 dynamic-slice_bitcast_fusion
  1.6 1.3 %collective-permute-start.2 = (bf16[16,4096]{1,0:T(8,128)(2,1)S(1)}, bf16[16,4096]{1,0:T(8,128)(2,1)S(1)}, u32[]{:S(2)}, u32[]{:S(2)}) collective-permute-start(bf16[16,4096]{1,0:T(8,128)(2,1)S(1)} %dynamic-slice_bitcast_fusion), channel_id=1, source_target_pairs={{0,4},{2,6},{4,8},{6,10},{8,12},{10,14},{12,0},{14,2},{1,5},{3,7},... | collective-permute-start | bytes 393224 | tf_op jit(solution)/shard_map/ppermute | solution.py:221
  2.9 1.1 %collective-permute-start.1 = (bf16[16,4096]{1,0:T(8,128)(2,1)S(1)}, bf16[16,4096]{1,0:T(8,128)(2,1)S(1)}, u32[]{:S(2)}, u32[]{:S(2)}) collective-permute-start(bf16[16,4096]{1,0:T(8,128)(2,1)S(1)} %dynamic-slice_bitcast_fusion), channel_id=1, source_target_pairs={{0,8},{2,10},{4,12},{6,14},{8,0},{10,2},{12,4},{14,6},{1,9},{3,11}... | collective-permute-start | bytes 393224 | tf_op jit(solution)/shard_map/ppermute | solution.py:221
  4.0 1.4 %collective-permute-start = (bf16[16,4096]{1,0:T(8,128)(2,1)S(1)}, bf16[16,4096]{1,0:T(8,128)(2,1)S(1)}, u32[]{:S(2)}, u32[]{:S(2)}) collective-permute-start(bf16[16,4096]{1,0:T(8,128)(2,1)S(1)} %dynamic-slice_bitcast_fusion), channel_id=1, source_target_pairs={{0,12},{2,14},{4,0},{6,2},{8,4},{10,6},{12,8},{14,10},{1,13},{3,15... | collective-permute-start | bytes 393224 | tf_op jit(solution)/shard_map/ppermute | solution.py:221
  5.4 1.2 %collective-permute-start.7 = (bf16[128,4096]{1,0:T(8,128)(2,1)}, bf16[128,4096]{1,0:T(8,128)(2,1)S(1)}, u32[]{:S(2)}, u32[]{:S(2)}) collective-permute-start(bf16[128,4096]{1,0:T(8,128)(2,1)} %own_ref.11), channel_id=1, source_target_pairs={{0,2},{2,0},{4,6},{6,4},{8,10},{10,8},{12,14},{14,12},{1,3},{3,1},... | collective-permute-start | bytes 3145736 | tf_op jit(solution)/shard_map/ppermute | solution.py:218
  6.6 6.9 %collective-permute-done.1.refs_1_ = bf16[16,4096]{1,0:T(8,128)(2,1)S(1)} collective-permute-done((bf16[16,4096]{1,0:T(8,128)(2,1)S(1)}, bf16[16,4096]{1,0:T(8,128)(2,1)S(1)}, u32[]{:S(2)}, u32[]{:S(2)}) %collective-permute-start.1) | collective-permute-done | bytes 131104 | tf_op jit(solution)/shard_map/ppermute | solution.py:221
  13.5 2.8 %collective-permute-done.refs_0_ = bf16[16,4096]{1,0:T(8,128)(2,1)S(1)} collective-permute-done((bf16[16,4096]{1,0:T(8,128)(2,1)S(1)}, bf16[16,4096]{1,0:T(8,128)(2,1)S(1)}, u32[]{:S(2)}, u32[]{:S(2)}) %collective-permute-start) | collective-permute-done | bytes 131104 | tf_op jit(solution)/shard_map/ppermute | solution.py:221
  16.3 0.8 select_reduce_fusion
  17.1 0.9 convert_reduce_fusion
  18.0 0.3 collective-permute-start.6
  18.3 1.2 %collective-permute-start.5 = (bf16[16,4096]{1,0:T(8,128)(2,1)S(1)}, bf16[16,4096]{1,0:T(8,128)(2,1)S(1)}, u32[]{:S(2)}, u32[]{:S(2)}) collective-permute-start(bf16[16,4096]{1,0:T(8,128)(2,1)S(1)} %collective-permute-done.1.refs_1_), channel_id=1, source_target_pairs={{0,16},{16,0},{1,17},{17,1},{2,18},{18,2},{3,19},{19,3},{4,20},{20... | collective-permute-start | bytes 393224 | tf_op jit(solution)/shard_map/ppermute | solution.py:224
  19.5 0.2 collective-permute-start.4
  19.7 2.9 %collective-permute-done.6.refs_5_ = bf16[16,4096]{1,0:T(8,128)(2,1)S(1)} collective-permute-done((bf16[16,4096]{1,0:T(8,128)(2,1)S(1)}, bf16[16,4096]{1,0:T(8,128)(2,1)S(1)}, u32[]{:S(2)}, u32[]{:S(2)}) %collective-permute-start.6) | collective-permute-done | bytes 131104 | tf_op jit(solution)/shard_map/ppermute | solution.py:224
  22.6 2.8 %collective-permute-done.5.refs_4_ = bf16[16,4096]{1,0:T(8,128)(2,1)S(1)} collective-permute-done((bf16[16,4096]{1,0:T(8,128)(2,1)S(1)}, bf16[16,4096]{1,0:T(8,128)(2,1)S(1)}, u32[]{:S(2)}, u32[]{:S(2)}) %collective-permute-start.5) | collective-permute-done | bytes 131104 | tf_op jit(solution)/shard_map/ppermute | solution.py:224
  25.4 2.8 %collective-permute-done.4.refs_3_ = bf16[16,4096]{1,0:T(8,128)(2,1)S(1)} collective-permute-done((bf16[16,4096]{1,0:T(8,128)(2,1)S(1)}, bf16[16,4096]{1,0:T(8,128)(2,1)S(1)}, u32[]{:S(2)}, u32[]{:S(2)}) %collective-permute-start.4) | collective-permute-done | bytes 131104 | tf_op jit(solution)/shard_map/ppermute | solution.py:224
  28.2 0.9 copy-done.2
  29.3 1.3 %collective-permute-start.8 = (f32[2,128]{1,0:T(2,128)S(1)}, f32[2,128]{1,0:T(2,128)S(1)}, u32[]{:S(2)}, u32[]{:S(2)}) collective-permute-start(f32[2,128]{1,0:T(2,128)S(1)} %pad_maximum_fusion.1), channel_id=1, source_target_pairs={{0,2},{2,0},{4,6},{6,4},{8,10},{10,8},{12,14},{14,12},{1,3},{3,1},... | collective-permute-start | bytes 3080 | tf_op jit(solution)/shard_map/ppermute | solution.py:218
  30.5 0.1 fusion.11
  30.6 1.2 %collective-permute-start.21 = (bf16[128,1024]{1,0:T(8,128)(2,1)S(1)}, bf16[128,1024]{1,0:T(8,128)(2,1)S(1)}, u32[]{:S(2)}, u32[]{:S(2)}) collective-permute-start(bf16[128,1024]{1,0:T(8,128)(2,1)S(1)} %get-tuple-element.79), channel_id=1, source_target_pairs={{0,2},{2,0},{4,6},{6,4},{8,10},{10,8},{12,14},{14,12},{1,3},{3,1},... | collective-permute-start | bytes 786440 | tf_op jit(solution)/shard_map/ppermute | solution.py:218
  31.8 0.4 collective-permute-start.16
  32.3 0.7 shard_map.95
  33.0 2.2 %collective-permute-start.15 = (f32[32,256]{1,0:T(8,128)S(1)}, f32[32,256]{1,0:T(8,128)S(1)}, u32[]{:S(2)}, u32[]{:S(2)}) collective-permute-start(f32[32,256]{1,0:T(8,128)S(1)} %shard_map.95), channel_id=1, source_target_pairs={{0,1},{1,0},{2,3},{3,2},{4,5},{5,4},{6,7},{7,6},{8,9},{9,8},{10,11... | collective-permute-start | bytes 98312 | tf_op jit(solution)/shard_map/ppermute | solution.py:227
  35.3 0.4 collective-permute-start.9
  35.8 1.1 %collective-permute-done.21.other_ref = bf16[128,1024]{1,0:T(8,128)(2,1)S(1)} collective-permute-done((bf16[128,1024]{1,0:T(8,128)(2,1)S(1)}, bf16[128,1024]{1,0:T(8,128)(2,1)S(1)}, u32[]{:S(2)}, u32[]{:S(2)}) %collective-permute-start.21) | collective-permute-done | bytes 262176 | tf_op jit(solution)/shard_map/ppermute | solution.py:218
  36.9 0.2 collective-permute-start.3
  37.1 1.2 %collective-permute-start.20 = (bf16[128,1024]{1,0:T(8,128)(2,1)S(1)}, bf16[128,1024]{1,0:T(8,128)(2,1)S(1)}, u32[]{:S(2)}, u32[]{:S(2)}) collective-permute-start(bf16[128,1024]{1,0:T(8,128)(2,1)S(1)} %get-tuple-element.80), channel_id=1, source_target_pairs={{0,2},{2,0},{4,6},{6,4},{8,10},{10,8},{12,14},{14,12},{1,3},{3,1},... | collective-permute-start | bytes 786440 | tf_op jit(solution)/shard_map/ppermute | solution.py:218
  38.3 0.3 shard_map.99
  38.6 1.6 %collective-permute-done.10.refs_2_ = bf16[16,4096]{1,0:T(8,128)(2,1)S(1)} collective-permute-done((bf16[16,4096]{1,0:T(8,128)(2,1)S(1)}, bf16[16,4096]{1,0:T(8,128)(2,1)S(1)}, u32[]{:S(2)}, u32[]{:S(2)}) %collective-permute-start.10) | collective-permute-done | bytes 131104 | tf_op jit(solution)/shard_map/ppermute | solution.py:221
  40.3 1.1 %collective-permute-start.14 = (bf16[128,1024]{1,0:T(8,128)(2,1)S(1)}, bf16[128,1024]{1,0:T(8,128)(2,1)S(1)}, u32[]{:S(2)}, u32[]{:S(2)}) collective-permute-start(bf16[128,1024]{1,0:T(8,128)(2,1)S(1)} %get-tuple-element.82), channel_id=1, source_target_pairs={{0,2},{2,0},{4,6},{6,4},{8,10},{10,8},{12,14},{14,12},{1,3},{3,1},... | collective-permute-start | bytes 786440 | tf_op jit(solution)/shard_map/ppermute | solution.py:218
  41.4 5.4 %collective-permute-done.9.refs_1_ = bf16[16,4096]{1,0:T(8,128)(2,1)S(1)} collective-permute-done((bf16[16,4096]{1,0:T(8,128)(2,1)S(1)}, bf16[16,4096]{1,0:T(8,128)(2,1)S(1)}, u32[]{:S(2)}, u32[]{:S(2)}) %collective-permute-start.9) | collective-permute-done | bytes 131104 | tf_op jit(solution)/shard_map/ppermute | solution.py:221
  46.7 1.5 %collective-permute-done.3.refs_0_ = bf16[16,4096]{1,0:T(8,128)(2,1)S(1)} collective-permute-done((bf16[16,4096]{1,0:T(8,128)(2,1)S(1)}, bf16[16,4096]{1,0:T(8,128)(2,1)S(1)}, u32[]{:S(2)}, u32[]{:S(2)}) %collective-permute-start.3) | collective-permute-done | bytes 131104 | tf_op jit(solution)/shard_map/ppermute | solution.py:221
  48.2 1.6 %collective-permute-start.23 = (bf16[32,1024]{1,0:T(8,128)(2,1)S(1)}, bf16[32,1024]{1,0:T(8,128)(2,1)S(1)}, u32[]{:S(2)}, u32[]{:S(2)}) collective-permute-start(bf16[32,1024]{1,0:T(8,128)(2,1)S(1)} %get-tuple-element.55), channel_id=1, source_target_pairs={{0,8},{2,10},{4,12},{6,14},{8,0},{10,2},{12,4},{14,6},{1,9},{3,11}... | collective-permute-start | bytes 196616 | tf_op jit(solution)/shard_map/ppermute | solution.py:221
  49.8 1.5 %collective-permute-start.24 = (bf16[32,1024]{1,0:T(8,128)(2,1)S(1)}, bf16[32,1024]{1,0:T(8,128)(2,1)S(1)}, u32[]{:S(2)}, u32[]{:S(2)}) collective-permute-start(bf16[32,1024]{1,0:T(8,128)(2,1)S(1)} %get-tuple-element.56), channel_id=1, source_target_pairs={{0,12},{2,14},{4,0},{6,2},{8,4},{10,6},{12,8},{14,10},{1,13},{3,15... | collective-permute-start | bytes 196616 | tf_op jit(solution)/shard_map/ppermute | solution.py:221
  51.3 0.1 broadcast_compare_fusion.1
  51.4 0.3 shard_map.97
  51.7 0.3 collective-permute-start.11
  52.0 0.8 collective-permute-done.23
  52.8 2.0 %collective-permute-start.18 = (bf16[32,1024]{1,0:T(8,128)(2,1)S(1)}, bf16[32,1024]{1,0:T(8,128)(2,1)S(1)}, u32[]{:S(2)}, u32[]{:S(2)}) collective-permute-start(bf16[32,1024]{1,0:T(8,128)(2,1)S(1)} %get-tuple-element.49), channel_id=1, source_target_pairs={{0,8},{2,10},{4,12},{6,14},{8,0},{10,2},{12,4},{14,6},{1,9},{3,11}... | collective-permute-start | bytes 196616 | tf_op jit(solution)/shard_map/ppermute | solution.py:221
  54.8 3.2 %collective-permute-done.24 = bf16[32,1024]{1,0:T(8,128)(2,1)S(1)} collective-permute-done((bf16[32,1024]{1,0:T(8,128)(2,1)S(1)}, bf16[32,1024]{1,0:T(8,128)(2,1)S(1)}, u32[]{:S(2)}, u32[]{:S(2)}) %collective-permute-start.24) | collective-permute-done | bytes 65568 | tf_op jit(solution)/shard_map/ppermute | solution.py:221
  58.0 0.3 shard_map.100
  58.4 1.4 %collective-permute-start.13 = (bf16[16,4096]{1,0:T(8,128)(2,1)S(1)}, bf16[16,4096]{1,0:T(8,128)(2,1)S(1)}, u32[]{:S(2)}, u32[]{:S(2)}) collective-permute-start(bf16[16,4096]{1,0:T(8,128)(2,1)S(1)} %collective-permute-done.10.refs_2_), channel_id=1, source_target_pairs={{0,16},{16,0},{1,17},{17,1},{2,18},{18,2},{3,19},{19,3},{4,20},{20... | collective-permute-start | bytes 393224 | tf_op jit(solution)/shard_map/ppermute | solution.py:224
  59.9 1.5 %collective-permute-start.25 = (bf16[32,1024]{1,0:T(8,128)(2,1)S(1)}, bf16[32,1024]{1,0:T(8,128)(2,1)S(1)}, u32[]{:S(2)}, u32[]{:S(2)}) collective-permute-start(bf16[32,1024]{1,0:T(8,128)(2,1)S(1)} %get-tuple-element.64), channel_id=1, source_target_pairs={{0,4},{2,6},{4,8},{6,10},{8,12},{10,14},{12,0},{14,2},{1,5},{3,7},... | collective-permute-start | bytes 196616 | tf_op jit(solution)/shard_map/ppermute | solution.py:221
  61.3 0.7 collective-permute-done.19
  62.0 1.8 %collective-permute-start.26 = (bf16[32,1024]{1,0:T(8,128)(2,1)S(1)}, bf16[32,1024]{1,0:T(8,128)(2,1)S(1)}, u32[]{:S(2)}, u32[]{:S(2)}) collective-permute-start(bf16[32,1024]{1,0:T(8,128)(2,1)S(1)} %get-tuple-element.65), channel_id=1, source_target_pairs={{0,8},{2,10},{4,12},{6,14},{8,0},{10,2},{12,4},{14,6},{1,9},{3,11}... | collective-permute-start | bytes 196616 | tf_op jit(solution)/shard_map/ppermute | solution.py:221
  63.9 0.3 shard_map.98
  64.2 1.2 %collective-permute-start.30 = (bf16[128,4096]{1,0:T(8,128)(2,1)S(1)}, bf16[128,4096]{1,0:T(8,128)(2,1)S(1)}, u32[]{:S(2)}, u32[]{:S(2)}) collective-permute-start(bf16[128,4096]{1,0:T(8,128)(2,1)S(1)} %shard_map.94.adapter_ref), channel_id=1, source_target_pairs={{0,2},{2,0},{4,6},{6,4},{8,10},{10,8},{12,14},{14,12},{1,3},{3,1},... | collective-permute-start | bytes 3145736 | tf_op jit(solution)/shard_map/ppermute | solution.py:218
  65.3 1.5 %collective-permute-start.34 = (bf16[32,1024]{1,0:T(8,128)(2,1)S(1)}, bf16[32,1024]{1,0:T(8,128)(2,1)S(1)}, u32[]{:S(2)}, u32[]{:S(2)}) collective-permute-start(bf16[32,1024]{1,0:T(8,128)(2,1)S(1)} %get-tuple-element.74), channel_id=1, source_target_pairs={{0,4},{2,6},{4,8},{6,10},{8,12},{10,14},{12,0},{14,2},{1,5},{3,7},... | collective-permute-start | bytes 196616 | tf_op jit(solution)/shard_map/ppermute | solution.py:221
  66.9 0.3 shard_map.101.base_ref
  67.2 0.3 shard_map.102.base_ref
  67.5 0.3 shard_map.103.base_ref
  67.8 0.3 shard_map.104
  68.1 2.4 %collective-permute-start.35 = (bf16[32,1024]{1,0:T(8,128)(2,1)S(1)}, bf16[32,1024]{1,0:T(8,128)(2,1)S(1)}, u32[]{:S(2)}, u32[]{:S(2)}) collective-permute-start(bf16[32,1024]{1,0:T(8,128)(2,1)S(1)} %get-tuple-element.75), channel_id=1, source_target_pairs={{0,8},{2,10},{4,12},{6,14},{8,0},{10,2},{12,4},{14,6},{1,9},{3,11}... | collective-permute-start | bytes 196616 | tf_op jit(solution)/shard_map/ppermute | solution.py:221
  70.5 3.4 %collective-permute-start.28 = (f32[32,256]{1,0:T(8,128)S(1)}, f32[32,256]{1,0:T(8,128)S(1)}, u32[]{:S(2)}, u32[]{:S(2)}) collective-permute-start(f32[32,256]{1,0:T(8,128)S(1)} %shard_map.104), channel_id=1, source_target_pairs={{0,1},{1,0},{2,3},{3,2},{4,5},{5,4},{6,7},{7,6},{8,9},{9,8},{10,11... | collective-permute-start | bytes 98312 | tf_op jit(solution)/shard_map/ppermute | solution.py:227
  74.0 0.9 collective-permute-done.36
  74.9 0.8 maximum_bitcast_fusion
  75.8 0.7 shard_map.105
  76.5 0.9 collective-permute-start.29
  77.4 0.3 collective-permute-start.31
  77.7 2.4 %collective-permute-start.32 = (bf16[32,4096]{1,0:T(8,128)(2,1)S(1)}, bf16[32,4096]{1,0:T(8,128)(2,1)S(1)}, u32[]{:S(2)}, u32[]{:S(2)}) collective-permute-start(bf16[32,4096]{1,0:T(8,128)(2,1)S(1)} %get-tuple-element.72), channel_id=1, source_target_pairs={{0,8},{2,10},{4,12},{6,14},{8,0},{10,2},{12,4},{14,6},{1,9},{3,11}... | collective-permute-start | bytes 786440 | tf_op jit(solution)/shard_map/ppermute | solution.py:221
  80.1 6.1 %collective-permute-done.29 = bf16[32,128]{1,0:T(8,128)(2,1)S(1)} collective-permute-done((bf16[32,128]{1,0:T(8,128)(2,1)S(1)}, bf16[32,128]{1,0:T(8,128)(2,1)S(1)}, u32[]{:S(2)}, u32[]{:S(2)}) %collective-permute-start.29) | collective-permute-done | bytes 8224 | tf_op jit(solution)/shard_map/ppermute | solution.py:218
  86.3 11.4 %collective-permute-done.32 = bf16[32,4096]{1,0:T(8,128)(2,1)S(1)} collective-permute-done((bf16[32,4096]{1,0:T(8,128)(2,1)S(1)}, bf16[32,4096]{1,0:T(8,128)(2,1)S(1)}, u32[]{:S(2)}, u32[]{:S(2)}) %collective-permute-start.32) | collective-permute-done | bytes 262176 | tf_op jit(solution)/shard_map/ppermute | solution.py:221
  97.7 6.0 %collective-permute-done.33 = bf16[32,4096]{1,0:T(8,128)(2,1)S(1)} collective-permute-done((bf16[32,4096]{1,0:T(8,128)(2,1)S(1)}, bf16[32,4096]{1,0:T(8,128)(2,1)S(1)}, u32[]{:S(2)}, u32[]{:S(2)}) %collective-permute-start.33) | collective-permute-done | bytes 262176 | tf_op jit(solution)/shard_map/ppermute | solution.py:221
  103.7 0.9 add_bitcast_fusion
  104.6 1.4 %convolution_convert_fusion = bf16[128,4096]{1,0:T(8,128)(2,1)} fusion(bf16[128,4096]{1,0:T(8,128)(2,1)S(1)} %collective-permute-done.30, bf16[128,4096]{1,0:T(8,128)(2,1)S(1)} %shard_map.94.adapter_ref, bf16[128,128]{1,0:T(8,128)(2,1)S(1)} %bitcast.21, bf16[128,128]{1,0:T(8,128)(2,1)S(1)} %bitcast.20), kind=kOutput, calls=%fused_computation | convolution fusion | flops 273285120 | bytes 3211264 | tf_op jit(solution)/shard_map/dot_general | solution.py:18
  (57 shorter events, 0.7 us)
Async XLA Ops:
  1.6 5.1 %collective-permute-start.2 = (bf16[16,4096]{1,0:T(8,128)(2,1)S(1)}, bf16[16,4096]{1,0:T(8,128)(2,1)S(1)}, u32[]{:S(2)}, u32[]{:S(2)}) collective-permute-start(bf16[16,4096]{1,0:T(8,128)(2,1)S(1)} %dynamic-slice_bitcast_fusion), channel_id=1, source_target_pairs={{0,4},{2,6},{4,8},{6,10},{8,12},{10,14},{12,0},{14,2},{1,5},{3,7},... | collective-permute-start | bytes 393224 | tf_op jit(solution)/shard_map/ppermute | solution.py:221
  2.9 10.6 %collective-permute-start.1 = (bf16[16,4096]{1,0:T(8,128)(2,1)S(1)}, bf16[16,4096]{1,0:T(8,128)(2,1)S(1)}, u32[]{:S(2)}, u32[]{:S(2)}) collective-permute-start(bf16[16,4096]{1,0:T(8,128)(2,1)S(1)} %dynamic-slice_bitcast_fusion), channel_id=1, source_target_pairs={{0,8},{2,10},{4,12},{6,14},{8,0},{10,2},{12,4},{14,6},{1,9},{3,11}... | collective-permute-start | bytes 393224 | tf_op jit(solution)/shard_map/ppermute | solution.py:221
  4.0 12.3 %collective-permute-start = (bf16[16,4096]{1,0:T(8,128)(2,1)S(1)}, bf16[16,4096]{1,0:T(8,128)(2,1)S(1)}, u32[]{:S(2)}, u32[]{:S(2)}) collective-permute-start(bf16[16,4096]{1,0:T(8,128)(2,1)S(1)} %dynamic-slice_bitcast_fusion), channel_id=1, source_target_pairs={{0,12},{2,14},{4,0},{6,2},{8,4},{10,6},{12,8},{14,10},{1,13},{3,15... | collective-permute-start | bytes 393224 | tf_op jit(solution)/shard_map/ppermute | solution.py:221
  5.4 26.9 %collective-permute-start.7 = (bf16[128,4096]{1,0:T(8,128)(2,1)}, bf16[128,4096]{1,0:T(8,128)(2,1)S(1)}, u32[]{:S(2)}, u32[]{:S(2)}) collective-permute-start(bf16[128,4096]{1,0:T(8,128)(2,1)} %own_ref.11), channel_id=1, source_target_pairs={{0,2},{2,0},{4,6},{6,4},{8,10},{10,8},{12,14},{14,12},{1,3},{3,1},... | collective-permute-start | bytes 3145736 | tf_op jit(solution)/shard_map/ppermute | solution.py:218
  18.0 4.6 %collective-permute-start.6 = (bf16[16,4096]{1,0:T(8,128)(2,1)S(1)}, bf16[16,4096]{1,0:T(8,128)(2,1)S(1)}, u32[]{:S(2)}, u32[]{:S(2)}) collective-permute-start(bf16[16,4096]{1,0:T(8,128)(2,1)S(1)} %collective-permute-done.2.refs_2_), channel_id=1, source_target_pairs={{0,16},{16,0},{1,17},{17,1},{2,18},{18,2},{3,19},{19,3},{4,20},{20... | collective-permute-start | bytes 393224 | tf_op jit(solution)/shard_map/ppermute | solution.py:224
  18.3 7.2 %collective-permute-start.5 = (bf16[16,4096]{1,0:T(8,128)(2,1)S(1)}, bf16[16,4096]{1,0:T(8,128)(2,1)S(1)}, u32[]{:S(2)}, u32[]{:S(2)}) collective-permute-start(bf16[16,4096]{1,0:T(8,128)(2,1)S(1)} %collective-permute-done.1.refs_1_), channel_id=1, source_target_pairs={{0,16},{16,0},{1,17},{17,1},{2,18},{18,2},{3,19},{19,3},{4,20},{20... | collective-permute-start | bytes 393224 | tf_op jit(solution)/shard_map/ppermute | solution.py:224
  19.5 8.7 %collective-permute-start.4 = (bf16[16,4096]{1,0:T(8,128)(2,1)S(1)}, bf16[16,4096]{1,0:T(8,128)(2,1)S(1)}, u32[]{:S(2)}, u32[]{:S(2)}) collective-permute-start(bf16[16,4096]{1,0:T(8,128)(2,1)S(1)} %collective-permute-done.refs_0_), channel_id=1, source_target_pairs={{0,16},{16,0},{1,17},{17,1},{2,18},{18,2},{3,19},{19,3},{4,20},{20... | collective-permute-start | bytes 393224 | tf_op jit(solution)/shard_map/ppermute | solution.py:224
  28.2 1.0 copy-start.2
  29.2 1.4 %copy-start = (bf16[128,4096]{1,0:T(8,128)(2,1)S(1)}, bf16[128,4096]{1,0:T(8,128)(2,1)}, u32[]{:S(2)}) copy-start(bf16[128,4096]{1,0:T(8,128)(2,1)} %own_ref.10) | copy-start | bytes 3145732
  29.3 3.0 %copy-start.1 = (bf16[128,4096]{1,0:T(8,128)(2,1)S(1)}, bf16[128,4096]{1,0:T(8,128)(2,1)}, u32[]{:S(2)}) copy-start(bf16[128,4096]{1,0:T(8,128)(2,1)} %own_ref.11) | copy-start | bytes 3145732
  29.3 2.9 %collective-permute-start.8 = (f32[2,128]{1,0:T(2,128)S(1)}, f32[2,128]{1,0:T(2,128)S(1)}, u32[]{:S(2)}, u32[]{:S(2)}) collective-permute-start(f32[2,128]{1,0:T(2,128)S(1)} %pad_maximum_fusion.1), channel_id=1, source_target_pairs={{0,2},{2,0},{4,6},{6,4},{8,10},{10,8},{12,14},{14,12},{1,3},{3,1},... | collective-permute-start | bytes 3080 | tf_op jit(solution)/shard_map/ppermute | solution.py:218
  30.6 6.3 %collective-permute-start.21 = (bf16[128,1024]{1,0:T(8,128)(2,1)S(1)}, bf16[128,1024]{1,0:T(8,128)(2,1)S(1)}, u32[]{:S(2)}, u32[]{:S(2)}) collective-permute-start(bf16[128,1024]{1,0:T(8,128)(2,1)S(1)} %get-tuple-element.79), channel_id=1, source_target_pairs={{0,2},{2,0},{4,6},{6,4},{8,10},{10,8},{12,14},{14,12},{1,3},{3,1},... | collective-permute-start | bytes 786440 | tf_op jit(solution)/shard_map/ppermute | solution.py:218
  31.8 18.0 %collective-permute-start.16 = (bf16[128,1024]{1,0:T(8,128)(2,1)S(1)}, bf16[128,1024]{1,0:T(8,128)(2,1)S(1)}, u32[]{:S(2)}, u32[]{:S(2)}) collective-permute-start(bf16[128,1024]{1,0:T(8,128)(2,1)S(1)} %get-tuple-element.81), channel_id=1, source_target_pairs={{0,2},{2,0},{4,6},{6,4},{8,10},{10,8},{12,14},{14,12},{1,3},{3,1},... | collective-permute-start | bytes 786440 | tf_op jit(solution)/shard_map/ppermute | solution.py:218
  32.3 3.0 %copy-start.3 = (bf16[1,32,4096]{2,1,0:T(8,128)(2,1)S(1)}, bf16[1,32,4096]{2,1,0:T(8,128)(2,1)}, u32[]{:S(2)}) copy-start(bf16[1,32,4096]{2,1,0:T(8,128)(2,1)} %param.13) | copy-start | bytes 786436
  33.0 4.1 %collective-permute-start.15 = (f32[32,256]{1,0:T(8,128)S(1)}, f32[32,256]{1,0:T(8,128)S(1)}, u32[]{:S(2)}, u32[]{:S(2)}) collective-permute-start(f32[32,256]{1,0:T(8,128)S(1)} %shard_map.95), channel_id=1, source_target_pairs={{0,1},{1,0},{2,3},{3,2},{4,5},{5,4},{6,7},{7,6},{8,9},{9,8},{10,11... | collective-permute-start | bytes 98312 | tf_op jit(solution)/shard_map/ppermute | solution.py:227
  35.3 5.0 %collective-permute-start.10 = (bf16[16,4096]{1,0:T(8,128)(2,1)S(1)}, bf16[16,4096]{1,0:T(8,128)(2,1)S(1)}, u32[]{:S(2)}, u32[]{:S(2)}) collective-permute-start(bf16[16,4096]{1,0:T(8,128)(2,1)S(1)} %constant_dynamic-slice_fusion), channel_id=1, source_target_pairs={{0,4},{2,6},{4,8},{6,10},{8,12},{10,14},{12,0},{14,2},{1,5},{3,7},... | collective-permute-start | bytes 393224 | tf_op jit(solution)/shard_map/ppermute | solution.py:221
  35.3 11.4 %collective-permute-start.9 = (bf16[16,4096]{1,0:T(8,128)(2,1)S(1)}, bf16[16,4096]{1,0:T(8,128)(2,1)S(1)}, u32[]{:S(2)}, u32[]{:S(2)}) collective-permute-start(bf16[16,4096]{1,0:T(8,128)(2,1)S(1)} %constant_dynamic-slice_fusion), channel_id=1, source_target_pairs={{0,8},{2,10},{4,12},{6,14},{8,0},{10,2},{12,4},{14,6},{1,9},{3,11}... | collective-permute-start | bytes 393224 | tf_op jit(solution)/shard_map/ppermute | solution.py:221
  36.9 11.3 %collective-permute-start.3 = (bf16[16,4096]{1,0:T(8,128)(2,1)S(1)}, bf16[16,4096]{1,0:T(8,128)(2,1)S(1)}, u32[]{:S(2)}, u32[]{:S(2)}) collective-permute-start(bf16[16,4096]{1,0:T(8,128)(2,1)S(1)} %constant_dynamic-slice_fusion), channel_id=1, source_target_pairs={{0,12},{2,14},{4,0},{6,2},{8,4},{10,6},{12,8},{14,10},{1,13},{3,15... | collective-permute-start | bytes 393224 | tf_op jit(solution)/shard_map/ppermute | solution.py:221
  37.1 14.6 %collective-permute-start.20 = (bf16[128,1024]{1,0:T(8,128)(2,1)S(1)}, bf16[128,1024]{1,0:T(8,128)(2,1)S(1)}, u32[]{:S(2)}, u32[]{:S(2)}) collective-permute-start(bf16[128,1024]{1,0:T(8,128)(2,1)S(1)} %get-tuple-element.80), channel_id=1, source_target_pairs={{0,2},{2,0},{4,6},{6,4},{8,10},{10,8},{12,14},{14,12},{1,3},{3,1},... | collective-permute-start | bytes 786440 | tf_op jit(solution)/shard_map/ppermute | solution.py:218
  40.3 18.1 %collective-permute-start.14 = (bf16[128,1024]{1,0:T(8,128)(2,1)S(1)}, bf16[128,1024]{1,0:T(8,128)(2,1)S(1)}, u32[]{:S(2)}, u32[]{:S(2)}) collective-permute-start(bf16[128,1024]{1,0:T(8,128)(2,1)S(1)} %get-tuple-element.82), channel_id=1, source_target_pairs={{0,2},{2,0},{4,6},{6,4},{8,10},{10,8},{12,14},{14,12},{1,3},{3,1},... | collective-permute-start | bytes 786440 | tf_op jit(solution)/shard_map/ppermute | solution.py:218
  46.7 5.2 %collective-permute-start.22 = (bf16[32,1024]{1,0:T(8,128)(2,1)S(1)}, bf16[32,1024]{1,0:T(8,128)(2,1)S(1)}, u32[]{:S(2)}, u32[]{:S(2)}) collective-permute-start(bf16[32,1024]{1,0:T(8,128)(2,1)S(1)} %get-tuple-element.54), channel_id=1, source_target_pairs={{0,4},{2,6},{4,8},{6,10},{8,12},{10,14},{12,0},{14,2},{1,5},{3,7},... | collective-permute-start | bytes 196616 | tf_op jit(solution)/shard_map/ppermute | solution.py:221
  48.2 4.6 %collective-permute-start.23 = (bf16[32,1024]{1,0:T(8,128)(2,1)S(1)}, bf16[32,1024]{1,0:T(8,128)(2,1)S(1)}, u32[]{:S(2)}, u32[]{:S(2)}) collective-permute-start(bf16[32,1024]{1,0:T(8,128)(2,1)S(1)} %get-tuple-element.55), channel_id=1, source_target_pairs={{0,8},{2,10},{4,12},{6,14},{8,0},{10,2},{12,4},{14,6},{1,9},{3,11}... | collective-permute-start | bytes 196616 | tf_op jit(solution)/shard_map/ppermute | solution.py:221
  49.8 8.2 %collective-permute-start.24 = (bf16[32,1024]{1,0:T(8,128)(2,1)S(1)}, bf16[32,1024]{1,0:T(8,128)(2,1)S(1)}, u32[]{:S(2)}, u32[]{:S(2)}) collective-permute-start(bf16[32,1024]{1,0:T(8,128)(2,1)S(1)} %get-tuple-element.56), channel_id=1, source_target_pairs={{0,12},{2,14},{4,0},{6,2},{8,4},{10,6},{12,8},{14,10},{1,13},{3,15... | collective-permute-start | bytes 196616 | tf_op jit(solution)/shard_map/ppermute | solution.py:221
  51.7 12.1 %collective-permute-start.11 = (bf16[16,4096]{1,0:T(8,128)(2,1)S(1)}, bf16[16,4096]{1,0:T(8,128)(2,1)S(1)}, u32[]{:S(2)}, u32[]{:S(2)}) collective-permute-start(bf16[16,4096]{1,0:T(8,128)(2,1)S(1)} %collective-permute-done.3.refs_0_), channel_id=1, source_target_pairs={{0,16},{16,0},{1,17},{17,1},{2,18},{18,2},{3,19},{19,3},{4,20},{20... | collective-permute-start | bytes 393224 | tf_op jit(solution)/shard_map/ppermute | solution.py:224
  52.0 6.4 %collective-permute-start.17 = (bf16[32,1024]{1,0:T(8,128)(2,1)S(1)}, bf16[32,1024]{1,0:T(8,128)(2,1)S(1)}, u32[]{:S(2)}, u32[]{:S(2)}) collective-permute-start(bf16[32,1024]{1,0:T(8,128)(2,1)S(1)} %get-tuple-element.48), channel_id=1, source_target_pairs={{0,4},{2,6},{4,8},{6,10},{8,12},{10,14},{12,0},{14,2},{1,5},{3,7},... | collective-permute-start | bytes 196616 | tf_op jit(solution)/shard_map/ppermute | solution.py:221
  52.8 7.1 %collective-permute-start.18 = (bf16[32,1024]{1,0:T(8,128)(2,1)S(1)}, bf16[32,1024]{1,0:T(8,128)(2,1)S(1)}, u32[]{:S(2)}, u32[]{:S(2)}) collective-permute-start(bf16[32,1024]{1,0:T(8,128)(2,1)S(1)} %get-tuple-element.49), channel_id=1, source_target_pairs={{0,8},{2,10},{4,12},{6,14},{8,0},{10,2},{12,4},{14,6},{1,9},{3,11}... | collective-permute-start | bytes 196616 | tf_op jit(solution)/shard_map/ppermute | solution.py:221
  58.0 4.0 %collective-permute-start.19 = (bf16[32,1024]{1,0:T(8,128)(2,1)S(1)}, bf16[32,1024]{1,0:T(8,128)(2,1)S(1)}, u32[]{:S(2)}, u32[]{:S(2)}) collective-permute-start(bf16[32,1024]{1,0:T(8,128)(2,1)S(1)} %get-tuple-element.50), channel_id=1, source_target_pairs={{0,12},{2,14},{4,0},{6,2},{8,4},{10,6},{12,8},{14,10},{1,13},{3,15... | collective-permute-start | bytes 196616 | tf_op jit(solution)/shard_map/ppermute | solution.py:221
  58.3 5.8 %collective-permute-start.12 = (bf16[16,4096]{1,0:T(8,128)(2,1)S(1)}, bf16[16,4096]{1,0:T(8,128)(2,1)S(1)}, u32[]{:S(2)}, u32[]{:S(2)}) collective-permute-start(bf16[16,4096]{1,0:T(8,128)(2,1)S(1)} %collective-permute-done.9.refs_1_), channel_id=1, source_target_pairs={{0,16},{16,0},{1,17},{17,1},{2,18},{18,2},{3,19},{19,3},{4,20},{20... | collective-permute-start | bytes 393224 | tf_op jit(solution)/shard_map/ppermute | solution.py:224
  58.4 6.9 %collective-permute-start.13 = (bf16[16,4096]{1,0:T(8,128)(2,1)S(1)}, bf16[16,4096]{1,0:T(8,128)(2,1)S(1)}, u32[]{:S(2)}, u32[]{:S(2)}) collective-permute-start(bf16[16,4096]{1,0:T(8,128)(2,1)S(1)} %collective-permute-done.10.refs_2_), channel_id=1, source_target_pairs={{0,16},{16,0},{1,17},{17,1},{2,18},{18,2},{3,19},{19,3},{4,20},{20... | collective-permute-start | bytes 393224 | tf_op jit(solution)/shard_map/ppermute | solution.py:224
  59.9 8.2 %collective-permute-start.25 = (bf16[32,1024]{1,0:T(8,128)(2,1)S(1)}, bf16[32,1024]{1,0:T(8,128)(2,1)S(1)}, u32[]{:S(2)}, u32[]{:S(2)}) collective-permute-start(bf16[32,1024]{1,0:T(8,128)(2,1)S(1)} %get-tuple-element.64), channel_id=1, source_target_pairs={{0,4},{2,6},{4,8},{6,10},{8,12},{10,14},{12,0},{14,2},{1,5},{3,7},... | collective-permute-start | bytes 196616 | tf_op jit(solution)/shard_map/ppermute | solution.py:221
  62.0 8.5 %collective-permute-start.26 = (bf16[32,1024]{1,0:T(8,128)(2,1)S(1)}, bf16[32,1024]{1,0:T(8,128)(2,1)S(1)}, u32[]{:S(2)}, u32[]{:S(2)}) collective-permute-start(bf16[32,1024]{1,0:T(8,128)(2,1)S(1)} %get-tuple-element.65), channel_id=1, source_target_pairs={{0,8},{2,10},{4,12},{6,14},{8,0},{10,2},{12,4},{14,6},{1,9},{3,11}... | collective-permute-start | bytes 196616 | tf_op jit(solution)/shard_map/ppermute | solution.py:221
  63.8 6.7 %collective-permute-start.27 = (bf16[32,1024]{1,0:T(8,128)(2,1)S(1)}, bf16[32,1024]{1,0:T(8,128)(2,1)S(1)}, u32[]{:S(2)}, u32[]{:S(2)}) collective-permute-start(bf16[32,1024]{1,0:T(8,128)(2,1)S(1)} %get-tuple-element.66), channel_id=1, source_target_pairs={{0,12},{2,14},{4,0},{6,2},{8,4},{10,6},{12,8},{14,10},{1,13},{3,15... | collective-permute-start | bytes 196616 | tf_op jit(solution)/shard_map/ppermute | solution.py:221
  64.2 40.4 %collective-permute-start.30 = (bf16[128,4096]{1,0:T(8,128)(2,1)S(1)}, bf16[128,4096]{1,0:T(8,128)(2,1)S(1)}, u32[]{:S(2)}, u32[]{:S(2)}) collective-permute-start(bf16[128,4096]{1,0:T(8,128)(2,1)S(1)} %shard_map.94.adapter_ref), channel_id=1, source_target_pairs={{0,2},{2,0},{4,6},{6,4},{8,10},{10,8},{12,14},{14,12},{1,3},{3,1},... | collective-permute-start | bytes 3145736 | tf_op jit(solution)/shard_map/ppermute | solution.py:218
  65.3 8.6 %collective-permute-start.34 = (bf16[32,1024]{1,0:T(8,128)(2,1)S(1)}, bf16[32,1024]{1,0:T(8,128)(2,1)S(1)}, u32[]{:S(2)}, u32[]{:S(2)}) collective-permute-start(bf16[32,1024]{1,0:T(8,128)(2,1)S(1)} %get-tuple-element.74), channel_id=1, source_target_pairs={{0,4},{2,6},{4,8},{6,10},{8,12},{10,14},{12,0},{14,2},{1,5},{3,7},... | collective-permute-start | bytes 196616 | tf_op jit(solution)/shard_map/ppermute | solution.py:221
  68.1 5.8 %collective-permute-start.35 = (bf16[32,1024]{1,0:T(8,128)(2,1)S(1)}, bf16[32,1024]{1,0:T(8,128)(2,1)S(1)}, u32[]{:S(2)}, u32[]{:S(2)}) collective-permute-start(bf16[32,1024]{1,0:T(8,128)(2,1)S(1)} %get-tuple-element.75), channel_id=1, source_target_pairs={{0,8},{2,10},{4,12},{6,14},{8,0},{10,2},{12,4},{14,6},{1,9},{3,11}... | collective-permute-start | bytes 196616 | tf_op jit(solution)/shard_map/ppermute | solution.py:221
  70.5 4.3 %collective-permute-start.36 = (bf16[32,1024]{1,0:T(8,128)(2,1)S(1)}, bf16[32,1024]{1,0:T(8,128)(2,1)S(1)}, u32[]{:S(2)}, u32[]{:S(2)}) collective-permute-start(bf16[32,1024]{1,0:T(8,128)(2,1)S(1)} %get-tuple-element.76), channel_id=1, source_target_pairs={{0,12},{2,14},{4,0},{6,2},{8,4},{10,6},{12,8},{14,10},{1,13},{3,15... | collective-permute-start | bytes 196616 | tf_op jit(solution)/shard_map/ppermute | solution.py:221
  70.5 5.2 %collective-permute-start.28 = (f32[32,256]{1,0:T(8,128)S(1)}, f32[32,256]{1,0:T(8,128)S(1)}, u32[]{:S(2)}, u32[]{:S(2)}) collective-permute-start(f32[32,256]{1,0:T(8,128)S(1)} %shard_map.104), channel_id=1, source_target_pairs={{0,1},{1,0},{2,3},{3,2},{4,5},{5,4},{6,7},{7,6},{8,9},{9,8},{10,11... | collective-permute-start | bytes 98312 | tf_op jit(solution)/shard_map/ppermute | solution.py:227
  76.5 9.8 %collective-permute-start.29 = (bf16[32,128]{1,0:T(8,128)(2,1)S(1)}, bf16[32,128]{1,0:T(8,128)(2,1)S(1)}, u32[]{:S(2)}, u32[]{:S(2)}) collective-permute-start(bf16[32,128]{1,0:T(8,128)(2,1)S(1)} %slice.31), channel_id=1, source_target_pairs={{0,2},{2,0},{4,6},{6,4},{8,10},{10,8},{12,14},{14,12},{1,3},{3,1},... | collective-permute-start | bytes 24584 | tf_op jit(solution)/shard_map/ppermute | solution.py:218
  77.4 8.9 %collective-permute-start.31 = (bf16[32,4096]{1,0:T(8,128)(2,1)S(1)}, bf16[32,4096]{1,0:T(8,128)(2,1)S(1)}, u32[]{:S(2)}, u32[]{:S(2)}) collective-permute-start(bf16[32,4096]{1,0:T(8,128)(2,1)S(1)} %get-tuple-element.71), channel_id=1, source_target_pairs={{0,4},{2,6},{4,8},{6,10},{8,12},{10,14},{12,0},{14,2},{1,5},{3,7},... | collective-permute-start | bytes 786440 | tf_op jit(solution)/shard_map/ppermute | solution.py:221
  77.7 20.0 %collective-permute-start.32 = (bf16[32,4096]{1,0:T(8,128)(2,1)S(1)}, bf16[32,4096]{1,0:T(8,128)(2,1)S(1)}, u32[]{:S(2)}, u32[]{:S(2)}) collective-permute-start(bf16[32,4096]{1,0:T(8,128)(2,1)S(1)} %get-tuple-element.72), channel_id=1, source_target_pairs={{0,8},{2,10},{4,12},{6,14},{8,0},{10,2},{12,4},{14,6},{1,9},{3,11}... | collective-permute-start | bytes 786440 | tf_op jit(solution)/shard_map/ppermute | solution.py:221
  80.1 23.6 %collective-permute-start.33 = (bf16[32,4096]{1,0:T(8,128)(2,1)S(1)}, bf16[32,4096]{1,0:T(8,128)(2,1)S(1)}, u32[]{:S(2)}, u32[]{:S(2)}) collective-permute-start(bf16[32,4096]{1,0:T(8,128)(2,1)S(1)} %get-tuple-element.73), channel_id=1, source_target_pairs={{0,12},{2,14},{4,0},{6,2},{8,4},{10,6},{12,8},{14,10},{1,13},{3,15... | collective-permute-start | bytes 786440 | tf_op jit(solution)/shard_map/ppermute | solution.py:221

commit v3 on v2

--- a/solution.py
+++ b/solution.py
@@ -1,3 +1,5 @@
+import functools
+
 import jax
 import jax.numpy as jnp
 from jax import lax
@@ -6,6 +8,7 @@
 from jax.sharding import PartitionSpec as P
 
 adapter_scale_factor = 2.0
+CFG = {'zero': True, 'cuts': ((0, 4), (4, 4)), 'xcuts': ((0, 4), (4, 4)), 'db': 'dd', 'da': 'split', 'fetch': 'half', 'ya': 'y3', 'yb': 'y3', 'zorder': (3, 2, 1), 'sorder': (1, 2, 3), 'a_ids_first': True, 'a_y2': False, 'a_y3y1': True, 'a_y3x': False, 'a_slice': False, 'a_up': 'z', 'a_upy': True, 'a_idsdown': True, 'a_g': False, 'a_xup': True, 'a_xg': 1, 'a_g0up': 1, 'a_prev': False, 'a_prev2': False, 'a_pu': True, 'a_last': 1, 'a_back': 'late', 'a_su': True, 'late_b': 0, 'a_there': None, 'a_chain': 0, 'a_backgot': 0, 'a_bz': False, 's2': (0, 2, 2, 2), 'fin': 'three'}
 
 
 def contract_last(left, right):
@@ -95,6 +98,8 @@
 
 
 def cost(flops, moved):
+    if CFG['zero']:
+        flops = moved = 0
     return pl.CostEstimate(flops=flops, bytes_accessed=moved, transcendentals=0)
 
 
@@ -112,7 +117,7 @@
         out_ref[middle : low + rank, :] = jnp.where(first, other, got)
 
 
-def join(layer, own, got, other):
+def join(layer, own, got, other, at=0):
     rank, width = own.shape
     rows = (len(got) + 1) * rank
     return pl.pallas_call(
@@ -120,11 +125,31 @@
         grid=(1,),
         out_shape=jax.ShapeDtypeStruct((rows, width), own.dtype),
         in_specs=[pl.BlockSpec(memory_space=pltpu.SMEM), whole(rank, width)]
-        + [whole(rank // 2, width)] * (2 * len(got)),
+        + [pl.BlockSpec((rank // 2, width), lambda _: (at, 0))] * (2 * len(got)),
         out_specs=whole(rows, width),
         compiler_params=pltpu.CompilerParams(vmem_limit_bytes=VMEM_LIMIT),
         cost_estimate=cost(0, 4 * rows * width),
     )(layer, own, *got, *other)
+
+
+def stack_kernel(*refs):
+    *parts, out_ref = refs
+    rank = parts[0].shape[0]
+    for at, part in enumerate(parts):
+        out_ref[at * rank : (at + 1) * rank, :] = part[...]
+
+
+def stack_rows(parts):
+    rank, width = parts[0].shape
+    return pl.pallas_call(
+        stack_kernel,
+        grid=(1,),
+        out_shape=jax.ShapeDtypeStruct((rank * len(parts), width), parts[0].dtype),
+        in_specs=[whole(rank, width)] * len(parts),
+        out_specs=whole(rank * len(parts), width),
+        compiler_params=pltpu.CompilerParams(vmem_limit_bytes=VMEM_LIMIT),
+        cost_estimate=cost(0, 4 * rank * len(parts) * width),
+    )(*parts)
 
 
 def project_kernel(adapter_ref, own_ref, other_ref, held_ref, base_ref, out_ref):
@@ -163,7 +188,7 @@
     )(adapters, own_rows, other_rows, held, base)
 
 
-def partial_kernel(scaled_ref, held_ref, own_ref, other_ref, sum_ref, *send_refs):
+def partial_kernel(keep, away, scaled_ref, held_ref, own_ref, other_ref, keep_ref, *away_refs):
     columns, tokens = held_ref.shape
     rows = tokens // 2
     rank = scaled_ref.shape[0]
@@ -176,29 +201,142 @@
     )
     total = jnp.dot(left[:, :rows], own_ref[...], preferred_element_type=jnp.float32)
     total = total + jnp.dot(left[:, rows:], other_ref[...], preferred_element_type=jnp.float32)
-    sum_ref[...] = total[:rank]
-    for step, send_ref in enumerate(send_refs):
-        send_ref[...] = total[(step + 1) * rank : (step + 2) * rank].astype(jnp.bfloat16)
-
-
-def partials(scaled, held, own_rows, other_rows, at):
+    for group, out_ref in zip((keep,) + away, (keep_ref,) + away_refs):
+        for at, block in enumerate(group):
+            out_ref[at * rank : (at + 1) * rank, :] = total[
+                block * rank : (block + 1) * rank
+            ].astype(out_ref.dtype)
+
+
+def partials(scaled, held, own_rows, other_rows, at, keep, away, kind=jnp.float32, wide=None):
     columns, tokens = held.shape
-    rows, wide = other_rows.shape
+    rows = other_rows.shape[0]
+    there_at = at if wide else 0
+    wide = wide or other_rows.shape[1]
     rank = scaled.shape[0]
+    shapes = [(len(group) * rank, wide) for group in (keep,) + away]
     return pl.pallas_call(
-        partial_kernel,
+        functools.partial(partial_kernel, keep, away),
         grid=(1,),
-        out_shape=[jax.ShapeDtypeStruct((rank, wide), jnp.float32)]
-        + [jax.ShapeDtypeStruct((rank, wide), jnp.bfloat16)] * (columns - 1),
+        out_shape=[jax.ShapeDtypeStruct(shapes[0], kind)]
+        + [jax.ShapeDtypeStruct(shape, jnp.bfloat16) for shape in shapes[1:]],
         in_specs=[
             whole(*scaled.shape),
             whole(*held.shape),
             column_cut(rows, wide, at),
-            whole(rows, wide),
+            column_cut(rows, wide, there_at),
         ],
-        out_specs=[whole(rank, wide)] * columns,
+        out_specs=[whole(*shape) for shape in shapes],
         compiler_params=pltpu.CompilerParams(vmem_limit_bytes=VMEM_LIMIT),
         cost_estimate=cost(2 * columns * rank * tokens * wide, 8 * rows * wide),
+    )(scaled, held, own_rows, other_rows)
+
+
+def sums_into(out_ref, rank, cuts, refs):
+    refs = list(refs)
+    for start, wide, count in cuts:
+        first = refs.pop(0)
+        total = first[:rank, :].astype(jnp.float32)
+        if count == 1:
+            for at in range(1, first.shape[0] // rank):
+                total = total + first[at * rank : (at + 1) * rank, :].astype(jnp.float32)
+        for _ in range(count - 1):
+            total = total + refs.pop(0)[:rank, :].astype(jnp.float32)
+        out_ref[0, :, start : start + wide] = total
+
+
+def dx_into(dx_ref, low_ref, low_there_ref, held_ref, held_there_ref, down_ref, there_ref):
+    left = jnp.concatenate(
+        [
+            jnp.where(mask_ref[step : step + 1, :] > 0, low[...], 0.0).astype(jnp.bfloat16)
+            for low, mask_ref in ((low_ref, held_ref), (low_there_ref, held_there_ref))
+            for step in range(held_ref.shape[0])
+        ]
+    )
+    half = down_ref.shape[0]
+    dx = contract_first(left[:half], down_ref[...]) + contract_first(left[half:], there_ref[...])
+    dx_ref[...] = dx.astype(dx_ref.dtype)
+
+
+def finish_kernel(rank, dx, groups, *refs):
+    refs = list(refs)
+    ins = [refs[: (6 if dx else 0)]]
+    del refs[: (6 if dx else 0)]
+    for cuts in groups:
+        count = sum(cut[2] for cut in cuts)
+        ins.append(refs[:count])
+        del refs[:count]
+    if dx:
+        dx_into(refs.pop(0), *ins[0])
+    for cuts, group, out_ref in zip(groups, ins[1:], refs):
+        sums_into(out_ref, rank, cuts, group)
+
+
+def finish(rank, width, dx_operands, groups):
+    operands, cuts, shapes = list(dx_operands), [], []
+    if dx_operands:
+        shapes.append(jax.ShapeDtypeStruct((dx_operands[0].shape[1], width), jnp.bfloat16))
+    for group in groups:
+        cuts.append([(start, wide, len(parts)) for start, wide, parts in group])
+        for _, _, parts in group:
+            operands.extend(parts)
+        shapes.append(jax.ShapeDtypeStruct((1, rank, width), jnp.float32))
+    return pl.pallas_call(
+        functools.partial(finish_kernel, rank, bool(dx_operands), cuts),
+        grid=(1,),
+        out_shape=shapes,
+        in_specs=[whole(*operand.shape) for operand in operands],
+        out_specs=[whole(*shape.shape) for shape in shapes],
+        compiler_params=pltpu.CompilerParams(vmem_limit_bytes=VMEM_LIMIT),
+        cost_estimate=cost(4 * 128 * 128 * width, 32 * rank * width),
+    )(*operands)
+
+
+def split_kernel(cuts, scaled_ref, held_ref, own_ref, other_ref, *out_refs):
+    columns, tokens = held_ref.shape
+    rows = tokens // 2
+    rank = scaled_ref.shape[0]
+    scaled = scaled_ref[...]
+    left = jnp.concatenate(
+        [
+            jnp.where(held_ref[step : step + 1, :] > 0, scaled, 0.0).astype(jnp.bfloat16)
+            for step in range(columns)
+        ]
+    )
+    for i, (start, wide) in enumerate(cuts):
+        cut = slice(start, start + wide)
+        total = jnp.dot(left[:, :rows], own_ref[:, cut], preferred_element_type=jnp.float32)
+        total = total + jnp.dot(
+            left[:, rows:], other_ref[:, cut], preferred_element_type=jnp.float32
+        )
+        for out_ref, blocks in zip(out_refs[2 * i : 2 * i + 2], ((0, 2), (1, 3))):
+            for at, block in enumerate(blocks):
+                out_ref[at * rank : (at + 1) * rank, :] = total[
+                    block * rank : (block + 1) * rank
+                ].astype(out_ref.dtype)
+
+
+def split_partials(scaled, held, own_rows, other_rows, cuts):
+    columns, tokens = held.shape
+    rows, width = other_rows.shape
+    rank = scaled.shape[0]
+    shapes = []
+    for _, wide in cuts:
+        shapes.append(jax.ShapeDtypeStruct((2 * rank, wide), jnp.float32))
+        shapes.append(jax.ShapeDtypeStruct((2 * rank, wide), jnp.bfloat16))
+    return pl.pallas_call(
+        functools.partial(split_kernel, cuts),
+        grid=(1,),
+        out_shape=shapes,
+        in_specs=[
+            whole(*scaled.shape),
+            whole(*held.shape),
+            whole(rows, width),
+            whole(rows, width),
+        ],
+        out_specs=[whole(*shape.shape) for shape in shapes],
+        compiler_params=pltpu.CompilerParams(vmem_limit_bytes=VMEM_LIMIT),
+        cost_estimate=cost(2 * columns * rank * tokens * width, 8 * rows * width),
     )(scaled, held, own_rows, other_rows)
 
 
@@ -217,8 +355,8 @@
     def swap_side(value):
         return lax.ppermute(value, "dp", [(i, i ^ 1) for i in range(ranks)])
 
-    def shift(value, by):
-        return lax.ppermute(value, "dp", [(i, (i + 2 * by) % ranks) for i in range(ranks)])
+    def hop(value, by):
+        return lax.ppermute(value, "dp", [(i, i ^ (2 * by)) for i in range(ranks)])
 
     def swap_layer(value):
         return lax.ppermute(value, "parts", [(0, 1), (1, 0)])
@@ -230,83 +368,226 @@
         return lax.dynamic_slice(own, (layer * half, 0), (half, width))
 
     def fetch(own):
-        return [shift(half_rows(own), -step) for step in range(1, columns)]
-
-    def send(blocks):
-        return [shift(block, step) for step, block in enumerate(blocks, 1)]
-
-    def add(total, got):
+        order = CFG["zorder"]
+        got = {step: hop(own, step) for step in order}
+        return [got[step] for step in range(1, columns)]
+
+    def add(total, *got):
         for block in got:
             total = total + block.astype(jnp.float32)
         return total
 
-    pieces = 4
-    wide = width // pieces
+    cuts = CFG["cuts"]
+    eighth = width // 8
     layer_of = layer.astype(jnp.int32)[None]
     other_x = swap_side(features)
-    down_got = fetch(adapter_down[0])
-    down_other = [swap_layer(got) for got in down_got]
-    up_own, cotangent, tenant_ids, document_index_per_token = lax.optimization_barrier(
-        (adapter_up[0], cotangent, tenant_ids, document_index_per_token) + tuple(down_got)
-    )[:4]
-    other_g = [swap_side(cotangent[:, i * wide : (i + 1) * wide]) for i in range(pieces)]
-    up_got = fetch(up_own)
-    down = join(layer_of, adapter_down[0], down_got, down_other)
-
-    owner = token_owner(tenant_ids, owner_map)
+    ids_there = swap_side(jnp.stack([tenant_ids, document_index_per_token]))
+    down_own, up_own = adapter_down[0], adapter_up[0]
+    if CFG["a_ids_first"]:
+        down_own = after(down_own, ids_there)
+
+    def exchange(got, mode, tie2=(), tie3=()):
+        if mode == "y1":
+            other = swap_layer(jnp.stack([after(got[0], *tie2)] + got[1:]))
+            return got, list(other)
+        if CFG["a_y2"]:
+            got[1] = after(got[1], *tie2)
+        other = [swap_layer(block) for block in got[:2]]
+        deps = tuple(tie3)
+        if CFG["a_y3y1"]:
+            deps += (other[0],)
+        if deps:
+            got[2] = after(got[2], *deps)
+        other.append(swap_layer(got[2]))
+        return got, other
+
+    own_g = [cotangent[:, i * eighth : (i + n) * eighth] for i, n in cuts]
+    tie3 = (other_x,) if CFG["a_y3x"] else ()
+    if CFG["fetch"] == "both":
+        src = jnp.concatenate([half_rows(down_own), half_rows(up_own)])
+        got = fetch(src)
+        if CFG["a_slice"]:
+            got[1], *own_g = lax.optimization_barrier((got[1], *own_g))
+        got, other = exchange(got, CFG["ya"], (), tie3)
+        down = join(layer_of, down_own, got, other, 0)
+        up = join(layer_of, up_own, got, other, 1)
+        up_got = got
+    else:
+        if CFG["fetch"] == "full":
+            down_got = fetch(down_own)
+            down = stack_rows([down_own] + down_got)
+        else:
+            down_got = fetch(half_rows(down_own))
+            if CFG["a_slice"]:
+                down_got[1], *own_g = lax.optimization_barrier((down_got[1], *own_g))
+            if CFG["a_bz"]:
+                up_got = fetch(half_rows(after(up_own, down_got[0]) if CFG["a_up"] else up_own))
+                tie3 += tuple(up_got)
+            down_got, down_other = exchange(down_got, CFG["ya"], (), tie3)
+            down = join(layer_of, down_own, down_got, down_other)
+        if CFG["a_up"] == "z":
+            up_own = after(up_own, down_got[0])
+        elif CFG["a_up"] == "y":
+            up_own = after(up_own, down)
+        if CFG["fetch"] == "full" or not CFG["a_bz"]:
+            up_got = fetch(half_rows(up_own))
+        up_gots = list(up_got)
+        if CFG["a_upy"]:
+            up_gots[0] = after(up_gots[0], down)
+        up_gots, up_other = exchange(up_gots, CFG["yb"])
+        up = join(layer_of, up_own, up_gots, up_other)
+    if CFG["a_idsdown"]:
+        ids_there = after(ids_there, down)
+    if CFG["a_g"]:
+        own_g[0] = after(own_g[0], down_got[0] if CFG["fetch"] != "both" else up_got[0])
+    line = [other_x]
+    for i, cut in enumerate(own_g):
+        back_by = CFG["a_chain"]
+        if back_by and i + 1 >= back_by:
+            cut = after(cut, line[i + 1 - back_by])
+        line.append(swap_side(cut))
+    other_g = line[1:]
+
+    owner, owner_there = token_owner(tenant_ids, owner_map), token_owner(ids_there[0], owner_map)
     weight = token_weight(document_index_per_token)
-    facts = jnp.stack([owner.astype(jnp.float32), weight])
-    facts = jnp.concatenate([facts, swap_side(after(facts, down))], axis=1)
-    owner_here = facts[0].astype(jnp.int32)
-    weight_here = facts[1]
+    owner_here = jnp.concatenate([owner, owner_there])
+    weight_here = jnp.concatenate([weight, token_weight(ids_there[1])])
     steps = jnp.arange(columns, dtype=jnp.int32)
-    block_owner = ((place + steps) % columns) * 2 + side
+    block_owner = (place ^ steps) * 2 + side
     block_owner_there = block_owner + 1 - 2 * side
     held = (block_owner[:, None] == owner_here[None, :]).astype(jnp.float32)
-    own_held = (block_owner[:, None] == owner[None, :])[:, None, :]
-    own_there = (block_owner_there[:, None] == owner[None, :])[:, None, :]
-
-    def spread(low, mask):
-        return jnp.where(mask, low[None], jnp.zeros((), low.dtype)).reshape(
-            columns * rank, low.shape[1]
-        )
+    plain = steps * 2 + side
+    held_plain = (plain[:, None] == owner_here[None, :]).astype(jnp.float32)
+    own_held = (block_owner[:, None] == owner[None, :]).astype(jnp.float32)
+    own_there = (block_owner_there[:, None] == owner[None, :]).astype(jnp.float32)
 
     def combine(low):
         return ((low + swap_core(low)) * weight_here[None, :]).astype(jnp.bfloat16)
 
     nothing = jnp.zeros((rank, 2 * rows), jnp.float32)
-    low_h = project(down, features, other_x, held, nothing, 0)
-    up_got = [after(got, low_h) for got in up_got]
-    up = join(layer_of, up_own, up_got, [swap_layer(got) for got in up_got])
-    scaled_h = combine(low_h)
+    x_in = after(other_x, *up_got) if CFG["a_xup"] else other_x
+    if CFG["a_xg"]:
+        x_in = after(x_in, *other_g[: CFG["a_xg"]])
+    scaled_h = combine(project(down, features, x_in, held, nothing, 0))
+    if CFG["a_g0up"] is not None:
+        at = min(CFG["a_g0up"], len(cuts) - 1)
+        other_g[at] = after(other_g[at], up)
+
+    def scatter(scaled, own_rows, there, start, count, mode, full=False):
+        at = start // count
+        wide = count * eighth if full else None
+        if mode == "a2a":
+            (away,) = partials(scaled, held_plain, own_rows, there, at, (0, 1, 2, 3), (), jnp.bfloat16, wide)
+            wide = away.shape[1]
+            got = lax.all_to_all(
+                away.reshape(columns, rank, wide), "dp", split_axis=0, concat_axis=0, tiled=True,
+                axis_index_groups=[list(range(s, ranks, 2)) for s in range(2)],
+            )
+            return away, [got.reshape(columns * rank, wide)]
+        if mode == "dd":
+            total, away = partials(scaled, held, own_rows, there, at, (0, 2), ((1, 3),), wide=wide)
+            return total, [total, hop(away, 1)]
+        total, *blocks = partials(scaled, held, own_rows, there, at, (0,), ((1,), (2,), (3,)), wide=wide)
+        order = CFG["sorder"]
+        got = {step: hop(blocks[step - 1], step) for step in order}
+        return total, [total] + [got[step] for step in order]
+
+    def forward(parts, *deps):
+        total, first = parts
+        here = after(first, *deps) if deps else first
+        src = add(total[rank:], here[rank:]).astype(jnp.bfloat16)
+        srcs.append(src)
+        return [total, first, hop(src, 2)]
+
+    srcs = []
     low_u = nothing
-    totals, gots = [], []
-    for i in range(pieces):
-        if i > 1:
-            other_g[i] = after(other_g[i], *gots[i - 2])
-        total, *blocks = partials(scaled_h, held, cotangent, other_g[i], i)
-        other_g[i] = after(other_g[i], total)
-        totals.append(total)
-        gots.append(send(blocks))
-        low_u = project(up, cotangent, other_g[i], held, low_u, i)
-    low_u = after(low_u, *gots[pieces - 2])
+    up_group = []
+    waits = CFG["s2"]
+    for i, (start, count) in enumerate(cuts):
+        there = other_g[i]
+        if i >= 1 and CFG["a_prev"]:
+            there = after(there, up_group[i - 1][2][-1])
+        if i >= 2 and CFG["a_prev2"] and (CFG["db"] != "dd" or waits[i - 2] == 0):
+            there = after(there, *up_group[i - 2][2])
+        if CFG["late_b"] and i == len(cuts) - 1:
+            up_group.append((start * eighth, count * eighth, None))
+        else:
+            total, parts = scatter(scaled_h, cotangent, there, start, count, CFG["db"])
+            if CFG["db"] == "dd" and waits[i] == 0:
+                parts = forward(parts)
+            up_group.append((start * eighth, count * eighth, parts))
+            if CFG["a_pu"]:
+                there = after(there, total)
+        low_u = project(up, cotangent, there, held, low_u, start // count)
+    if CFG["a_last"]:
+        low_u = after(low_u, *up_group[CFG["a_last"] - 1][2])
+    if CFG["db"] == "dd":
+        for i in range(len(cuts)):
+            if waits[i] == 1 and up_group[i][2]:
+                up_group[i] = up_group[i][:2] + (forward(up_group[i][2], low_u),)
     scaled_u = combine(low_u)
-    total, *blocks = partials(scaled_u, held, features, other_x, 0)
-    got = send(blocks)
-    back = swap_side(after(scaled_u, total)[:, rows:])
-    down_there = swap_side(after(down, other_g[1]))
-    up_adapter_gradient = jnp.concatenate([add(*pair) for pair in zip(totals, gots)], axis=1)
-    left = jnp.concatenate([spread(scaled_u[:, :rows], own_held), spread(back, own_there)])
-    input_grad = contract_first(left, jnp.concatenate([down, down_there])).astype(jnp.bfloat16)
-    grad_down = add(total, got)
-    return (input_grad, grad_down[None], up_adapter_gradient[None])
+    if CFG["a_su"]:
+        scaled_u = after(scaled_u, *srcs)
+    down_group = []
+    last = None
+    if CFG["da"] == "split":
+        outs = split_partials(
+            scaled_u, held, features, other_x,
+            tuple((start * eighth, count * eighth) for start, count in CFG["xcuts"]),
+        )
+        total = outs[0]
+        for i, (start, count) in enumerate(CFG["xcuts"]):
+            parts = [outs[2 * i], hop(outs[2 * i + 1], 1)]
+            down_group.append((start * eighth, count * eighth, parts))
+    for start, count in CFG["xcuts"] if CFG["da"] != "split" else ():
+        total, parts = scatter(scaled_u, features, other_x, start, count, CFG["da"], True)
+        down_group.append((start * eighth, count * eighth, parts))
+    if CFG["late_b"]:
+        start, count = cuts[-1]
+        _, parts = scatter(scaled_h, cotangent, after(other_g[-1], total), start, count, CFG["db"])
+        if CFG["late_b"] == 2:
+            parts = forward(parts)
+            waits = waits[: len(cuts) - 1] + (0,)
+        up_group[-1] = up_group[-1][:2] + (parts,)
+    if CFG["da"] in ("dd", "split"):
+        down_group = [group[:2] + (forward(group[2]),) for group in down_group]
+    if CFG["db"] == "dd":
+        for i in range(len(cuts)):
+            if waits[i] == 2:
+                up_group[i] = up_group[i][:2] + (forward(up_group[i][2], total),)
+            if waits[i] == 3:
+                up_group[i] = up_group[i][:2] + (forward(up_group[i][2], down_group[0][2][-1]),)
+    back_src = scaled_u
+    if CFG["a_back"] == "late":
+        back_src = after(scaled_u, srcs[-1])
+    elif CFG["a_back"]:
+        back_src = after(scaled_u, total)
+    back = swap_side(back_src[:, rows:])
+    down_there = swap_side(after(down, line[CFG["a_there"]]) if CFG["a_there"] is not None else down)
+    if CFG["a_backgot"] == "all":
+        back = after(back, *[part for group in down_group for part in group[2]])
+    elif CFG["a_backgot"] is not None:
+        back = after(back, down_group[0][2][-1])
+    dx_ops = (scaled_u[:, :rows], back, own_held, own_there, down, down_there)
+    if CFG["fin"] == "one":
+        return finish(rank, width, dx_ops, [down_group, up_group])
+    if CFG["fin"] == "two":
+        (up_grad,) = finish(rank, width, (), [up_group])
+        return finish(rank, width, dx_ops, [down_group]) + [up_grad]
+    (up_grad,) = finish(rank, width, (), [up_group])
+    (dx,) = finish(rank, width, dx_ops, [])
+    s0, c0, p0 = down_group[-1]
+    down_group[-1] = (s0, c0, p0[:-1] + [after(p0[-1], dx)])
+    (down_grad,) = finish(rank, width, (), [down_group])
+    return dx, down_grad, up_grad
 
 
 def shards(features, *others):
     ranks = lax.axis_size("dp")
     rank = others[-1].shape[1]
     slots = 2 * features.shape[0] // ranks
-    if slots >= rank and ranks % 2 == 0 and rank % 32 == 0 and lax.axis_size("parts") == 2:
+    fits = rank % 32 == 0 and features.shape[1] % 1024 == 0
+    if slots >= rank and fits and ranks == 8 and lax.axis_size("parts") == 2:
         return route_adapters(features, *others)
     return route_tokens(features, *others)
 

time: 106 us -> 94.6 us (0.89)
  the two profiles are of different devices: /device:TPU:13 before, /device:TPU:0 now
where the time goes in v3:
time: 94.6 us; the launch traced here: 94.4 us
  waiting for transfers between devices  45.6 us (48%)
  starting transfers between devices  36.1 us (38%)
  Pallas kernels  6.71 us (7%)
  local copies, waits for them, and re-layouts  4.39 us (5%)
    ppermute x14, waiting for transfers between devices, hop(): return lax.ppermute(value, 'dp', [(i, i ^ 2 * by) for i in range(ranks)])  28.7 us
    ppermute x14, starting transfers between devices, hop(): return lax.ppermute(value, 'dp', [(i, i ^ 2 * by) for i in range(ranks)])  22.6 us
    ppermute x6, waiting for transfers between devices, swap_layer(): return lax.ppermute(value, 'parts', [(0, 1), (1, 0)])  9.62 us
    ppermute x6, starting transfers between devices, swap_layer(): return lax.ppermute(value, 'parts', [(0, 1), (1, 0)])  7.12 us
    ppermute x6, starting transfers between devices, swap_side(): return lax.ppermute(value, 'dp', [(i, i ^ 1) for i in range(ranks)])  6.28 us
    ppermute x6, waiting for transfers between devices, swap_side(): return lax.ppermute(value, 'dp', [(i, i ^ 1) for i in range(ranks)])  5.55 us
    pallas_call x3, Pallas kernels, finish(): pl.pallas_call(functools.partial(finish_kernel, rank, bool(dx_operands),...  3.47 us
    slice x1, local copies, waits for them, and re-layouts, route_adapters(): own_g = [cotangent[:, i * eighth:(i + n) * eighth] for i, n in cuts]  2.08 us
  transfers between devices with their start and end apart: 28, of which 16 were waited for; matrix products, arithmetic and copies ran while one was open for 4% of the time, Pallas kernels for 5%

profile of v3, /device:TPU:0, one launch (start us, length us, event | category | flops | bytes accessed | tf_op | source)
XLA Modules:
  0.0 94.4 jit_solution(9180462018193002604)
XLA Ops:
  0.7 0.6 copy-done.4
  1.3 0.0 copy-done.6
  1.3 3.0 %collective-permute-start = (s32[2,128]{1,0:T(2,128)S(1)}, s32[2,128]{1,0:T(2,128)S(1)}, u32[]{:S(2)}, u32[]{:S(2)}) collective-permute-start(s32[2,128]{1,0:T(2,128)S(1)} %pad_add_fusion), channel_id=1, source_target_pairs={{0,2},{2,0},{4,6},{6,4},{8,10},{10,8},{12,14},{14,12},{1,3},{3,1},... | collective-permute-start | bytes 3080 | tf_op jit(solution)/shard_map/ppermute | solution.py:356
  4.3 0.1 collective-permute-start.14
  4.4 1.5 %collective-permute-done = s32[2,128]{1,0:T(2,128)S(1)} collective-permute-done((s32[2,128]{1,0:T(2,128)S(1)}, s32[2,128]{1,0:T(2,128)S(1)}, u32[]{:S(2)}, u32[]{:S(2)}) %collective-permute-start) | collective-permute-done | bytes 1056 | tf_op jit(solution)/shard_map/ppermute | solution.py:356
  5.9 0.9 constant_dynamic-slice_fusion.1
  6.8 2.2 %collective-permute-start.1 = (bf16[16,4096]{1,0:T(8,128)(2,1)S(1)}, bf16[16,4096]{1,0:T(8,128)(2,1)S(1)}, u32[]{:S(2)}, u32[]{:S(2)}) collective-permute-start(bf16[16,4096]{1,0:T(8,128)(2,1)S(1)} %constant_dynamic-slice_fusion.1), channel_id=1, source_target_pairs={{0,4},{2,6},{4,0},{6,2},{8,12},{10,14},{12,8},{14,10},{1,5},{3,7},... | collective-permute-start | bytes 393224 | tf_op jit(solution)/shard_map/ppermute | solution.py:359
  9.0 2.1 %fusion = (bf16[128,2048]{1,0:T(8,128)(2,1)}, bf16[128,2048]{1,0:T(8,128)(2,1)S(1)}) fusion(bf16[128,4096]{1,0:T(8,128)(2,1)} %own_ref.10), kind=kLoop, calls=%fused_computation.26 | loop fusion | bytes 2097152 | tf_op jit(solution)/shard_map/slice | solution.py:404
  11.0 1.5 %collective-permute-start.15 = (bf16[128,2048]{1,0:T(8,128)(2,1)}, bf16[128,2048]{1,0:T(8,128)(2,1)S(1)}, u32[]{:S(2)}, u32[]{:S(2)}) collective-permute-start(bf16[128,2048]{1,0:T(8,128)(2,1)} %get-tuple-element.57), channel_id=1, source_target_pairs={{0,2},{2,0},{4,6},{6,4},{8,10},{10,8},{12,14},{14,12},{1,3},{3,1},... | collective-permute-start | bytes 1572872 | tf_op jit(solution)/shard_map/ppermute | solution.py:356
  12.5 0.2 convert_reduce_fusion.1
  12.7 2.5 %collective-permute-start.4 = (bf16[16,4096]{1,0:T(8,128)(2,1)S(1)}, bf16[16,4096]{1,0:T(8,128)(2,1)S(1)}, u32[]{:S(2)}, u32[]{:S(2)}) collective-permute-start(bf16[16,4096]{1,0:T(8,128)(2,1)S(1)} %constant_dynamic-slice_fusion.1), channel_id=1, source_target_pairs={{0,12},{2,14},{4,8},{6,10},{8,4},{10,6},{12,0},{14,2},{1,13},{3,15... | collective-permute-start | bytes 393224 | tf_op jit(solution)/shard_map/ppermute | solution.py:359
  15.2 0.2 collective-permute-start.3
  15.4 1.5 %collective-permute-start.5 = (bf16[16,4096]{1,0:T(8,128)(2,1)S(1)}, bf16[16,4096]{1,0:T(8,128)(2,1)S(1)}, u32[]{:S(2)}, u32[]{:S(2)}) collective-permute-start(bf16[16,4096]{1,0:T(8,128)(2,1)S(1)} %collective-permute-done.1.refs_0_), channel_id=1, source_target_pairs={{0,16},{16,0},{1,17},{17,1},{2,18},{18,2},{3,19},{19,3},{4,20},{20... | collective-permute-start | bytes 393224 | tf_op jit(solution)/shard_map/ppermute | solution.py:362
  17.0 8.6 %collective-permute-done.3.refs_1_ = bf16[16,4096]{1,0:T(8,128)(2,1)S(1)} collective-permute-done((bf16[16,4096]{1,0:T(8,128)(2,1)S(1)}, bf16[16,4096]{1,0:T(8,128)(2,1)S(1)}, u32[]{:S(2)}, u32[]{:S(2)}) %collective-permute-start.3) | collective-permute-done | bytes 131104 | tf_op jit(solution)/shard_map/ppermute | solution.py:359
  25.6 1.5 %collective-permute-start.6 = (bf16[16,4096]{1,0:T(8,128)(2,1)S(1)}, bf16[16,4096]{1,0:T(8,128)(2,1)S(1)}, u32[]{:S(2)}, u32[]{:S(2)}) collective-permute-start(bf16[16,4096]{1,0:T(8,128)(2,1)S(1)} %collective-permute-done.3.refs_1_), channel_id=1, source_target_pairs={{0,16},{16,0},{1,17},{17,1},{2,18},{18,2},{3,19},{19,3},{4,20},{20... | collective-permute-start | bytes 393224 | tf_op jit(solution)/shard_map/ppermute | solution.py:362
  27.1 0.5 collective-permute-start.7
  27.6 0.1 collective-permute-start.8
  27.7 3.7 %collective-permute-done.6.refs_4_ = bf16[16,4096]{1,0:T(8,128)(2,1)S(1)} collective-permute-done((bf16[16,4096]{1,0:T(8,128)(2,1)S(1)}, bf16[16,4096]{1,0:T(8,128)(2,1)S(1)}, u32[]{:S(2)}, u32[]{:S(2)}) %collective-permute-start.6) | collective-permute-done | bytes 131104 | tf_op jit(solution)/shard_map/ppermute | solution.py:362
  31.4 1.4 %collective-permute-done.7.refs_5_ = bf16[16,4096]{1,0:T(8,128)(2,1)S(1)} collective-permute-done((bf16[16,4096]{1,0:T(8,128)(2,1)S(1)}, bf16[16,4096]{1,0:T(8,128)(2,1)S(1)}, u32[]{:S(2)}, u32[]{:S(2)}) %collective-permute-start.7) | collective-permute-done | bytes 131104 | tf_op jit(solution)/shard_map/ppermute | solution.py:362
  32.8 2.8 %collective-permute-start.9 = (bf16[16,4096]{1,0:T(8,128)(2,1)S(1)}, bf16[16,4096]{1,0:T(8,128)(2,1)S(1)}, u32[]{:S(2)}, u32[]{:S(2)}) collective-permute-start(bf16[16,4096]{1,0:T(8,128)(2,1)S(1)} %constant_dynamic-slice_fusion), channel_id=1, source_target_pairs={{0,12},{2,14},{4,8},{6,10},{8,4},{10,6},{12,0},{14,2},{1,13},{3,15... | collective-permute-start | bytes 393224 | tf_op jit(solution)/shard_map/ppermute | solution.py:359
  35.6 0.1 shard_map.94.adapter_ref.refs_4_
  35.7 0.2 convert_reduce_fusion
  35.9 0.7 copy-done.5
  36.6 0.1 select_reduce_fusion.1
  36.7 0.1 compare_convert_fusion.held_ref
  36.7 0.9 collective-permute-done.8.refs_1_
  37.6 2.2 %collective-permute-done.2.refs_0_ = bf16[16,4096]{1,0:T(8,128)(2,1)S(1)} collective-permute-done((bf16[16,4096]{1,0:T(8,128)(2,1)S(1)}, bf16[16,4096]{1,0:T(8,128)(2,1)S(1)}, u32[]{:S(2)}, u32[]{:S(2)}) %collective-permute-start.2) | collective-permute-done | bytes 131104 | tf_op jit(solution)/shard_map/ppermute | solution.py:359
  39.8 0.6 collective-permute-done.15.other_ref
  40.4 0.7 shard_map.96
  41.1 0.1 collective-permute-start.16
  41.2 1.2 %collective-permute-done.16 = f32[32,256]{1,0:T(8,128)S(1)} collective-permute-done((f32[32,256]{1,0:T(8,128)S(1)}, f32[32,256]{1,0:T(8,128)S(1)}, u32[]{:S(2)}, u32[]{:S(2)}) %collective-permute-start.16) | collective-permute-done | bytes 32800 | tf_op jit(solution)/shard_map/ppermute | solution.py:365
  42.4 0.4 shard_map.98
  42.8 1.6 %collective-permute-start.17 = (bf16[64,2048]{1,0:T(8,128)(2,1)S(1)}, bf16[64,2048]{1,0:T(8,128)(2,1)S(1)}, u32[]{:S(2)}, u32[]{:S(2)}) collective-permute-start(bf16[64,2048]{1,0:T(8,128)(2,1)S(1)} %get-tuple-element.41), channel_id=1, source_target_pairs={{0,4},{2,6},{4,0},{6,2},{8,12},{10,14},{12,8},{14,10},{1,5},{3,7},... | collective-permute-start | bytes 786440 | tf_op jit(solution)/shard_map/ppermute | solution.py:359
  44.5 1.5 %collective-permute-start.10 = (bf16[16,4096]{1,0:T(8,128)(2,1)S(1)}, bf16[16,4096]{1,0:T(8,128)(2,1)S(1)}, u32[]{:S(2)}, u32[]{:S(2)}) collective-permute-start(bf16[16,4096]{1,0:T(8,128)(2,1)S(1)} %collective-permute-done.2.refs_0_), channel_id=1, source_target_pairs={{0,16},{16,0},{1,17},{17,1},{2,18},{18,2},{3,19},{19,3},{4,20},{20... | collective-permute-start | bytes 393224 | tf_op jit(solution)/shard_map/ppermute | solution.py:362
  46.0 0.5 collective-permute-start.13
  46.5 0.5 collective-permute-start.11
  47.0 3.8 %collective-permute-done.10.refs_3_ = bf16[16,4096]{1,0:T(8,128)(2,1)S(1)} collective-permute-done((bf16[16,4096]{1,0:T(8,128)(2,1)S(1)}, bf16[16,4096]{1,0:T(8,128)(2,1)S(1)}, u32[]{:S(2)}, u32[]{:S(2)}) %collective-permute-start.10) | collective-permute-done | bytes 131104 | tf_op jit(solution)/shard_map/ppermute | solution.py:362
  50.8 1.5 %collective-permute-start.12 = (bf16[16,4096]{1,0:T(8,128)(2,1)S(1)}, bf16[16,4096]{1,0:T(8,128)(2,1)S(1)}, u32[]{:S(2)}, u32[]{:S(2)}) collective-permute-start(bf16[16,4096]{1,0:T(8,128)(2,1)S(1)} %collective-permute-done.9.refs_2_), channel_id=1, source_target_pairs={{0,16},{16,0},{1,17},{17,1},{2,18},{18,2},{3,19},{19,3},{4,20},{20... | collective-permute-start | bytes 393224 | tf_op jit(solution)/shard_map/ppermute | solution.py:362
  52.4 2.7 %collective-permute-start.18 = (bf16[32,2048]{1,0:T(8,128)(2,1)S(1)}, bf16[32,2048]{1,0:T(8,128)(2,1)S(1)}, u32[]{:S(2)}, u32[]{:S(2)}) collective-permute-start(bf16[32,2048]{1,0:T(8,128)(2,1)S(1)} %add_convert_fusion.3), channel_id=1, source_target_pairs={{0,8},{2,10},{4,12},{6,14},{8,0},{10,2},{12,4},{14,6},{1,9},{3,11}... | collective-permute-start | bytes 393224 | tf_op jit(solution)/shard_map/ppermute | solution.py:359
  55.1 0.7 collective-permute-done.12.refs_5_
  55.8 0.1 shard_map.95.adapter_ref
  55.9 3.5 %collective-permute-done.13.other_ref = bf16[128,2048]{1,0:T(8,128)(2,1)S(1)} collective-permute-done((bf16[128,2048]{1,0:T(8,128)(2,1)S(1)}, bf16[128,2048]{1,0:T(8,128)(2,1)S(1)}, u32[]{:S(2)}, u32[]{:S(2)}) %collective-permute-start.13) | collective-permute-done | bytes 524320 | tf_op jit(solution)/shard_map/ppermute | solution.py:356
  59.4 0.4 shard_map.97
  59.8 0.5 collective-permute-start.20
  60.3 0.4 shard_map.99.base_ref
  60.8 0.4 shard_map.100
  61.2 0.1 collective-permute-start.19
  61.3 0.6 collective-permute-start.24
  61.9 0.6 collective-permute-done.19
  62.5 0.7 shard_map.101
  63.2 3.5 %collective-permute-done.20.refs_4_ = bf16[64,2048]{1,0:T(8,128)(2,1)S(1)} collective-permute-done((bf16[64,2048]{1,0:T(8,128)(2,1)S(1)}, bf16[64,2048]{1,0:T(8,128)(2,1)S(1)}, u32[]{:S(2)}, u32[]{:S(2)}) %collective-permute-start.20) | collective-permute-done | bytes 262176 | tf_op jit(solution)/shard_map/ppermute | solution.py:359
  66.8 0.5 collective-permute-start.25
  67.3 2.6 %collective-permute-start.27 = (bf16[32,2048]{1,0:T(8,128)(2,1)S(1)}, bf16[32,2048]{1,0:T(8,128)(2,1)S(1)}, u32[]{:S(2)}, u32[]{:S(2)}) collective-permute-start(bf16[32,2048]{1,0:T(8,128)(2,1)S(1)} %add_convert_fusion.2), channel_id=1, source_target_pairs={{0,8},{2,10},{4,12},{6,14},{8,0},{10,2},{12,4},{14,6},{1,9},{3,11}... | collective-permute-start | bytes 393224 | tf_op jit(solution)/shard_map/ppermute | solution.py:359
  69.9 1.6 %collective-permute-start.22 = (bf16[64,2048]{1,0:T(8,128)(2,1)S(1)}, bf16[64,2048]{1,0:T(8,128)(2,1)S(1)}, u32[]{:S(2)}, u32[]{:S(2)}) collective-permute-start(bf16[64,2048]{1,0:T(8,128)(2,1)S(1)} %get-tuple-element.48), channel_id=1, source_target_pairs={{0,4},{2,6},{4,0},{6,2},{8,12},{10,14},{12,8},{14,10},{1,5},{3,7},... | collective-permute-start | bytes 786440 | tf_op jit(solution)/shard_map/ppermute | solution.py:359
  71.5 0.6 collective-permute-start.21
  72.0 6.8 %collective-permute-done.25.refs_4_ = bf16[64,2048]{1,0:T(8,128)(2,1)S(1)} collective-permute-done((bf16[64,2048]{1,0:T(8,128)(2,1)S(1)}, bf16[64,2048]{1,0:T(8,128)(2,1)S(1)}, u32[]{:S(2)}, u32[]{:S(2)}) %collective-permute-start.25) | collective-permute-done | bytes 262176 | tf_op jit(solution)/shard_map/ppermute | solution.py:359
  78.9 1.5 %collective-permute-start.26 = (bf16[32,2048]{1,0:T(8,128)(2,1)S(1)}, bf16[32,2048]{1,0:T(8,128)(2,1)S(1)}, u32[]{:S(2)}, u32[]{:S(2)}) collective-permute-start(bf16[32,2048]{1,0:T(8,128)(2,1)S(1)} %add_convert_fusion), channel_id=1, source_target_pairs={{0,8},{2,10},{4,12},{6,14},{8,0},{10,2},{12,4},{14,6},{1,9},{3,11}... | collective-permute-start | bytes 393224 | tf_op jit(solution)/shard_map/ppermute | solution.py:359
  80.4 2.1 %collective-permute-done.22.refs_1_ = bf16[64,2048]{1,0:T(8,128)(2,1)S(1)} collective-permute-done((bf16[64,2048]{1,0:T(8,128)(2,1)S(1)}, bf16[64,2048]{1,0:T(8,128)(2,1)S(1)}, u32[]{:S(2)}, u32[]{:S(2)}) %collective-permute-start.22) | collective-permute-done | bytes 262176 | tf_op jit(solution)/shard_map/ppermute | solution.py:359
  82.6 3.8 %collective-permute-start.23 = (bf16[32,2048]{1,0:T(8,128)(2,1)S(1)}, bf16[32,2048]{1,0:T(8,128)(2,1)S(1)}, u32[]{:S(2)}, u32[]{:S(2)}) collective-permute-start(bf16[32,2048]{1,0:T(8,128)(2,1)S(1)} %add_convert_fusion.1), channel_id=1, source_target_pairs={{0,8},{2,10},{4,12},{6,14},{8,0},{10,2},{12,4},{14,6},{1,9},{3,11}... | collective-permute-start | bytes 393224 | tf_op jit(solution)/shard_map/ppermute | solution.py:359
  86.4 0.1 compare_convert_fusion.1
  86.4 0.9 shard_map.104
  87.3 4.5 %collective-permute-done.23.refs_2_ = bf16[32,2048]{1,0:T(8,128)(2,1)S(1)} collective-permute-done((bf16[32,2048]{1,0:T(8,128)(2,1)S(1)}, bf16[32,2048]{1,0:T(8,128)(2,1)S(1)}, u32[]{:S(2)}, u32[]{:S(2)}) %collective-permute-start.23) | collective-permute-done | bytes 131104 | tf_op jit(solution)/shard_map/ppermute | solution.py:359
  91.8 1.7 %shard_map.102 = bf16[128,4096]{1,0:T(8,128)(2,1)} custom-call(bf16[32,128]{1,0:T(8,128)(2,1)S(1)} %slice.48.refs_0_, bf16[32,128]{1,0:T(8,128)(2,1)S(1)} %collective-permute-done.21.refs_1_, f32[4,128]{1,0:T(4,128)S(1)} %get-tuple-element.62.refs_2_, f32[4,128]{1,0:T(4,128)S(1)} %get-tuple-element.61.refs_3_, ...), custom_call_target="tpu_custom_call" | custom-call | tf_op jit(solution)/shard_map/pallas_call | solution.py:284
  93.5 0.9 shard_map.103
  (41 shorter events, 0.3 us)
Async XLA Ops:
  0.6 0.7 copy-start.4
  0.6 0.7 copy-start.6
  1.3 4.5 %collective-permute-start = (s32[2,128]{1,0:T(2,128)S(1)}, s32[2,128]{1,0:T(2,128)S(1)}, u32[]{:S(2)}, u32[]{:S(2)}) collective-permute-start(s32[2,128]{1,0:T(2,128)S(1)} %pad_add_fusion), channel_id=1, source_target_pairs={{0,2},{2,0},{4,6},{6,4},{8,10},{10,8},{12,14},{14,12},{1,3},{3,1},... | collective-permute-start | bytes 3080 | tf_op jit(solution)/shard_map/ppermute | solution.py:356
  4.3 35.5 %collective-permute-start.14 = (bf16[128,4096]{1,0:T(8,128)(2,1)}, bf16[128,4096]{1,0:T(8,128)(2,1)S(1)}, u32[]{:S(2)}, u32[]{:S(2)}) collective-permute-start(bf16[128,4096]{1,0:T(8,128)(2,1)} %own_ref.11), channel_id=1, source_target_pairs={{0,2},{2,0},{4,6},{6,4},{8,10},{10,8},{12,14},{14,12},{1,3},{3,1},... | collective-permute-start | bytes 3145736 | tf_op jit(solution)/shard_map/ppermute | solution.py:356
  6.8 20.8 %copy-start.3 = (bf16[1,32,4096]{2,1,0:T(8,128)(2,1)S(1)}, bf16[1,32,4096]{2,1,0:T(8,128)(2,1)}, u32[]{:S(2)}) copy-start(bf16[1,32,4096]{2,1,0:T(8,128)(2,1)} %param.13) | copy-start | bytes 786436
  6.8 8.7 %collective-permute-start.1 = (bf16[16,4096]{1,0:T(8,128)(2,1)S(1)}, bf16[16,4096]{1,0:T(8,128)(2,1)S(1)}, u32[]{:S(2)}, u32[]{:S(2)}) collective-permute-start(bf16[16,4096]{1,0:T(8,128)(2,1)S(1)} %constant_dynamic-slice_fusion.1), channel_id=1, source_target_pairs={{0,4},{2,6},{4,0},{6,2},{8,12},{10,14},{12,8},{14,10},{1,5},{3,7},... | collective-permute-start | bytes 393224 | tf_op jit(solution)/shard_map/ppermute | solution.py:359
  11.0 24.5 %copy-start.2 = (bf16[1,32,4096]{2,1,0:T(8,128)(2,1)S(1)}, bf16[1,32,4096]{2,1,0:T(8,128)(2,1)}, u32[]{:S(2)}) copy-start(bf16[1,32,4096]{2,1,0:T(8,128)(2,1)} %param.12) | copy-start | bytes 786436
  11.0 29.3 %collective-permute-start.15 = (bf16[128,2048]{1,0:T(8,128)(2,1)}, bf16[128,2048]{1,0:T(8,128)(2,1)S(1)}, u32[]{:S(2)}, u32[]{:S(2)}) collective-permute-start(bf16[128,2048]{1,0:T(8,128)(2,1)} %get-tuple-element.57), channel_id=1, source_target_pairs={{0,2},{2,0},{4,6},{6,4},{8,10},{10,8},{12,14},{14,12},{1,3},{3,1},... | collective-permute-start | bytes 1572872 | tf_op jit(solution)/shard_map/ppermute | solution.py:356
  12.7 14.4 %collective-permute-start.4 = (bf16[16,4096]{1,0:T(8,128)(2,1)S(1)}, bf16[16,4096]{1,0:T(8,128)(2,1)S(1)}, u32[]{:S(2)}, u32[]{:S(2)}) collective-permute-start(bf16[16,4096]{1,0:T(8,128)(2,1)S(1)} %constant_dynamic-slice_fusion.1), channel_id=1, source_target_pairs={{0,12},{2,14},{4,8},{6,10},{8,4},{10,6},{12,0},{14,2},{1,13},{3,15... | collective-permute-start | bytes 393224 | tf_op jit(solution)/shard_map/ppermute | solution.py:359
  15.2 10.3 %collective-permute-start.3 = (bf16[16,4096]{1,0:T(8,128)(2,1)S(1)}, bf16[16,4096]{1,0:T(8,128)(2,1)S(1)}, u32[]{:S(2)}, u32[]{:S(2)}) collective-permute-start(bf16[16,4096]{1,0:T(8,128)(2,1)S(1)} %constant_dynamic-slice_fusion.1), channel_id=1, source_target_pairs={{0,8},{2,10},{4,12},{6,14},{8,0},{10,2},{12,4},{14,6},{1,9},{3,11}... | collective-permute-start | bytes 393224 | tf_op jit(solution)/shard_map/ppermute | solution.py:359
  15.4 11.7 %collective-permute-start.5 = (bf16[16,4096]{1,0:T(8,128)(2,1)S(1)}, bf16[16,4096]{1,0:T(8,128)(2,1)S(1)}, u32[]{:S(2)}, u32[]{:S(2)}) collective-permute-start(bf16[16,4096]{1,0:T(8,128)(2,1)S(1)} %collective-permute-done.1.refs_0_), channel_id=1, source_target_pairs={{0,16},{16,0},{1,17},{17,1},{2,18},{18,2},{3,19},{19,3},{4,20},{20... | collective-permute-start | bytes 393224 | tf_op jit(solution)/shard_map/ppermute | solution.py:362
  25.6 5.8 %collective-permute-start.6 = (bf16[16,4096]{1,0:T(8,128)(2,1)S(1)}, bf16[16,4096]{1,0:T(8,128)(2,1)S(1)}, u32[]{:S(2)}, u32[]{:S(2)}) collective-permute-start(bf16[16,4096]{1,0:T(8,128)(2,1)S(1)} %collective-permute-done.3.refs_1_), channel_id=1, source_target_pairs={{0,16},{16,0},{1,17},{17,1},{2,18},{18,2},{3,19},{19,3},{4,20},{20... | collective-permute-start | bytes 393224 | tf_op jit(solution)/shard_map/ppermute | solution.py:362
  27.1 5.7 %collective-permute-start.7 = (bf16[16,4096]{1,0:T(8,128)(2,1)S(1)}, bf16[16,4096]{1,0:T(8,128)(2,1)S(1)}, u32[]{:S(2)}, u32[]{:S(2)}) collective-permute-start(bf16[16,4096]{1,0:T(8,128)(2,1)S(1)} %collective-permute-done.4.refs_2_), channel_id=1, source_target_pairs={{0,16},{16,0},{1,17},{17,1},{2,18},{18,2},{3,19},{19,3},{4,20},{20... | collective-permute-start | bytes 393224 | tf_op jit(solution)/shard_map/ppermute | solution.py:362
  27.6 10.0 %collective-permute-start.8 = (bf16[16,4096]{1,0:T(8,128)(2,1)S(1)}, bf16[16,4096]{1,0:T(8,128)(2,1)S(1)}, u32[]{:S(2)}, u32[]{:S(2)}) collective-permute-start(bf16[16,4096]{1,0:T(8,128)(2,1)S(1)} %constant_dynamic-slice_fusion), channel_id=1, source_target_pairs={{0,8},{2,10},{4,12},{6,14},{8,0},{10,2},{12,4},{14,6},{1,9},{3,11}... | collective-permute-start | bytes 393224 | tf_op jit(solution)/shard_map/ppermute | solution.py:359
  31.4 8.4 %collective-permute-start.2 = (bf16[16,4096]{1,0:T(8,128)(2,1)S(1)}, bf16[16,4096]{1,0:T(8,128)(2,1)S(1)}, u32[]{:S(2)}, u32[]{:S(2)}) collective-permute-start(bf16[16,4096]{1,0:T(8,128)(2,1)S(1)} %constant_dynamic-slice_fusion), channel_id=1, source_target_pairs={{0,4},{2,6},{4,0},{6,2},{8,12},{10,14},{12,8},{14,10},{1,5},{3,7},... | collective-permute-start | bytes 393224 | tf_op jit(solution)/shard_map/ppermute | solution.py:359
  32.8 7.0 %collective-permute-start.9 = (bf16[16,4096]{1,0:T(8,128)(2,1)S(1)}, bf16[16,4096]{1,0:T(8,128)(2,1)S(1)}, u32[]{:S(2)}, u32[]{:S(2)}) collective-permute-start(bf16[16,4096]{1,0:T(8,128)(2,1)S(1)} %constant_dynamic-slice_fusion), channel_id=1, source_target_pairs={{0,12},{2,14},{4,8},{6,10},{8,4},{10,6},{12,0},{14,2},{1,13},{3,15... | collective-permute-start | bytes 393224 | tf_op jit(solution)/shard_map/ppermute | solution.py:359
  35.6 4.8 %copy-start.1 = (bf16[128,4096]{1,0:T(8,128)(2,1)S(1)}, bf16[128,4096]{1,0:T(8,128)(2,1)}, u32[]{:S(2)}) copy-start(bf16[128,4096]{1,0:T(8,128)(2,1)} %own_ref.11) | copy-start | bytes 3145732
  35.8 0.7 copy-start.5
  40.4 2.0 %copy-start = (bf16[128,4096]{1,0:T(8,128)(2,1)S(1)}, bf16[128,4096]{1,0:T(8,128)(2,1)}, u32[]{:S(2)}) copy-start(bf16[128,4096]{1,0:T(8,128)(2,1)} %own_ref.10) | copy-start | bytes 3145732
  41.1 1.3 %collective-permute-start.16 = (f32[32,256]{1,0:T(8,128)S(1)}, f32[32,256]{1,0:T(8,128)S(1)}, u32[]{:S(2)}, u32[]{:S(2)}) collective-permute-start(f32[32,256]{1,0:T(8,128)S(1)} %shard_map.96), channel_id=1, source_target_pairs={{0,1},{1,0},{2,3},{3,2},{4,5},{5,4},{6,7},{7,6},{8,9},{9,8},{10,11... | collective-permute-start | bytes 98312 | tf_op jit(solution)/shard_map/ppermute | solution.py:365
  42.8 9.6 %collective-permute-start.17 = (bf16[64,2048]{1,0:T(8,128)(2,1)S(1)}, bf16[64,2048]{1,0:T(8,128)(2,1)S(1)}, u32[]{:S(2)}, u32[]{:S(2)}) collective-permute-start(bf16[64,2048]{1,0:T(8,128)(2,1)S(1)} %get-tuple-element.41), channel_id=1, source_target_pairs={{0,4},{2,6},{4,0},{6,2},{8,12},{10,14},{12,8},{14,10},{1,5},{3,7},... | collective-permute-start | bytes 786440 | tf_op jit(solution)/shard_map/ppermute | solution.py:359
  44.5 6.4 %collective-permute-start.10 = (bf16[16,4096]{1,0:T(8,128)(2,1)S(1)}, bf16[16,4096]{1,0:T(8,128)(2,1)S(1)}, u32[]{:S(2)}, u32[]{:S(2)}) collective-permute-start(bf16[16,4096]{1,0:T(8,128)(2,1)S(1)} %collective-permute-done.2.refs_0_), channel_id=1, source_target_pairs={{0,16},{16,0},{1,17},{17,1},{2,18},{18,2},{3,19},{19,3},{4,20},{20... | collective-permute-start | bytes 393224 | tf_op jit(solution)/shard_map/ppermute | solution.py:362
  46.0 13.4 %collective-permute-start.13 = (bf16[128,2048]{1,0:T(8,128)(2,1)S(1)}, bf16[128,2048]{1,0:T(8,128)(2,1)S(1)}, u32[]{:S(2)}, u32[]{:S(2)}) collective-permute-start(bf16[128,2048]{1,0:T(8,128)(2,1)S(1)} %get-tuple-element.58), channel_id=1, source_target_pairs={{0,2},{2,0},{4,6},{6,4},{8,10},{10,8},{12,14},{14,12},{1,3},{3,1},... | collective-permute-start | bytes 1572872 | tf_op jit(solution)/shard_map/ppermute | solution.py:356
  46.5 8.6 %collective-permute-start.11 = (bf16[16,4096]{1,0:T(8,128)(2,1)S(1)}, bf16[16,4096]{1,0:T(8,128)(2,1)S(1)}, u32[]{:S(2)}, u32[]{:S(2)}) collective-permute-start(bf16[16,4096]{1,0:T(8,128)(2,1)S(1)} %collective-permute-done.8.refs_1_), channel_id=1, source_target_pairs={{0,16},{16,0},{1,17},{17,1},{2,18},{18,2},{3,19},{19,3},{4,20},{20... | collective-permute-start | bytes 393224 | tf_op jit(solution)/shard_map/ppermute | solution.py:362
  50.8 5.0 %collective-permute-start.12 = (bf16[16,4096]{1,0:T(8,128)(2,1)S(1)}, bf16[16,4096]{1,0:T(8,128)(2,1)S(1)}, u32[]{:S(2)}, u32[]{:S(2)}) collective-permute-start(bf16[16,4096]{1,0:T(8,128)(2,1)S(1)} %collective-permute-done.9.refs_2_), channel_id=1, source_target_pairs={{0,16},{16,0},{1,17},{17,1},{2,18},{18,2},{3,19},{19,3},{4,20},{20... | collective-permute-start | bytes 393224 | tf_op jit(solution)/shard_map/ppermute | solution.py:362
  52.4 8.8 %collective-permute-start.18 = (bf16[32,2048]{1,0:T(8,128)(2,1)S(1)}, bf16[32,2048]{1,0:T(8,128)(2,1)S(1)}, u32[]{:S(2)}, u32[]{:S(2)}) collective-permute-start(bf16[32,2048]{1,0:T(8,128)(2,1)S(1)} %add_convert_fusion.3), channel_id=1, source_target_pairs={{0,8},{2,10},{4,12},{6,14},{8,0},{10,2},{12,4},{14,6},{1,9},{3,11}... | collective-permute-start | bytes 393224 | tf_op jit(solution)/shard_map/ppermute | solution.py:359
  59.8 6.9 %collective-permute-start.20 = (bf16[64,2048]{1,0:T(8,128)(2,1)S(1)}, bf16[64,2048]{1,0:T(8,128)(2,1)S(1)}, u32[]{:S(2)}, u32[]{:S(2)}) collective-permute-start(bf16[64,2048]{1,0:T(8,128)(2,1)S(1)} %get-tuple-element.44), channel_id=1, source_target_pairs={{0,4},{2,6},{4,0},{6,2},{8,12},{10,14},{12,8},{14,10},{1,5},{3,7},... | collective-permute-start | bytes 786440 | tf_op jit(solution)/shard_map/ppermute | solution.py:359
  61.2 1.3 %collective-permute-start.19 = (f32[32,256]{1,0:T(8,128)S(1)}, f32[32,256]{1,0:T(8,128)S(1)}, u32[]{:S(2)}, u32[]{:S(2)}) collective-permute-start(f32[32,256]{1,0:T(8,128)S(1)} %shard_map.100), channel_id=1, source_target_pairs={{0,1},{1,0},{2,3},{3,2},{4,5},{5,4},{6,7},{7,6},{8,9},{9,8},{10,11... | collective-permute-start | bytes 98312 | tf_op jit(solution)/shard_map/ppermute | solution.py:365
  61.3 30.5 %collective-permute-start.24 = (bf16[128,4096]{1,0:T(8,128)(2,1)S(1)}, bf16[128,4096]{1,0:T(8,128)(2,1)S(1)}, u32[]{:S(2)}, u32[]{:S(2)}) collective-permute-start(bf16[128,4096]{1,0:T(8,128)(2,1)S(1)} %shard_map.94.adapter_ref.refs_4_), channel_id=1, source_target_pairs={{0,2},{2,0},{4,6},{6,4},{8,10},{10,8},{12,14},{14,12},{1,3},{3,1},... | collective-permute-start | bytes 3145736 | tf_op jit(solution)/shard_map/ppermute | solution.py:356
  66.8 12.1 %collective-permute-start.25 = (bf16[64,2048]{1,0:T(8,128)(2,1)S(1)}, bf16[64,2048]{1,0:T(8,128)(2,1)S(1)}, u32[]{:S(2)}, u32[]{:S(2)}) collective-permute-start(bf16[64,2048]{1,0:T(8,128)(2,1)S(1)} %get-tuple-element.51), channel_id=1, source_target_pairs={{0,4},{2,6},{4,0},{6,2},{8,12},{10,14},{12,8},{14,10},{1,5},{3,7},... | collective-permute-start | bytes 786440 | tf_op jit(solution)/shard_map/ppermute | solution.py:359
  67.3 19.2 %collective-permute-start.27 = (bf16[32,2048]{1,0:T(8,128)(2,1)S(1)}, bf16[32,2048]{1,0:T(8,128)(2,1)S(1)}, u32[]{:S(2)}, u32[]{:S(2)}) collective-permute-start(bf16[32,2048]{1,0:T(8,128)(2,1)S(1)} %add_convert_fusion.2), channel_id=1, source_target_pairs={{0,8},{2,10},{4,12},{6,14},{8,0},{10,2},{12,4},{14,6},{1,9},{3,11}... | collective-permute-start | bytes 393224 | tf_op jit(solution)/shard_map/ppermute | solution.py:359
  69.9 12.7 %collective-permute-start.22 = (bf16[64,2048]{1,0:T(8,128)(2,1)S(1)}, bf16[64,2048]{1,0:T(8,128)(2,1)S(1)}, u32[]{:S(2)}, u32[]{:S(2)}) collective-permute-start(bf16[64,2048]{1,0:T(8,128)(2,1)S(1)} %get-tuple-element.48), channel_id=1, source_target_pairs={{0,4},{2,6},{4,0},{6,2},{8,12},{10,14},{12,8},{14,10},{1,5},{3,7},... | collective-permute-start | bytes 786440 | tf_op jit(solution)/shard_map/ppermute | solution.py:359
  71.5 15.9 %collective-permute-start.21 = (bf16[32,128]{1,0:T(8,128)(2,1)S(1)}, bf16[32,128]{1,0:T(8,128)(2,1)S(1)}, u32[]{:S(2)}, u32[]{:S(2)}) collective-permute-start(bf16[32,128]{1,0:T(8,128)(2,1)S(1)} %slice.51), channel_id=1, source_target_pairs={{0,2},{2,0},{4,6},{6,4},{8,10},{10,8},{12,14},{14,12},{1,3},{3,1},... | collective-permute-start | bytes 24584 | tf_op jit(solution)/shard_map/ppermute | solution.py:356
  78.9 14.7 %collective-permute-start.26 = (bf16[32,2048]{1,0:T(8,128)(2,1)S(1)}, bf16[32,2048]{1,0:T(8,128)(2,1)S(1)}, u32[]{:S(2)}, u32[]{:S(2)}) collective-permute-start(bf16[32,2048]{1,0:T(8,128)(2,1)S(1)} %add_convert_fusion), channel_id=1, source_target_pairs={{0,8},{2,10},{4,12},{6,14},{8,0},{10,2},{12,4},{14,6},{1,9},{3,11}... | collective-permute-start | bytes 393224 | tf_op jit(solution)/shard_map/ppermute | solution.py:359
  82.6 9.2 %collective-permute-start.23 = (bf16[32,2048]{1,0:T(8,128)(2,1)S(1)}, bf16[32,2048]{1,0:T(8,128)(2,1)S(1)}, u32[]{:S(2)}, u32[]{:S(2)}) collective-permute-start(bf16[32,2048]{1,0:T(8,128)(2,1)S(1)} %add_convert_fusion.1), channel_id=1, source_target_pairs={{0,8},{2,10},{4,12},{6,14},{8,0},{10,2},{12,4},{14,6},{1,9},{3,11}... | collective-permute-start | bytes 393224 | tf_op jit(solution)/shard_map/ppermute | solution.py:359

commit v4 on v2

v4 whole, which is shorter than its diff:
```python
import jax
import jax.numpy as jnp
from jax import lax
from jax.experimental import pallas as pl
from jax.experimental.pallas import tpu as pltpu
from jax.sharding import PartitionSpec as P

adapter_scale_factor = 2.0


def contract_last(left, right):
    return lax.dot_general(
        left, right, (((1,), (1,)), ((), ())), preferred_element_type=jnp.float32
    )


def contract_first(left, right):
    return lax.dot_general(
        left, right, (((0,), (0,)), ((), ())), preferred_element_type=jnp.float32
    )


def token_owner(tenant_ids, owner_map):
    tenant_total = owner_map.shape[0]
    match = tenant_ids[:, None] == jnp.arange(tenant_total, dtype=jnp.int32)[None, :]
    return jnp.sum(jnp.where(match, owner_map[None, :], 0), axis=1)


def token_weight(document_index_per_token):
    same_doc = document_index_per_token[:, None] == document_index_per_token[None, :]
    sequence_length = jnp.sum(same_doc.astype(jnp.float32), axis=1)
    return adapter_scale_factor / sequence_length


def after(value, *others):
    return lax.optimization_barrier((value,) + others)[0]


def route_tokens(
    features, cotangent, tenant_ids, document_index_per_token, owner_map, adapter_down, adapter_up
):
    ranks = lax.axis_size("dp")
    rows = features.shape[0]
    width = features.shape[1]
    capacity = max(2, 2 * rows // ranks)
    slots = ranks * capacity
    token_row_index = jnp.arange(rows, dtype=jnp.int32)
    target = token_owner(tenant_ids, owner_map)
    routing_weight = token_weight(document_index_per_token)
    earlier = (token_row_index[:, None] > token_row_index[None, :]) & (
        target[:, None] == target[None, :]
    )
    before = jnp.sum(earlier.astype(jnp.int32), axis=1)
    slot_of = target * capacity + before
    placed = slot_of[None, :] == jnp.arange(slots, dtype=jnp.int32)[:, None]
    slot_weight = jnp.sum(
        jnp.where(placed, routing_weight[None, :], jnp.zeros_like(routing_weight)[None, :]), axis=1
    )

    def pack(values):
        return jnp.dot(
            placed.astype(values.dtype), values, preferred_element_type=jnp.float32
        ).astype(values.dtype)

    def exchange(values):
        return lax.all_to_all(values, "dp", split_axis=0, concat_axis=0, tiled=True)

    down_own = adapter_down[0]
    up_own = adapter_up[0]
    got_x = exchange(pack(features).reshape(ranks, capacity, width)).reshape(slots, width)
    got_g = exchange(pack(cotangent).reshape(ranks, capacity, width)).reshape(slots, width)
    got_w = exchange(slot_weight.reshape(ranks, capacity)).reshape(slots)
    low_h, low_u = lax.psum(
        (contract_last(got_x, down_own), contract_last(got_g, up_own)), "tensor"
    )
    scaled_h = (low_h * got_w[:, None]).astype(jnp.bfloat16)
    scaled_u = (low_u * got_w[:, None]).astype(jnp.bfloat16)
    up_adapter_gradient = contract_first(scaled_h, got_g)
    grad_down = contract_first(scaled_u, got_x)
    slot_dx = jnp.dot(scaled_u, down_own, preferred_element_type=jnp.float32).astype(jnp.bfloat16)
    returned = exchange(slot_dx.reshape(ranks, capacity, width)).reshape(slots, width)
    input_grad = contract_first(placed.astype(jnp.bfloat16), returned).astype(jnp.bfloat16)
    return (input_grad, grad_down[None], up_adapter_gradient[None])


VMEM_LIMIT = 32 * 1024 * 1024


def whole(*shape):
    return pl.BlockSpec(shape, lambda _: (0,) * len(shape))


def column_cut(rows, wide, at):
    return pl.BlockSpec((rows, wide), lambda _: (0, at))


def small_kernel(kernel, out_shape, in_specs, out_specs):
    return pl.pallas_call(
        kernel,
        grid=(1,),
        out_shape=out_shape,
        in_specs=in_specs,
        out_specs=out_specs,
        compiler_params=pltpu.CompilerParams(vmem_limit_bytes=VMEM_LIMIT),
        cost_estimate=pl.CostEstimate(flops=0, bytes_accessed=0, transcendentals=0),
    )


def spread(scaled, held_ref):
    return jnp.concatenate(
        [
            jnp.where(held_ref[step : step + 1, :] > 0, scaled, 0.0).astype(jnp.bfloat16)
            for step in range(held_ref.shape[0])
        ]
    )


def join_kernel(layer_ref, own_ref, *refs):
    *halves, out_ref = refs
    count = len(halves) // 2
    rank = own_ref.shape[0]
    out_ref[:rank, :] = own_ref[...]
    first = layer_ref[0] == 0
    for step in range(count):
        got, other = halves[step][...], halves[count + step][...]
        low = (step + 1) * rank
        middle = low + rank // 2
        out_ref[low:middle, :] = jnp.where(first, got, other)
        out_ref[middle : low + rank, :] = jnp.where(first, other, got)


def join(layer, own, got, other):
    rank, width = own.shape
    rows = (len(got) + 1) * rank
    return small_kernel(
        join_kernel,
        jax.ShapeDtypeStruct((rows, width), own.dtype),
        [pl.BlockSpec(memory_space=pltpu.SMEM), whole(rank, width)]
        + [whole(rank // 2, width)] * (2 * len(got)),
        whole(rows, width),
    )(layer, own, *got, *other)


def project_kernel(adapter_ref, own_ref, other_ref, held_ref, base_ref, out_ref):
    columns, tokens = held_ref.shape
    rows = tokens // 2
    rank = adapter_ref.shape[0] // columns
    adapters = adapter_ref[...]
    for part, rows_ref in enumerate((own_ref, other_ref)):
        cut = slice(part * rows, (part + 1) * rows)
        low = contract_last(adapters, rows_ref[...])
        total = base_ref[:, cut]
        for step in range(columns):
            total = total + jnp.where(
                held_ref[step : step + 1, cut] > 0, low[step * rank : (step + 1) * rank], 0.0
            )
        out_ref[:, cut] = total


def project(adapters, own_rows, other_rows, held, base, at):
    rows, wide = other_rows.shape
    return small_kernel(
        project_kernel,
        jax.ShapeDtypeStruct(base.shape, jnp.float32),
        [
            column_cut(adapters.shape[0], wide, at),
            column_cut(rows, wide, at),
            whole(rows, wide),
            whole(*held.shape),
            whole(*base.shape),
        ],
        whole(*base.shape),
    )(adapters, own_rows, other_rows, held, base)


def partial_kernel(scaled_ref, held_ref, own_ref, other_ref, *out_refs):
    rows = own_ref.shape[0]
    rank = scaled_ref.shape[0]
    left = spread(scaled_ref[...], held_ref)
    wide = out_refs[0].shape[1]
    for i in range(len(out_refs) // 2):
        cut = slice(i * wide, (i + 1) * wide)
        total = jnp.dot(left[:, :rows], own_ref[:, cut], preferred_element_type=jnp.float32)
        total = total + jnp.dot(
            left[:, rows:], other_ref[:, cut], preferred_element_type=jnp.float32
        )
        for out_ref, blocks in zip(out_refs[2 * i : 2 * i + 2], ((0, 2), (1, 3))):
            for at, block in enumerate(blocks):
                out_ref[at * rank : (at + 1) * rank, :] = total[
                    block * rank : (block + 1) * rank
                ].astype(out_ref.dtype)


def partials(scaled, held, own_rows, other_rows, at, pieces):
    rows, wide = other_rows.shape
    shape = (2 * scaled.shape[0], wide // pieces)
    kinds = [jnp.float32, jnp.bfloat16] * pieces
    return small_kernel(
        partial_kernel,
        [jax.ShapeDtypeStruct(shape, kind) for kind in kinds],
        [
            whole(*scaled.shape),
            whole(*held.shape),
            column_cut(rows, wide, at),
            whole(rows, wide),
        ],
        [whole(*shape)] * len(kinds),
    )(scaled, held, own_rows, other_rows)


def add_kernel(*refs):
    *parts, out_ref = refs
    rank = out_ref.shape[1]
    wide = parts[0].shape[1]
    for i in range(len(parts) // 3):
        total = parts[3 * i][:rank, :]
        for part in parts[3 * i + 1 : 3 * i + 3]:
            total = total + part[:rank, :].astype(jnp.float32)
        out_ref[0, :, i * wide : (i + 1) * wide] = total


def add_parts(groups, rank, width):
    operands = [part for group in groups for part in group]
    return small_kernel(
        add_kernel,
        jax.ShapeDtypeStruct((1, rank, width), jnp.float32),
        [whole(*operand.shape) for operand in operands],
        whole(1, rank, width),
    )(*operands)


def input_grad_kernel(low_ref, low_there_ref, held_ref, held_there_ref, down_ref, there_ref, dx_ref):
    dx = contract_first(spread(low_ref[...], held_ref), down_ref[...])
    dx = dx + contract_first(spread(low_there_ref[...], held_there_ref), there_ref[...])
    dx_ref[...] = dx.astype(dx_ref.dtype)


def input_gradient(*operands):
    shape = (operands[0].shape[1], operands[-1].shape[1])
    return small_kernel(
        input_grad_kernel,
        jax.ShapeDtypeStruct(shape, jnp.bfloat16),
        [whole(*operand.shape) for operand in operands],
        whole(*shape),
    )(*operands)


def route_adapters(
    features, cotangent, tenant_ids, document_index_per_token, owner_map, adapter_down, adapter_up
):
    ranks = lax.axis_size("dp")
    columns = ranks // 2
    rows, width = features.shape
    rank = adapter_down.shape[1]
    half = rank // 2
    me = lax.axis_index("dp")
    side, place = me % 2, me // 2
    layer = lax.axis_index("parts")

    def swap_side(value):
        return lax.ppermute(value, "dp", [(i, i ^ 1) for i in range(ranks)])

    def hop(value, by):
        return lax.ppermute(value, "dp", [(i, i ^ (2 * by)) for i in range(ranks)])

    def swap_layer(value):
        return lax.ppermute(value, "parts", [(0, 1), (1, 0)])

    def swap_core(value):
        return lax.ppermute(value, "tensor", [(0, 1), (1, 0)])

    def fetch(own):
        mine = lax.dynamic_slice(own, (layer * half, 0), (half, width))
        got = {step: hop(mine, step) for step in range(columns - 1, 0, -1)}
        return [got[step] for step in range(1, columns)]

    pieces = 2
    wide = width // pieces
    layer_of = layer.astype(jnp.int32)[None]
    other_x = swap_side(features)
    ids_there = swap_side(jnp.stack([tenant_ids, document_index_per_token]))
    down_own = after(adapter_down[0], ids_there)
    own_g = [cotangent[:, i * wide : (i + 1) * wide] for i in range(pieces)]
    down_got = fetch(down_own)
    down = join(layer_of, down_own, down_got, [swap_layer(got) for got in down_got])
    up_own = after(adapter_up[0], down_got[0])
    up_got = fetch(up_own)
    up_halves = [after(up_got[0], down)] + up_got[1:]
    up = join(layer_of, up_own, up_halves, [swap_layer(got) for got in up_halves])
    ids_there = after(ids_there, down)
    other_g = [swap_side(cut) for cut in own_g]

    owner, owner_there = token_owner(tenant_ids, owner_map), token_owner(ids_there[0], owner_map)
    weight = token_weight(document_index_per_token)
    owner_here = jnp.concatenate([owner, owner_there])
    weight_here = jnp.concatenate([weight, token_weight(ids_there[1])])
    block_owner = (place ^ jnp.arange(columns, dtype=jnp.int32)) * 2 + side
    block_owner_there = block_owner + 1 - 2 * side
    held = (block_owner[:, None] == owner_here[None, :]).astype(jnp.float32)
    own_held = (block_owner[:, None] == owner[None, :]).astype(jnp.float32)
    own_there = (block_owner_there[:, None] == owner[None, :]).astype(jnp.float32)

    def combine(low):
        return ((low + swap_core(low)) * weight_here[None, :]).astype(jnp.bfloat16)

    def second_block(kept, came):
        return (kept[rank:] + came[rank:].astype(jnp.float32)).astype(jnp.bfloat16)

    nothing = jnp.zeros((rank, 2 * rows), jnp.float32)
    x_in = after(after(other_x, *up_got), other_g[0])
    scaled_h = combine(project(down, features, x_in, held, nothing, 0))

    first_g = after(other_g[0], up)
    kept, away = partials(scaled_h, held, cotangent, first_g, 0, 1)
    came = hop(away, 1)
    onward = second_block(kept, came)
    up_groups = [(kept, came, hop(onward, 2))]
    low_u = project(up, cotangent, after(first_g, kept), held, nothing, 0)
    low_u = project(up, cotangent, other_g[1], held, low_u, 1)
    scaled_u = after(combine(low_u), onward)

    outs = partials(scaled_u, held, features, other_x, 0, pieces)
    down_kept, down_came = outs[0::2], [hop(away, 1) for away in outs[1::2]]
    kept, away = partials(scaled_h, held, cotangent, after(other_g[1], outs[0]), 1, 1)
    came = hop(away, 1)
    down_groups = [
        (kept_x, came_x, hop(second_block(kept_x, came_x), 2))
        for kept_x, came_x in zip(down_kept, down_came)
    ]
    onward = second_block(kept, after(came, outs[0]))
    up_groups.append((kept, came, hop(onward, 2)))
    back = swap_side(after(scaled_u, onward)[:, rows:])
    down_there = swap_side(after(down, other_g[1]))
    up_adapter_gradient = add_parts(up_groups, rank, width)
    input_grad = input_gradient(scaled_u[:, :rows], back, own_held, own_there, down, down_there)
    kept, came, last = down_groups[-1]
    down_groups[-1] = (kept, came, after(last, input_grad))
    grad_down = add_parts(down_groups, rank, width)
    return (input_grad, grad_down, up_adapter_gradient)


def shards(features, *others):
    ranks = lax.axis_size("dp")
    rank = others[-1].shape[1]
    slots = 2 * features.shape[0] // ranks
    fits = rank % 32 == 0 and features.shape[1] % 1024 == 0
    if slots >= rank and fits and ranks == 8 and lax.axis_size("parts") == 2:
        return route_adapters(features, *others)
    return route_tokens(features, *others)


def solution(mesh):
    return jax.shard_map(
        shards,
        mesh=mesh,
        in_specs=(
            P(("parts", "dp"), "tensor"),
            P(("parts", "dp"), "tensor"),
            P(("parts", "dp")),
            P(("parts", "dp")),
            P(),
            P("dp", None, "tensor"),
            P("dp", None, "tensor"),
        ),
        out_specs=(
            P(("parts", "dp"), "tensor"),
            P(("parts", "dp"), None, "tensor"),
            P(("parts", "dp"), None, "tensor"),
        ),
        check_vma=False,
    )
```

time: 106 us -> 92.6 us (0.87)
  the two profiles are of different devices: /device:TPU:13 before, /device:TPU:0 now
where the time goes in v4:
time: 92.6 us; the launch traced here: 92.4 us
  waiting for transfers between devices  45.6 us (49%)
  starting transfers between devices  35 us (38%)
  Pallas kernels  6.71 us (7%)
  local copies, waits for them, and re-layouts  3.36 us (4%)
    ppermute x14, waiting for transfers between devices, hop(): return lax.ppermute(value, 'dp', [(i, i ^ 2 * by) for i in range(ranks)])  34.2 us
    ppermute x14, starting transfers between devices, hop(): return lax.ppermute(value, 'dp', [(i, i ^ 2 * by) for i in range(ranks)])  21.6 us
    ppermute x6, waiting for transfers between devices, swap_side(): return lax.ppermute(value, 'dp', [(i, i ^ 1) for i in range(ranks)])  7.21 us
    ppermute x6, starting transfers between devices, swap_layer(): return lax.ppermute(value, 'parts', [(0, 1), (1, 0)])  6.69 us
    ppermute x6, starting transfers between devices, swap_side(): return lax.ppermute(value, 'dp', [(i, i ^ 1) for i in range(ranks)])  6.62 us
    ppermute x6, waiting for transfers between devices, swap_layer(): return lax.ppermute(value, 'parts', [(0, 1), (1, 0)])  3.02 us
  transfers between devices with their start and end apart: 28, of which 15 were waited for; matrix products, arithmetic and copies ran while one was open for 3% of the time, Pallas kernels for 5%

profile of v4, /device:TPU:0, one launch (start us, length us, event | category | flops | bytes accessed | tf_op | source)
XLA Modules:
  0.0 92.4 jit_solution(18282278400022904301)
XLA Ops:
  0.7 0.6 copy-done.4
  1.3 0.0 copy-done.6
  1.3 3.0 %collective-permute-start = (s32[2,128]{1,0:T(2,128)S(1)}, s32[2,128]{1,0:T(2,128)S(1)}, u32[]{:S(2)}, u32[]{:S(2)}) collective-permute-start(s32[2,128]{1,0:T(2,128)S(1)} %pad_add_fusion), channel_id=1, source_target_pairs={{0,2},{2,0},{4,6},{6,4},{8,10},{10,8},{12,14},{14,12},{1,3},{3,1},... | collective-permute-start | bytes 3080 | tf_op jit(solution)/shard_map/ppermute | solution.py:261
  4.3 0.1 collective-permute-start.15
  4.4 1.3 %fusion = (bf16[128,2048]{1,0:T(8,128)(2,1)S(1)}, bf16[128,2048]{1,0:T(8,128)(2,1)S(1)}) fusion(bf16[128,4096]{1,0:T(8,128)(2,1)} %own_ref.11), kind=kLoop, calls=%fused_computation.26 | loop fusion | bytes 2097152 | tf_op jit(solution)/shard_map/slice | solution.py:283
  5.7 2.0 %collective-permute-start.14 = (bf16[128,2048]{1,0:T(8,128)(2,1)S(1)}, bf16[128,2048]{1,0:T(8,128)(2,1)S(1)}, u32[]{:S(2)}, u32[]{:S(2)}) collective-permute-start(bf16[128,2048]{1,0:T(8,128)(2,1)S(1)} %get-tuple-element.51), channel_id=1, source_target_pairs={{0,2},{2,0},{4,6},{6,4},{8,10},{10,8},{12,14},{14,12},{1,3},{3,1},... | collective-permute-start | bytes 1572872 | tf_op jit(solution)/shard_map/ppermute | solution.py:261
  7.7 0.2 convert_reduce_fusion.1
  7.9 0.7 constant_dynamic-slice_fusion.1
  8.6 1.6 %collective-permute-start.1 = (bf16[16,4096]{1,0:T(8,128)(2,1)}, bf16[16,4096]{1,0:T(8,128)(2,1)S(1)}, u32[]{:S(2)}, u32[]{:S(2)}) collective-permute-start(bf16[16,4096]{1,0:T(8,128)(2,1)} %constant_dynamic-slice_fusion.1), channel_id=1, source_target_pairs={{0,4},{2,6},{4,0},{6,2},{8,12},{10,14},{12,8},{14,10},{1,5},{3,7},... | collective-permute-start | bytes 393224 | tf_op jit(solution)/shard_map/ppermute | solution.py:264
  10.1 2.6 %collective-permute-start.3 = (bf16[16,4096]{1,0:T(8,128)(2,1)}, bf16[16,4096]{1,0:T(8,128)(2,1)S(1)}, u32[]{:S(2)}, u32[]{:S(2)}) collective-permute-start(bf16[16,4096]{1,0:T(8,128)(2,1)} %constant_dynamic-slice_fusion.1), channel_id=1, source_target_pairs={{0,8},{2,10},{4,12},{6,14},{8,0},{10,2},{12,4},{14,6},{1,9},{3,11}... | collective-permute-start | bytes 393224 | tf_op jit(solution)/shard_map/ppermute | solution.py:264
  12.7 0.2 collective-permute-start.4
  13.0 2.2 %collective-permute-done.1.refs_0_ = bf16[16,4096]{1,0:T(8,128)(2,1)S(1)} collective-permute-done((bf16[16,4096]{1,0:T(8,128)(2,1)}, bf16[16,4096]{1,0:T(8,128)(2,1)S(1)}, u32[]{:S(2)}, u32[]{:S(2)}) %collective-permute-start.1) | collective-permute-done | bytes 131104 | tf_op jit(solution)/shard_map/ppermute | solution.py:264
  15.2 1.5 %collective-permute-start.5 = (bf16[16,4096]{1,0:T(8,128)(2,1)S(1)}, bf16[16,4096]{1,0:T(8,128)(2,1)S(1)}, u32[]{:S(2)}, u32[]{:S(2)}) collective-permute-start(bf16[16,4096]{1,0:T(8,128)(2,1)S(1)} %collective-permute-done.1.refs_0_), channel_id=1, source_target_pairs={{0,16},{16,0},{1,17},{17,1},{2,18},{18,2},{3,19},{19,3},{4,20},{20... | collective-permute-start | bytes 393224 | tf_op jit(solution)/shard_map/ppermute | solution.py:267
  16.7 5.7 %collective-permute-done.3.refs_1_ = bf16[16,4096]{1,0:T(8,128)(2,1)S(1)} collective-permute-done((bf16[16,4096]{1,0:T(8,128)(2,1)}, bf16[16,4096]{1,0:T(8,128)(2,1)S(1)}, u32[]{:S(2)}, u32[]{:S(2)}) %collective-permute-start.3) | collective-permute-done | bytes 131104 | tf_op jit(solution)/shard_map/ppermute | solution.py:264
  22.5 1.5 %collective-permute-start.6 = (bf16[16,4096]{1,0:T(8,128)(2,1)S(1)}, bf16[16,4096]{1,0:T(8,128)(2,1)S(1)}, u32[]{:S(2)}, u32[]{:S(2)}) collective-permute-start(bf16[16,4096]{1,0:T(8,128)(2,1)S(1)} %collective-permute-done.3.refs_1_), channel_id=1, source_target_pairs={{0,16},{16,0},{1,17},{17,1},{2,18},{18,2},{3,19},{19,3},{4,20},{20... | collective-permute-start | bytes 393224 | tf_op jit(solution)/shard_map/ppermute | solution.py:267
  24.0 0.5 collective-permute-start.7
  24.5 2.5 %collective-permute-start.8 = (bf16[16,4096]{1,0:T(8,128)(2,1)S(1)}, bf16[16,4096]{1,0:T(8,128)(2,1)S(1)}, u32[]{:S(2)}, u32[]{:S(2)}) collective-permute-start(bf16[16,4096]{1,0:T(8,128)(2,1)S(1)} %constant_dynamic-slice_fusion), channel_id=1, source_target_pairs={{0,8},{2,10},{4,12},{6,14},{8,0},{10,2},{12,4},{14,6},{1,9},{3,11}... | collective-permute-start | bytes 393224 | tf_op jit(solution)/shard_map/ppermute | solution.py:264
  27.0 0.4 collective-permute-done.6.refs_4_
  27.4 2.5 %collective-permute-start.9 = (bf16[16,4096]{1,0:T(8,128)(2,1)S(1)}, bf16[16,4096]{1,0:T(8,128)(2,1)S(1)}, u32[]{:S(2)}, u32[]{:S(2)}) collective-permute-start(bf16[16,4096]{1,0:T(8,128)(2,1)S(1)} %constant_dynamic-slice_fusion), channel_id=1, source_target_pairs={{0,12},{2,14},{4,8},{6,10},{8,4},{10,6},{12,0},{14,2},{1,13},{3,15... | collective-permute-start | bytes 393224 | tf_op jit(solution)/shard_map/ppermute | solution.py:264
  29.9 0.0 collective-permute-start.2
  29.9 0.1 shard_map.94.adapter_ref.down_ref
  30.0 0.7 copy-done.5
  30.7 0.1 select_reduce_fusion.1
  30.8 0.1 compare_convert_fusion.held_ref
  30.9 5.8 %collective-permute-done.2.refs_0_ = bf16[16,4096]{1,0:T(8,128)(2,1)S(1)} collective-permute-done((bf16[16,4096]{1,0:T(8,128)(2,1)S(1)}, bf16[16,4096]{1,0:T(8,128)(2,1)S(1)}, u32[]{:S(2)}, u32[]{:S(2)}) %collective-permute-start.2) | collective-permute-done | bytes 131104 | tf_op jit(solution)/shard_map/ppermute | solution.py:264
  36.7 0.5 collective-permute-start.13
  37.3 0.2 convert_reduce_fusion
  37.5 1.1 %collective-permute-start.10 = (bf16[16,4096]{1,0:T(8,128)(2,1)S(1)}, bf16[16,4096]{1,0:T(8,128)(2,1)S(1)}, u32[]{:S(2)}, u32[]{:S(2)}) collective-permute-start(bf16[16,4096]{1,0:T(8,128)(2,1)S(1)} %collective-permute-done.2.refs_0_), channel_id=1, source_target_pairs={{0,16},{16,0},{1,17},{17,1},{2,18},{18,2},{3,19},{19,3},{4,20},{20... | collective-permute-start | bytes 393224 | tf_op jit(solution)/shard_map/ppermute | solution.py:267
  38.6 1.0 %collective-permute-start.11 = (bf16[16,4096]{1,0:T(8,128)(2,1)S(1)}, bf16[16,4096]{1,0:T(8,128)(2,1)S(1)}, u32[]{:S(2)}, u32[]{:S(2)}) collective-permute-start(bf16[16,4096]{1,0:T(8,128)(2,1)S(1)} %collective-permute-done.8.refs_1_), channel_id=1, source_target_pairs={{0,16},{16,0},{1,17},{17,1},{2,18},{18,2},{3,19},{19,3},{4,20},{20... | collective-permute-start | bytes 393224 | tf_op jit(solution)/shard_map/ppermute | solution.py:267
  39.6 1.1 %collective-permute-start.12 = (bf16[16,4096]{1,0:T(8,128)(2,1)S(1)}, bf16[16,4096]{1,0:T(8,128)(2,1)S(1)}, u32[]{:S(2)}, u32[]{:S(2)}) collective-permute-start(bf16[16,4096]{1,0:T(8,128)(2,1)S(1)} %collective-permute-done.9.refs_2_), channel_id=1, source_target_pairs={{0,16},{16,0},{1,17},{17,1},{2,18},{18,2},{3,19},{19,3},{4,20},{20... | collective-permute-start | bytes 393224 | tf_op jit(solution)/shard_map/ppermute | solution.py:267
  40.6 1.2 %collective-permute-done.14.other_ref = bf16[128,2048]{1,0:T(8,128)(2,1)S(1)} collective-permute-done((bf16[128,2048]{1,0:T(8,128)(2,1)S(1)}, bf16[128,2048]{1,0:T(8,128)(2,1)S(1)}, u32[]{:S(2)}, u32[]{:S(2)}) %collective-permute-start.14) | collective-permute-done | bytes 524320 | tf_op jit(solution)/shard_map/ppermute | solution.py:261
  41.9 0.7 shard_map.96
  42.6 0.1 collective-permute-start.16
  42.7 1.2 %collective-permute-done.11.refs_4_ = bf16[16,4096]{1,0:T(8,128)(2,1)S(1)} collective-permute-done((bf16[16,4096]{1,0:T(8,128)(2,1)S(1)}, bf16[16,4096]{1,0:T(8,128)(2,1)S(1)}, u32[]{:S(2)}, u32[]{:S(2)}) %collective-permute-start.11) | collective-permute-done | bytes 131104 | tf_op jit(solution)/shard_map/ppermute | solution.py:267
  43.9 1.4 %collective-permute-done.12.refs_5_ = bf16[16,4096]{1,0:T(8,128)(2,1)S(1)} collective-permute-done((bf16[16,4096]{1,0:T(8,128)(2,1)S(1)}, bf16[16,4096]{1,0:T(8,128)(2,1)S(1)}, u32[]{:S(2)}, u32[]{:S(2)}) %collective-permute-start.12) | collective-permute-done | bytes 131104 | tf_op jit(solution)/shard_map/ppermute | solution.py:267
  45.3 0.1 shard_map.95.adapter_ref
  45.4 0.4 shard_map.97
  45.8 0.7 collective-permute-start.18
  46.5 0.4 shard_map.98.base_ref
  47.0 4.6 %collective-permute-done.13.other_ref = bf16[128,2048]{1,0:T(8,128)(2,1)S(1)} collective-permute-done((bf16[128,2048]{1,0:T(8,128)(2,1)S(1)}, bf16[128,2048]{1,0:T(8,128)(2,1)S(1)}, u32[]{:S(2)}, u32[]{:S(2)}) %collective-permute-start.13) | collective-permute-done | bytes 524320 | tf_op jit(solution)/shard_map/ppermute | solution.py:261
  51.6 0.4 shard_map.99
  52.1 0.1 collective-permute-start.17
  52.1 1.2 %collective-permute-done.17 = f32[32,256]{1,0:T(8,128)S(1)} collective-permute-done((f32[32,256]{1,0:T(8,128)S(1)}, f32[32,256]{1,0:T(8,128)S(1)}, u32[]{:S(2)}, u32[]{:S(2)}) %collective-permute-start.17) | collective-permute-done | bytes 32800 | tf_op jit(solution)/shard_map/ppermute | solution.py:270
  53.4 0.7 shard_map.100
  54.1 0.4 shard_map.101
  54.5 1.6 %collective-permute-start.19 = (bf16[64,2048]{1,0:T(8,128)(2,1)S(1)}, bf16[64,2048]{1,0:T(8,128)(2,1)S(1)}, u32[]{:S(2)}, u32[]{:S(2)}) collective-permute-start(bf16[64,2048]{1,0:T(8,128)(2,1)S(1)} %get-tuple-element.39), channel_id=1, source_target_pairs={{0,4},{2,6},{4,0},{6,2},{8,12},{10,14},{12,8},{14,10},{1,5},{3,7},... | collective-permute-start | bytes 786440 | tf_op jit(solution)/shard_map/ppermute | solution.py:264
  56.2 0.5 collective-permute-start.21
  56.7 2.6 %collective-permute-start.26 = (bf16[32,2048]{1,0:T(8,128)(2,1)S(1)}, bf16[32,2048]{1,0:T(8,128)(2,1)S(1)}, u32[]{:S(2)}, u32[]{:S(2)}) collective-permute-start(bf16[32,2048]{1,0:T(8,128)(2,1)S(1)} %add_convert_fusion.3), channel_id=1, source_target_pairs={{0,8},{2,10},{4,12},{6,14},{8,0},{10,2},{12,4},{14,6},{1,9},{3,11}... | collective-permute-start | bytes 393224 | tf_op jit(solution)/shard_map/ppermute | solution.py:264
  59.3 0.5 collective-permute-start.24
  59.7 1.6 %collective-permute-start.22 = (bf16[64,2048]{1,0:T(8,128)(2,1)S(1)}, bf16[64,2048]{1,0:T(8,128)(2,1)S(1)}, u32[]{:S(2)}, u32[]{:S(2)}) collective-permute-start(bf16[64,2048]{1,0:T(8,128)(2,1)S(1)} %get-tuple-element.43), channel_id=1, source_target_pairs={{0,4},{2,6},{4,0},{6,2},{8,12},{10,14},{12,8},{14,10},{1,5},{3,7},... | collective-permute-start | bytes 786440 | tf_op jit(solution)/shard_map/ppermute | solution.py:264
  61.3 5.2 %collective-permute-done.19.refs_4_ = bf16[64,2048]{1,0:T(8,128)(2,1)S(1)} collective-permute-done((bf16[64,2048]{1,0:T(8,128)(2,1)S(1)}, bf16[64,2048]{1,0:T(8,128)(2,1)S(1)}, u32[]{:S(2)}, u32[]{:S(2)}) %collective-permute-start.19) | collective-permute-done | bytes 262176 | tf_op jit(solution)/shard_map/ppermute | solution.py:264
  66.6 1.8 %collective-permute-start.27 = (bf16[32,2048]{1,0:T(8,128)(2,1)S(1)}, bf16[32,2048]{1,0:T(8,128)(2,1)S(1)}, u32[]{:S(2)}, u32[]{:S(2)}) collective-permute-start(bf16[32,2048]{1,0:T(8,128)(2,1)S(1)} %add_convert_fusion.2), channel_id=1, source_target_pairs={{0,8},{2,10},{4,12},{6,14},{8,0},{10,2},{12,4},{14,6},{1,9},{3,11}... | collective-permute-start | bytes 393224 | tf_op jit(solution)/shard_map/ppermute | solution.py:264
  68.3 6.6 %collective-permute-done.24.refs_4_ = bf16[64,2048]{1,0:T(8,128)(2,1)S(1)} collective-permute-done((bf16[64,2048]{1,0:T(8,128)(2,1)S(1)}, bf16[64,2048]{1,0:T(8,128)(2,1)S(1)}, u32[]{:S(2)}, u32[]{:S(2)}) %collective-permute-start.24) | collective-permute-done | bytes 262176 | tf_op jit(solution)/shard_map/ppermute | solution.py:264
  75.0 1.8 %collective-permute-start.25 = (bf16[32,2048]{1,0:T(8,128)(2,1)S(1)}, bf16[32,2048]{1,0:T(8,128)(2,1)S(1)}, u32[]{:S(2)}, u32[]{:S(2)}) collective-permute-start(bf16[32,2048]{1,0:T(8,128)(2,1)S(1)} %add_convert_fusion), channel_id=1, source_target_pairs={{0,8},{2,10},{4,12},{6,14},{8,0},{10,2},{12,4},{14,6},{1,9},{3,11}... | collective-permute-start | bytes 393224 | tf_op jit(solution)/shard_map/ppermute | solution.py:264
  76.8 4.7 %collective-permute-done.22.refs_1_ = bf16[64,2048]{1,0:T(8,128)(2,1)S(1)} collective-permute-done((bf16[64,2048]{1,0:T(8,128)(2,1)S(1)}, bf16[64,2048]{1,0:T(8,128)(2,1)S(1)}, u32[]{:S(2)}, u32[]{:S(2)}) %collective-permute-start.22) | collective-permute-done | bytes 262176 | tf_op jit(solution)/shard_map/ppermute | solution.py:264
  81.4 0.4 collective-permute-start.20
  81.9 1.7 %collective-permute-start.23 = (bf16[32,2048]{1,0:T(8,128)(2,1)S(1)}, bf16[32,2048]{1,0:T(8,128)(2,1)S(1)}, u32[]{:S(2)}, u32[]{:S(2)}) collective-permute-start(bf16[32,2048]{1,0:T(8,128)(2,1)S(1)} %add_convert_fusion.1), channel_id=1, source_target_pairs={{0,8},{2,10},{4,12},{6,14},{8,0},{10,2},{12,4},{14,6},{1,9},{3,11}... | collective-permute-start | bytes 393224 | tf_op jit(solution)/shard_map/ppermute | solution.py:264
  83.7 0.1 compare_convert_fusion.1
  83.8 1.3 %collective-permute-done.20.low_there_ref = bf16[32,128]{1,0:T(8,128)(2,1)S(1)} collective-permute-done((bf16[32,128]{1,0:T(8,128)(2,1)S(1)}, bf16[32,128]{1,0:T(8,128)(2,1)S(1)}, u32[]{:S(2)}, u32[]{:S(2)}) %collective-permute-start.20) | collective-permute-done | bytes 8224 | tf_op jit(solution)/shard_map/ppermute | solution.py:261
  85.1 1.7 %shard_map.102 = bf16[128,4096]{1,0:T(8,128)(2,1)} custom-call(bf16[32,128]{1,0:T(8,128)(2,1)S(1)} %slice.48.low_ref, bf16[32,128]{1,0:T(8,128)(2,1)S(1)} %collective-permute-done.20.low_there_ref, f32[4,128]{1,0:T(4,128)S(1)} %get-tuple-element.56.held_ref, f32[4,128]{1,0:T(4,128)S(1)} %get-tuple-element.55.held_there_ref, ...), custom_call_target="tpu_custom_call" | custom-call | tf_op jit(solution)/shard_map/pallas_call | solution.py:240
  86.8 3.1 %collective-permute-done.25.refs_5_ = bf16[32,2048]{1,0:T(8,128)(2,1)S(1)} collective-permute-done((bf16[32,2048]{1,0:T(8,128)(2,1)S(1)}, bf16[32,2048]{1,0:T(8,128)(2,1)S(1)}, u32[]{:S(2)}, u32[]{:S(2)}) %collective-permute-start.25) | collective-permute-done | bytes 131104 | tf_op jit(solution)/shard_map/ppermute | solution.py:264
  89.9 0.9 shard_map.104
  90.8 0.7 collective-permute-done.23.refs_2_
  91.5 0.9 shard_map.103
  (41 shorter events, 0.3 us)
Async XLA Ops:
  0.6 0.7 copy-start.4
  0.6 0.7 copy-start.6
  1.3 6.6 %copy-start.2 = (bf16[1,32,4096]{2,1,0:T(8,128)(2,1)S(1)}, bf16[1,32,4096]{2,1,0:T(8,128)(2,1)}, u32[]{:S(2)}) copy-start(bf16[1,32,4096]{2,1,0:T(8,128)(2,1)} %param.12) | copy-start | bytes 786436
  1.3 6.6 %collective-permute-start = (s32[2,128]{1,0:T(2,128)S(1)}, s32[2,128]{1,0:T(2,128)S(1)}, u32[]{:S(2)}, u32[]{:S(2)}) collective-permute-start(s32[2,128]{1,0:T(2,128)S(1)} %pad_add_fusion), channel_id=1, source_target_pairs={{0,2},{2,0},{4,6},{6,4},{8,10},{10,8},{12,14},{14,12},{1,3},{3,1},... | collective-permute-start | bytes 3080 | tf_op jit(solution)/shard_map/ppermute | solution.py:261
  4.3 35.2 %collective-permute-start.15 = (bf16[128,4096]{1,0:T(8,128)(2,1)}, bf16[128,4096]{1,0:T(8,128)(2,1)S(1)}, u32[]{:S(2)}, u32[]{:S(2)}) collective-permute-start(bf16[128,4096]{1,0:T(8,128)(2,1)} %own_ref.10), channel_id=1, source_target_pairs={{0,2},{2,0},{4,6},{6,4},{8,10},{10,8},{12,14},{14,12},{1,3},{3,1},... | collective-permute-start | bytes 3145736 | tf_op jit(solution)/shard_map/ppermute | solution.py:261
  5.7 18.8 %copy-start.3 = (bf16[1,32,4096]{2,1,0:T(8,128)(2,1)S(1)}, bf16[1,32,4096]{2,1,0:T(8,128)(2,1)}, u32[]{:S(2)}) copy-start(bf16[1,32,4096]{2,1,0:T(8,128)(2,1)} %param.13) | copy-start | bytes 786436
  5.7 36.2 %collective-permute-start.14 = (bf16[128,2048]{1,0:T(8,128)(2,1)S(1)}, bf16[128,2048]{1,0:T(8,128)(2,1)S(1)}, u32[]{:S(2)}, u32[]{:S(2)}) collective-permute-start(bf16[128,2048]{1,0:T(8,128)(2,1)S(1)} %get-tuple-element.51), channel_id=1, source_target_pairs={{0,2},{2,0},{4,6},{6,4},{8,10},{10,8},{12,14},{14,12},{1,3},{3,1},... | collective-permute-start | bytes 1572872 | tf_op jit(solution)/shard_map/ppermute | solution.py:261
  8.6 6.6 %collective-permute-start.1 = (bf16[16,4096]{1,0:T(8,128)(2,1)}, bf16[16,4096]{1,0:T(8,128)(2,1)S(1)}, u32[]{:S(2)}, u32[]{:S(2)}) collective-permute-start(bf16[16,4096]{1,0:T(8,128)(2,1)} %constant_dynamic-slice_fusion.1), channel_id=1, source_target_pairs={{0,4},{2,6},{4,0},{6,2},{8,12},{10,14},{12,8},{14,10},{1,5},{3,7},... | collective-permute-start | bytes 393224 | tf_op jit(solution)/shard_map/ppermute | solution.py:264
  10.1 12.3 %collective-permute-start.3 = (bf16[16,4096]{1,0:T(8,128)(2,1)}, bf16[16,4096]{1,0:T(8,128)(2,1)S(1)}, u32[]{:S(2)}, u32[]{:S(2)}) collective-permute-start(bf16[16,4096]{1,0:T(8,128)(2,1)} %constant_dynamic-slice_fusion.1), channel_id=1, source_target_pairs={{0,8},{2,10},{4,12},{6,14},{8,0},{10,2},{12,4},{14,6},{1,9},{3,11}... | collective-permute-start | bytes 393224 | tf_op jit(solution)/shard_map/ppermute | solution.py:264
  12.7 11.2 %collective-permute-start.4 = (bf16[16,4096]{1,0:T(8,128)(2,1)}, bf16[16,4096]{1,0:T(8,128)(2,1)S(1)}, u32[]{:S(2)}, u32[]{:S(2)}) collective-permute-start(bf16[16,4096]{1,0:T(8,128)(2,1)} %constant_dynamic-slice_fusion.1), channel_id=1, source_target_pairs={{0,12},{2,14},{4,8},{6,10},{8,4},{10,6},{12,0},{14,2},{1,13},{3,15... | collective-permute-start | bytes 393224 | tf_op jit(solution)/shard_map/ppermute | solution.py:264
  15.2 9.3 %collective-permute-start.5 = (bf16[16,4096]{1,0:T(8,128)(2,1)S(1)}, bf16[16,4096]{1,0:T(8,128)(2,1)S(1)}, u32[]{:S(2)}, u32[]{:S(2)}) collective-permute-start(bf16[16,4096]{1,0:T(8,128)(2,1)S(1)} %collective-permute-done.1.refs_0_), channel_id=1, source_target_pairs={{0,16},{16,0},{1,17},{17,1},{2,18},{18,2},{3,19},{19,3},{4,20},{20... | collective-permute-start | bytes 393224 | tf_op jit(solution)/shard_map/ppermute | solution.py:267
  22.5 5.0 %collective-permute-start.6 = (bf16[16,4096]{1,0:T(8,128)(2,1)S(1)}, bf16[16,4096]{1,0:T(8,128)(2,1)S(1)}, u32[]{:S(2)}, u32[]{:S(2)}) collective-permute-start(bf16[16,4096]{1,0:T(8,128)(2,1)S(1)} %collective-permute-done.3.refs_1_), channel_id=1, source_target_pairs={{0,16},{16,0},{1,17},{17,1},{2,18},{18,2},{3,19},{19,3},{4,20},{20... | collective-permute-start | bytes 393224 | tf_op jit(solution)/shard_map/ppermute | solution.py:267
  24.0 5.9 %collective-permute-start.7 = (bf16[16,4096]{1,0:T(8,128)(2,1)S(1)}, bf16[16,4096]{1,0:T(8,128)(2,1)S(1)}, u32[]{:S(2)}, u32[]{:S(2)}) collective-permute-start(bf16[16,4096]{1,0:T(8,128)(2,1)S(1)} %collective-permute-done.4.refs_2_), channel_id=1, source_target_pairs={{0,16},{16,0},{1,17},{17,1},{2,18},{18,2},{3,19},{19,3},{4,20},{20... | collective-permute-start | bytes 393224 | tf_op jit(solution)/shard_map/ppermute | solution.py:267
  24.5 12.9 %collective-permute-start.8 = (bf16[16,4096]{1,0:T(8,128)(2,1)S(1)}, bf16[16,4096]{1,0:T(8,128)(2,1)S(1)}, u32[]{:S(2)}, u32[]{:S(2)}) collective-permute-start(bf16[16,4096]{1,0:T(8,128)(2,1)S(1)} %constant_dynamic-slice_fusion), channel_id=1, source_target_pairs={{0,8},{2,10},{4,12},{6,14},{8,0},{10,2},{12,4},{14,6},{1,9},{3,11}... | collective-permute-start | bytes 393224 | tf_op jit(solution)/shard_map/ppermute | solution.py:264
  27.4 11.2 %collective-permute-start.9 = (bf16[16,4096]{1,0:T(8,128)(2,1)S(1)}, bf16[16,4096]{1,0:T(8,128)(2,1)S(1)}, u32[]{:S(2)}, u32[]{:S(2)}) collective-permute-start(bf16[16,4096]{1,0:T(8,128)(2,1)S(1)} %constant_dynamic-slice_fusion), channel_id=1, source_target_pairs={{0,12},{2,14},{4,8},{6,10},{8,4},{10,6},{12,0},{14,2},{1,13},{3,15... | collective-permute-start | bytes 393224 | tf_op jit(solution)/shard_map/ppermute | solution.py:264
  29.9 6.9 %collective-permute-start.2 = (bf16[16,4096]{1,0:T(8,128)(2,1)S(1)}, bf16[16,4096]{1,0:T(8,128)(2,1)S(1)}, u32[]{:S(2)}, u32[]{:S(2)}) collective-permute-start(bf16[16,4096]{1,0:T(8,128)(2,1)S(1)} %constant_dynamic-slice_fusion), channel_id=1, source_target_pairs={{0,4},{2,6},{4,0},{6,2},{8,12},{10,14},{12,8},{14,10},{1,5},{3,7},... | collective-permute-start | bytes 393224 | tf_op jit(solution)/shard_map/ppermute | solution.py:264
  29.9 11.9 %copy-start.1 = (bf16[128,4096]{1,0:T(8,128)(2,1)S(1)}, bf16[128,4096]{1,0:T(8,128)(2,1)}, u32[]{:S(2)}) copy-start(bf16[128,4096]{1,0:T(8,128)(2,1)} %own_ref.10) | copy-start | bytes 3145732
  30.0 0.7 copy-start.5
  36.7 14.9 %collective-permute-start.13 = (bf16[128,2048]{1,0:T(8,128)(2,1)S(1)}, bf16[128,2048]{1,0:T(8,128)(2,1)S(1)}, u32[]{:S(2)}, u32[]{:S(2)}) collective-permute-start(bf16[128,2048]{1,0:T(8,128)(2,1)S(1)} %get-tuple-element.52), channel_id=1, source_target_pairs={{0,2},{2,0},{4,6},{6,4},{8,10},{10,8},{12,14},{14,12},{1,3},{3,1},... | collective-permute-start | bytes 1572872 | tf_op jit(solution)/shard_map/ppermute | solution.py:261
  37.5 5.2 %collective-permute-start.10 = (bf16[16,4096]{1,0:T(8,128)(2,1)S(1)}, bf16[16,4096]{1,0:T(8,128)(2,1)S(1)}, u32[]{:S(2)}, u32[]{:S(2)}) collective-permute-start(bf16[16,4096]{1,0:T(8,128)(2,1)S(1)} %collective-permute-done.2.refs_0_), channel_id=1, source_target_pairs={{0,16},{16,0},{1,17},{17,1},{2,18},{18,2},{3,19},{19,3},{4,20},{20... | collective-permute-start | bytes 393224 | tf_op jit(solution)/shard_map/ppermute | solution.py:267
  38.6 5.3 %collective-permute-start.11 = (bf16[16,4096]{1,0:T(8,128)(2,1)S(1)}, bf16[16,4096]{1,0:T(8,128)(2,1)S(1)}, u32[]{:S(2)}, u32[]{:S(2)}) collective-permute-start(bf16[16,4096]{1,0:T(8,128)(2,1)S(1)} %collective-permute-done.8.refs_1_), channel_id=1, source_target_pairs={{0,16},{16,0},{1,17},{17,1},{2,18},{18,2},{3,19},{19,3},{4,20},{20... | collective-permute-start | bytes 393224 | tf_op jit(solution)/shard_map/ppermute | solution.py:267
  39.6 5.7 %collective-permute-start.12 = (bf16[16,4096]{1,0:T(8,128)(2,1)S(1)}, bf16[16,4096]{1,0:T(8,128)(2,1)S(1)}, u32[]{:S(2)}, u32[]{:S(2)}) collective-permute-start(bf16[16,4096]{1,0:T(8,128)(2,1)S(1)} %collective-permute-done.9.refs_2_), channel_id=1, source_target_pairs={{0,16},{16,0},{1,17},{17,1},{2,18},{18,2},{3,19},{19,3},{4,20},{20... | collective-permute-start | bytes 393224 | tf_op jit(solution)/shard_map/ppermute | solution.py:267
  42.6 2.8 %collective-permute-start.16 = (f32[32,256]{1,0:T(8,128)S(1)}, f32[32,256]{1,0:T(8,128)S(1)}, u32[]{:S(2)}, u32[]{:S(2)}) collective-permute-start(f32[32,256]{1,0:T(8,128)S(1)} %shard_map.96), channel_id=1, source_target_pairs={{0,1},{1,0},{2,3},{3,2},{4,5},{5,4},{6,7},{7,6},{8,9},{9,8},{10,11... | collective-permute-start | bytes 98312 | tf_op jit(solution)/shard_map/ppermute | solution.py:270
  42.7 2.7 %copy-start = (bf16[128,4096]{1,0:T(8,128)(2,1)S(1)}, bf16[128,4096]{1,0:T(8,128)(2,1)}, u32[]{:S(2)}) copy-start(bf16[128,4096]{1,0:T(8,128)(2,1)} %own_ref.11) | copy-start | bytes 3145732
  45.8 7.5 %collective-permute-start.18 = (bf16[64,2048]{1,0:T(8,128)(2,1)S(1)}, bf16[64,2048]{1,0:T(8,128)(2,1)S(1)}, u32[]{:S(2)}, u32[]{:S(2)}) collective-permute-start(bf16[64,2048]{1,0:T(8,128)(2,1)S(1)} %get-tuple-element.34), channel_id=1, source_target_pairs={{0,4},{2,6},{4,0},{6,2},{8,12},{10,14},{12,8},{14,10},{1,5},{3,7},... | collective-permute-start | bytes 786440 | tf_op jit(solution)/shard_map/ppermute | solution.py:264
  52.1 1.3 %collective-permute-start.17 = (f32[32,256]{1,0:T(8,128)S(1)}, f32[32,256]{1,0:T(8,128)S(1)}, u32[]{:S(2)}, u32[]{:S(2)}) collective-permute-start(f32[32,256]{1,0:T(8,128)S(1)} %shard_map.99), channel_id=1, source_target_pairs={{0,1},{1,0},{2,3},{3,2},{4,5},{5,4},{6,7},{7,6},{8,9},{9,8},{10,11... | collective-permute-start | bytes 98312 | tf_op jit(solution)/shard_map/ppermute | solution.py:270
  54.5 12.0 %collective-permute-start.19 = (bf16[64,2048]{1,0:T(8,128)(2,1)S(1)}, bf16[64,2048]{1,0:T(8,128)(2,1)S(1)}, u32[]{:S(2)}, u32[]{:S(2)}) collective-permute-start(bf16[64,2048]{1,0:T(8,128)(2,1)S(1)} %get-tuple-element.39), channel_id=1, source_target_pairs={{0,4},{2,6},{4,0},{6,2},{8,12},{10,14},{12,8},{14,10},{1,5},{3,7},... | collective-permute-start | bytes 786440 | tf_op jit(solution)/shard_map/ppermute | solution.py:264
  56.2 25.8 %collective-permute-start.21 = (bf16[128,4096]{1,0:T(8,128)(2,1)S(1)}, bf16[128,4096]{1,0:T(8,128)(2,1)S(1)}, u32[]{:S(2)}, u32[]{:S(2)}) collective-permute-start(bf16[128,4096]{1,0:T(8,128)(2,1)S(1)} %shard_map.94.adapter_ref.down_ref), channel_id=1, source_target_pairs={{0,2},{2,0},{4,6},{6,4},{8,10},{10,8},{12,14},{14,12},{1,3},{3,1},... | collective-permute-start | bytes 3145736 | tf_op jit(solution)/shard_map/ppermute | solution.py:261
  56.7 33.2 %collective-permute-start.26 = (bf16[32,2048]{1,0:T(8,128)(2,1)S(1)}, bf16[32,2048]{1,0:T(8,128)(2,1)S(1)}, u32[]{:S(2)}, u32[]{:S(2)}) collective-permute-start(bf16[32,2048]{1,0:T(8,128)(2,1)S(1)} %add_convert_fusion.3), channel_id=1, source_target_pairs={{0,8},{2,10},{4,12},{6,14},{8,0},{10,2},{12,4},{14,6},{1,9},{3,11}... | collective-permute-start | bytes 393224 | tf_op jit(solution)/shard_map/ppermute | solution.py:264
  59.3 15.7 %collective-permute-start.24 = (bf16[64,2048]{1,0:T(8,128)(2,1)S(1)}, bf16[64,2048]{1,0:T(8,128)(2,1)S(1)}, u32[]{:S(2)}, u32[]{:S(2)}) collective-permute-start(bf16[64,2048]{1,0:T(8,128)(2,1)S(1)} %get-tuple-element.45), channel_id=1, source_target_pairs={{0,4},{2,6},{4,0},{6,2},{8,12},{10,14},{12,8},{14,10},{1,5},{3,7},... | collective-permute-start | bytes 786440 | tf_op jit(solution)/shard_map/ppermute | solution.py:264
  59.7 21.7 %collective-permute-start.22 = (bf16[64,2048]{1,0:T(8,128)(2,1)S(1)}, bf16[64,2048]{1,0:T(8,128)(2,1)S(1)}, u32[]{:S(2)}, u32[]{:S(2)}) collective-permute-start(bf16[64,2048]{1,0:T(8,128)(2,1)S(1)} %get-tuple-element.43), channel_id=1, source_target_pairs={{0,4},{2,6},{4,0},{6,2},{8,12},{10,14},{12,8},{14,10},{1,5},{3,7},... | collective-permute-start | bytes 786440 | tf_op jit(solution)/shard_map/ppermute | solution.py:264
  66.6 23.3 %collective-permute-start.27 = (bf16[32,2048]{1,0:T(8,128)(2,1)S(1)}, bf16[32,2048]{1,0:T(8,128)(2,1)S(1)}, u32[]{:S(2)}, u32[]{:S(2)}) collective-permute-start(bf16[32,2048]{1,0:T(8,128)(2,1)S(1)} %add_convert_fusion.2), channel_id=1, source_target_pairs={{0,8},{2,10},{4,12},{6,14},{8,0},{10,2},{12,4},{14,6},{1,9},{3,11}... | collective-permute-start | bytes 393224 | tf_op jit(solution)/shard_map/ppermute | solution.py:264
  75.0 14.9 %collective-permute-start.25 = (bf16[32,2048]{1,0:T(8,128)(2,1)S(1)}, bf16[32,2048]{1,0:T(8,128)(2,1)S(1)}, u32[]{:S(2)}, u32[]{:S(2)}) collective-permute-start(bf16[32,2048]{1,0:T(8,128)(2,1)S(1)} %add_convert_fusion), channel_id=1, source_target_pairs={{0,8},{2,10},{4,12},{6,14},{8,0},{10,2},{12,4},{14,6},{1,9},{3,11}... | collective-permute-start | bytes 393224 | tf_op jit(solution)/shard_map/ppermute | solution.py:264
  81.4 3.7 %collective-permute-start.20 = (bf16[32,128]{1,0:T(8,128)(2,1)S(1)}, bf16[32,128]{1,0:T(8,128)(2,1)S(1)}, u32[]{:S(2)}, u32[]{:S(2)}) collective-permute-start(bf16[32,128]{1,0:T(8,128)(2,1)S(1)} %slice.51), channel_id=1, source_target_pairs={{0,2},{2,0},{4,6},{6,4},{8,10},{10,8},{12,14},{14,12},{1,3},{3,1},... | collective-permute-start | bytes 24584 | tf_op jit(solution)/shard_map/ppermute | solution.py:261
  81.9 9.6 %collective-permute-start.23 = (bf16[32,2048]{1,0:T(8,128)(2,1)S(1)}, bf16[32,2048]{1,0:T(8,128)(2,1)S(1)}, u32[]{:S(2)}, u32[]{:S(2)}) collective-permute-start(bf16[32,2048]{1,0:T(8,128)(2,1)S(1)} %add_convert_fusion.1), channel_id=1, source_target_pairs={{0,8},{2,10},{4,12},{6,14},{8,0},{10,2},{12,4},{14,6},{1,9},{3,11}... | collective-permute-start | bytes 393224 | tf_op jit(solution)/shard_map/ppermute | solution.py:264

commit v5 on v4

--- a/solution.py
+++ b/solution.py
@@ -285,7 +285,7 @@
     down = join(layer_of, down_own, down_got, [swap_layer(got) for got in down_got])
     up_own = after(adapter_up[0], down_got[0])
     up_got = fetch(up_own)
-    up_halves = [after(up_got[0], down)] + up_got[1:]
+    up_halves = up_got
     up = join(layer_of, up_own, up_halves, [swap_layer(got) for got in up_halves])
     ids_there = after(ids_there, down)
     other_g = [swap_side(cut) for cut in own_g]
@@ -307,7 +307,7 @@
         return (kept[rank:] + came[rank:].astype(jnp.float32)).astype(jnp.bfloat16)
 
     nothing = jnp.zeros((rank, 2 * rows), jnp.float32)
-    x_in = after(after(other_x, *up_got), other_g[0])
+    x_in = after(other_x, *up_got)
     scaled_h = combine(project(down, features, x_in, held, nothing, 0))
 
     first_g = after(other_g[0], up)
@@ -329,8 +329,8 @@
     ]
     onward = second_block(kept, after(came, outs[0]))
     up_groups.append((kept, came, hop(onward, 2)))
-    back = swap_side(after(scaled_u, onward)[:, rows:])
-    down_there = swap_side(after(down, other_g[1]))
+    back = swap_side(after(scaled_u, down_came[0])[:, rows:])
+    down_there = swap_side(down)
     up_adapter_gradient = add_parts(up_groups, rank, width)
     input_grad = input_gradient(scaled_u[:, :rows], back, own_held, own_there, down, down_there)
     kept, came, last = down_groups[-1]

time: 92.6 us -> 92.6 us (level)
    ppermute x6, waiting for transfers between devices: 3.02 us -> 6.73 us  [swap_layer(): return lax.ppermute(value, 'parts', [(0, 1), (1, 0)])]
    ppermute x6, waiting for transfers between devices: 7.21 us -> 4.73 us  [swap_side(): return lax.ppermute(value, 'dp', [(i, i ^ 1) for i in range(ranks)])]
    ppermute x14, waiting for transfers between devices: 34.2 us -> 32.7 us  [hop(): return lax.ppermute(value, 'dp', [(i, i ^ 2 * by) for i in range(ranks)])]
  transfers between devices with their start and end apart: 28 -> 28, of which waited for: 15 -> 16; matrix products, arithmetic and copies ran while one was open for 3% -> 3% of each run, Pallas kernels for 5% -> 5%
where the time goes in v5:
time: 92.6 us; the launch traced here: 92.4 us
  waiting for transfers between devices  45.3 us (49%)
  starting transfers between devices  35.4 us (38%)
  Pallas kernels  6.72 us (7%)
  local copies, waits for them, and re-layouts  3.36 us (4%)
    ppermute x14, waiting for transfers between devices, hop(): return lax.ppermute(value, 'dp', [(i, i ^ 2 * by) for i in range(ranks)])  32.7 us
    ppermute x14, starting transfers between devices, hop(): return lax.ppermute(value, 'dp', [(i, i ^ 2 * by) for i in range(ranks)])  22.1 us
    ppermute x6, waiting for transfers between devices, swap_layer(): return lax.ppermute(value, 'parts', [(0, 1), (1, 0)])  6.73 us
    ppermute x6, starting transfers between devices, swap_side(): return lax.ppermute(value, 'dp', [(i, i ^ 1) for i in range(ranks)])  6.71 us
    ppermute x6, starting transfers between devices, swap_layer(): return lax.ppermute(value, 'parts', [(0, 1), (1, 0)])  6.46 us
    ppermute x6, waiting for transfers between devices, swap_side(): return lax.ppermute(value, 'dp', [(i, i ^ 1) for i in range(ranks)])  4.73 us
  transfers between devices with their start and end apart: 28, of which 16 were waited for; matrix products, arithmetic and copies ran while one was open for 3% of the time, Pallas kernels for 5%

profile of v5, /device:TPU:0, one launch (start us, length us, event | category | flops | bytes accessed | tf_op | source)
XLA Modules:
  0.0 92.4 jit_solution(9326523839987472729)
XLA Ops:
  0.7 0.6 copy-done.4
  1.3 0.0 copy-done.6
  1.3 3.0 %collective-permute-start = (s32[2,128]{1,0:T(2,128)S(1)}, s32[2,128]{1,0:T(2,128)S(1)}, u32[]{:S(2)}, u32[]{:S(2)}) collective-permute-start(s32[2,128]{1,0:T(2,128)S(1)} %pad_add_fusion), channel_id=1, source_target_pairs={{0,2},{2,0},{4,6},{6,4},{8,10},{10,8},{12,14},{14,12},{1,3},{3,1},... | collective-permute-start | bytes 3080 | tf_op jit(solution)/shard_map/ppermute | solution.py:261
  4.3 0.1 collective-permute-start.15
  4.4 1.3 %fusion = (bf16[128,2048]{1,0:T(8,128)(2,1)S(1)}, bf16[128,2048]{1,0:T(8,128)(2,1)S(1)}) fusion(bf16[128,4096]{1,0:T(8,128)(2,1)} %own_ref.11), kind=kLoop, calls=%fused_computation.26 | loop fusion | bytes 2097152 | tf_op jit(solution)/shard_map/slice | solution.py:283
  5.7 2.0 %collective-permute-start.14 = (bf16[128,2048]{1,0:T(8,128)(2,1)S(1)}, bf16[128,2048]{1,0:T(8,128)(2,1)S(1)}, u32[]{:S(2)}, u32[]{:S(2)}) collective-permute-start(bf16[128,2048]{1,0:T(8,128)(2,1)S(1)} %get-tuple-element.45), channel_id=1, source_target_pairs={{0,2},{2,0},{4,6},{6,4},{8,10},{10,8},{12,14},{14,12},{1,3},{3,1},... | collective-permute-start | bytes 1572872 | tf_op jit(solution)/shard_map/ppermute | solution.py:261
  7.7 0.2 convert_reduce_fusion.1
  7.9 0.7 constant_dynamic-slice_fusion.1
  8.6 1.6 %collective-permute-start.1 = (bf16[16,4096]{1,0:T(8,128)(2,1)}, bf16[16,4096]{1,0:T(8,128)(2,1)S(1)}, u32[]{:S(2)}, u32[]{:S(2)}) collective-permute-start(bf16[16,4096]{1,0:T(8,128)(2,1)} %constant_dynamic-slice_fusion.1), channel_id=1, source_target_pairs={{0,4},{2,6},{4,0},{6,2},{8,12},{10,14},{12,8},{14,10},{1,5},{3,7},... | collective-permute-start | bytes 393224 | tf_op jit(solution)/shard_map/ppermute | solution.py:264
  10.1 2.6 %collective-permute-start.9 = (bf16[16,4096]{1,0:T(8,128)(2,1)}, bf16[16,4096]{1,0:T(8,128)(2,1)S(1)}, u32[]{:S(2)}, u32[]{:S(2)}) collective-permute-start(bf16[16,4096]{1,0:T(8,128)(2,1)} %constant_dynamic-slice_fusion.1), channel_id=1, source_target_pairs={{0,8},{2,10},{4,12},{6,14},{8,0},{10,2},{12,4},{14,6},{1,9},{3,11}... | collective-permute-start | bytes 393224 | tf_op jit(solution)/shard_map/ppermute | solution.py:264
  12.7 0.2 collective-permute-start.10
  13.0 2.2 %collective-permute-done.1.refs_0_ = bf16[16,4096]{1,0:T(8,128)(2,1)S(1)} collective-permute-done((bf16[16,4096]{1,0:T(8,128)(2,1)}, bf16[16,4096]{1,0:T(8,128)(2,1)S(1)}, u32[]{:S(2)}, u32[]{:S(2)}) %collective-permute-start.1) | collective-permute-done | bytes 131104 | tf_op jit(solution)/shard_map/ppermute | solution.py:264
  15.2 1.5 %collective-permute-start.11 = (bf16[16,4096]{1,0:T(8,128)(2,1)S(1)}, bf16[16,4096]{1,0:T(8,128)(2,1)S(1)}, u32[]{:S(2)}, u32[]{:S(2)}) collective-permute-start(bf16[16,4096]{1,0:T(8,128)(2,1)S(1)} %collective-permute-done.1.refs_0_), channel_id=1, source_target_pairs={{0,16},{16,0},{1,17},{17,1},{2,18},{18,2},{3,19},{19,3},{4,20},{20... | collective-permute-start | bytes 393224 | tf_op jit(solution)/shard_map/ppermute | solution.py:267
  16.7 5.7 %collective-permute-done.9.refs_1_ = bf16[16,4096]{1,0:T(8,128)(2,1)S(1)} collective-permute-done((bf16[16,4096]{1,0:T(8,128)(2,1)}, bf16[16,4096]{1,0:T(8,128)(2,1)S(1)}, u32[]{:S(2)}, u32[]{:S(2)}) %collective-permute-start.9) | collective-permute-done | bytes 131104 | tf_op jit(solution)/shard_map/ppermute | solution.py:264
  22.5 1.5 %collective-permute-start.12 = (bf16[16,4096]{1,0:T(8,128)(2,1)S(1)}, bf16[16,4096]{1,0:T(8,128)(2,1)S(1)}, u32[]{:S(2)}, u32[]{:S(2)}) collective-permute-start(bf16[16,4096]{1,0:T(8,128)(2,1)S(1)} %collective-permute-done.9.refs_1_), channel_id=1, source_target_pairs={{0,16},{16,0},{1,17},{17,1},{2,18},{18,2},{3,19},{19,3},{4,20},{20... | collective-permute-start | bytes 393224 | tf_op jit(solution)/shard_map/ppermute | solution.py:267
  24.0 0.5 collective-permute-start.13
  24.5 1.5 %collective-permute-start.2 = (bf16[16,4096]{1,0:T(8,128)(2,1)S(1)}, bf16[16,4096]{1,0:T(8,128)(2,1)S(1)}, u32[]{:S(2)}, u32[]{:S(2)}) collective-permute-start(bf16[16,4096]{1,0:T(8,128)(2,1)S(1)} %constant_dynamic-slice_fusion), channel_id=1, source_target_pairs={{0,4},{2,6},{4,0},{6,2},{8,12},{10,14},{12,8},{14,10},{1,5},{3,7},... | collective-permute-start | bytes 393224 | tf_op jit(solution)/shard_map/ppermute | solution.py:264
  26.0 1.4 %collective-permute-done.12.refs_4_ = bf16[16,4096]{1,0:T(8,128)(2,1)S(1)} collective-permute-done((bf16[16,4096]{1,0:T(8,128)(2,1)S(1)}, bf16[16,4096]{1,0:T(8,128)(2,1)S(1)}, u32[]{:S(2)}, u32[]{:S(2)}) %collective-permute-start.12) | collective-permute-done | bytes 131104 | tf_op jit(solution)/shard_map/ppermute | solution.py:267
  27.4 0.3 collective-permute-start.3
  27.7 1.2 %collective-permute-done.13.refs_5_ = bf16[16,4096]{1,0:T(8,128)(2,1)S(1)} collective-permute-done((bf16[16,4096]{1,0:T(8,128)(2,1)S(1)}, bf16[16,4096]{1,0:T(8,128)(2,1)S(1)}, u32[]{:S(2)}, u32[]{:S(2)}) %collective-permute-start.13) | collective-permute-done | bytes 131104 | tf_op jit(solution)/shard_map/ppermute | solution.py:267
  28.9 2.5 %collective-permute-start.4 = (bf16[16,4096]{1,0:T(8,128)(2,1)S(1)}, bf16[16,4096]{1,0:T(8,128)(2,1)S(1)}, u32[]{:S(2)}, u32[]{:S(2)}) collective-permute-start(bf16[16,4096]{1,0:T(8,128)(2,1)S(1)} %constant_dynamic-slice_fusion), channel_id=1, source_target_pairs={{0,12},{2,14},{4,8},{6,10},{8,4},{10,6},{12,0},{14,2},{1,13},{3,15... | collective-permute-start | bytes 393224 | tf_op jit(solution)/shard_map/ppermute | solution.py:264
  31.4 0.1 shard_map.95.adapter_ref.down_ref
  31.5 0.7 copy-done.5
  32.2 0.1 select_reduce_fusion.1
  32.3 0.1 compare_convert_fusion.held_ref
  32.4 0.2 convert_reduce_fusion
  32.6 0.6 collective-permute-start.8
  33.2 4.3 %collective-permute-done.3.refs_1_ = bf16[16,4096]{1,0:T(8,128)(2,1)S(1)} collective-permute-done((bf16[16,4096]{1,0:T(8,128)(2,1)S(1)}, bf16[16,4096]{1,0:T(8,128)(2,1)S(1)}, u32[]{:S(2)}, u32[]{:S(2)}) %collective-permute-start.3) | collective-permute-done | bytes 131104 | tf_op jit(solution)/shard_map/ppermute | solution.py:264
  37.5 0.9 collective-permute-start.5
  38.4 1.1 %collective-permute-start.6 = (bf16[16,4096]{1,0:T(8,128)(2,1)S(1)}, bf16[16,4096]{1,0:T(8,128)(2,1)S(1)}, u32[]{:S(2)}, u32[]{:S(2)}) collective-permute-start(bf16[16,4096]{1,0:T(8,128)(2,1)S(1)} %collective-permute-done.3.refs_1_), channel_id=1, source_target_pairs={{0,16},{16,0},{1,17},{17,1},{2,18},{18,2},{3,19},{19,3},{4,20},{20... | collective-permute-start | bytes 393224 | tf_op jit(solution)/shard_map/ppermute | solution.py:267
  39.5 0.9 collective-permute-start.7
  40.4 0.7 shard_map.96
  41.1 1.3 %collective-permute-done.5.refs_3_ = bf16[16,4096]{1,0:T(8,128)(2,1)S(1)} collective-permute-done((bf16[16,4096]{1,0:T(8,128)(2,1)S(1)}, bf16[16,4096]{1,0:T(8,128)(2,1)S(1)}, u32[]{:S(2)}, u32[]{:S(2)}) %collective-permute-start.5) | collective-permute-done | bytes 131104 | tf_op jit(solution)/shard_map/ppermute | solution.py:267
  42.5 1.4 %collective-permute-done.6.refs_4_ = bf16[16,4096]{1,0:T(8,128)(2,1)S(1)} collective-permute-done((bf16[16,4096]{1,0:T(8,128)(2,1)S(1)}, bf16[16,4096]{1,0:T(8,128)(2,1)S(1)}, u32[]{:S(2)}, u32[]{:S(2)}) %collective-permute-start.6) | collective-permute-done | bytes 131104 | tf_op jit(solution)/shard_map/ppermute | solution.py:267
  43.9 1.4 %collective-permute-done.7.refs_5_ = bf16[16,4096]{1,0:T(8,128)(2,1)S(1)} collective-permute-done((bf16[16,4096]{1,0:T(8,128)(2,1)S(1)}, bf16[16,4096]{1,0:T(8,128)(2,1)S(1)}, u32[]{:S(2)}, u32[]{:S(2)}) %collective-permute-start.7) | collective-permute-done | bytes 131104 | tf_op jit(solution)/shard_map/ppermute | solution.py:267
  45.3 0.1 shard_map.94.adapter_ref
  45.4 0.4 shard_map.97
  45.8 2.0 %collective-permute-start.18 = (bf16[64,2048]{1,0:T(8,128)(2,1)S(1)}, bf16[64,2048]{1,0:T(8,128)(2,1)S(1)}, u32[]{:S(2)}, u32[]{:S(2)}) collective-permute-start(bf16[64,2048]{1,0:T(8,128)(2,1)S(1)} %get-tuple-element.29), channel_id=1, source_target_pairs={{0,4},{2,6},{4,0},{6,2},{8,12},{10,14},{12,8},{14,10},{1,5},{3,7},... | collective-permute-start | bytes 786440 | tf_op jit(solution)/shard_map/ppermute | solution.py:264
  47.8 0.4 shard_map.98.base_ref
  48.2 3.4 %collective-permute-done.8.other_ref = bf16[128,2048]{1,0:T(8,128)(2,1)S(1)} collective-permute-done((bf16[128,2048]{1,0:T(8,128)(2,1)S(1)}, bf16[128,2048]{1,0:T(8,128)(2,1)S(1)}, u32[]{:S(2)}, u32[]{:S(2)}) %collective-permute-start.8) | collective-permute-done | bytes 524320 | tf_op jit(solution)/shard_map/ppermute | solution.py:261
  51.6 0.4 shard_map.99
  52.1 0.1 collective-permute-start.17
  52.1 1.2 %collective-permute-done.17 = f32[32,256]{1,0:T(8,128)S(1)} collective-permute-done((f32[32,256]{1,0:T(8,128)S(1)}, f32[32,256]{1,0:T(8,128)S(1)}, u32[]{:S(2)}, u32[]{:S(2)}) %collective-permute-start.17) | collective-permute-done | bytes 32800 | tf_op jit(solution)/shard_map/ppermute | solution.py:270
  53.4 0.7 shard_map.100
  54.1 0.4 shard_map.103
  54.5 1.6 %collective-permute-start.26 = (bf16[64,2048]{1,0:T(8,128)(2,1)S(1)}, bf16[64,2048]{1,0:T(8,128)(2,1)S(1)}, u32[]{:S(2)}, u32[]{:S(2)}) collective-permute-start(bf16[64,2048]{1,0:T(8,128)(2,1)S(1)} %get-tuple-element.39), channel_id=1, source_target_pairs={{0,4},{2,6},{4,0},{6,2},{8,12},{10,14},{12,8},{14,10},{1,5},{3,7},... | collective-permute-start | bytes 786440 | tf_op jit(solution)/shard_map/ppermute | solution.py:264
  56.2 0.5 collective-permute-start.21
  56.7 2.6 %collective-permute-start.25 = (bf16[32,2048]{1,0:T(8,128)(2,1)S(1)}, bf16[32,2048]{1,0:T(8,128)(2,1)S(1)}, u32[]{:S(2)}, u32[]{:S(2)}) collective-permute-start(bf16[32,2048]{1,0:T(8,128)(2,1)S(1)} %add_convert_fusion.3), channel_id=1, source_target_pairs={{0,8},{2,10},{4,12},{6,14},{8,0},{10,2},{12,4},{14,6},{1,9},{3,11}... | collective-permute-start | bytes 393224 | tf_op jit(solution)/shard_map/ppermute | solution.py:264
  59.3 0.5 collective-permute-start.23
  59.7 1.6 %collective-permute-start.19 = (bf16[64,2048]{1,0:T(8,128)(2,1)S(1)}, bf16[64,2048]{1,0:T(8,128)(2,1)S(1)}, u32[]{:S(2)}, u32[]{:S(2)}) collective-permute-start(bf16[64,2048]{1,0:T(8,128)(2,1)S(1)} %get-tuple-element.31), channel_id=1, source_target_pairs={{0,4},{2,6},{4,0},{6,2},{8,12},{10,14},{12,8},{14,10},{1,5},{3,7},... | collective-permute-start | bytes 786440 | tf_op jit(solution)/shard_map/ppermute | solution.py:264
  61.3 5.2 %collective-permute-done.26.refs_4_ = bf16[64,2048]{1,0:T(8,128)(2,1)S(1)} collective-permute-done((bf16[64,2048]{1,0:T(8,128)(2,1)S(1)}, bf16[64,2048]{1,0:T(8,128)(2,1)S(1)}, u32[]{:S(2)}, u32[]{:S(2)}) %collective-permute-start.26) | collective-permute-done | bytes 262176 | tf_op jit(solution)/shard_map/ppermute | solution.py:264
  66.6 1.8 %collective-permute-start.27 = (bf16[32,2048]{1,0:T(8,128)(2,1)S(1)}, bf16[32,2048]{1,0:T(8,128)(2,1)S(1)}, u32[]{:S(2)}, u32[]{:S(2)}) collective-permute-start(bf16[32,2048]{1,0:T(8,128)(2,1)S(1)} %add_convert_fusion), channel_id=1, source_target_pairs={{0,8},{2,10},{4,12},{6,14},{8,0},{10,2},{12,4},{14,6},{1,9},{3,11}... | collective-permute-start | bytes 393224 | tf_op jit(solution)/shard_map/ppermute | solution.py:264
  68.3 6.6 %collective-permute-done.23.refs_4_ = bf16[64,2048]{1,0:T(8,128)(2,1)S(1)} collective-permute-done((bf16[64,2048]{1,0:T(8,128)(2,1)S(1)}, bf16[64,2048]{1,0:T(8,128)(2,1)S(1)}, u32[]{:S(2)}, u32[]{:S(2)}) %collective-permute-start.23) | collective-permute-done | bytes 262176 | tf_op jit(solution)/shard_map/ppermute | solution.py:264
  75.0 1.8 %collective-permute-start.24 = (bf16[32,2048]{1,0:T(8,128)(2,1)S(1)}, bf16[32,2048]{1,0:T(8,128)(2,1)S(1)}, u32[]{:S(2)}, u32[]{:S(2)}) collective-permute-start(bf16[32,2048]{1,0:T(8,128)(2,1)S(1)} %add_convert_fusion.1), channel_id=1, source_target_pairs={{0,8},{2,10},{4,12},{6,14},{8,0},{10,2},{12,4},{14,6},{1,9},{3,11}... | collective-permute-start | bytes 393224 | tf_op jit(solution)/shard_map/ppermute | solution.py:264
  76.8 4.7 %collective-permute-done.19.refs_1_ = bf16[64,2048]{1,0:T(8,128)(2,1)S(1)} collective-permute-done((bf16[64,2048]{1,0:T(8,128)(2,1)S(1)}, bf16[64,2048]{1,0:T(8,128)(2,1)S(1)}, u32[]{:S(2)}, u32[]{:S(2)}) %collective-permute-start.19) | collective-permute-done | bytes 262176 | tf_op jit(solution)/shard_map/ppermute | solution.py:264
  81.4 0.5 collective-permute-start.20
  82.0 1.7 %collective-permute-start.22 = (bf16[32,2048]{1,0:T(8,128)(2,1)S(1)}, bf16[32,2048]{1,0:T(8,128)(2,1)S(1)}, u32[]{:S(2)}, u32[]{:S(2)}) collective-permute-start(bf16[32,2048]{1,0:T(8,128)(2,1)S(1)} %add_convert_fusion.2), channel_id=1, source_target_pairs={{0,8},{2,10},{4,12},{6,14},{8,0},{10,2},{12,4},{14,6},{1,9},{3,11}... | collective-permute-start | bytes 393224 | tf_op jit(solution)/shard_map/ppermute | solution.py:264
  83.7 0.1 compare_convert_fusion.1
  83.8 1.3 %collective-permute-done.20.low_there_ref = bf16[32,128]{1,0:T(8,128)(2,1)S(1)} collective-permute-done((bf16[32,128]{1,0:T(8,128)(2,1)S(1)}, bf16[32,128]{1,0:T(8,128)(2,1)S(1)}, u32[]{:S(2)}, u32[]{:S(2)}) %collective-permute-start.20) | collective-permute-done | bytes 8224 | tf_op jit(solution)/shard_map/ppermute | solution.py:261
  85.1 1.7 %shard_map.101 = bf16[128,4096]{1,0:T(8,128)(2,1)} custom-call(bf16[32,128]{1,0:T(8,128)(2,1)S(1)} %slice.48.low_ref, bf16[32,128]{1,0:T(8,128)(2,1)S(1)} %collective-permute-done.20.low_there_ref, f32[4,128]{1,0:T(4,128)S(1)} %get-tuple-element.50.held_ref, f32[4,128]{1,0:T(4,128)S(1)} %get-tuple-element.49.held_there_ref, ...), custom_call_target="tpu_custom_call" | custom-call | tf_op jit(solution)/shard_map/pallas_call | solution.py:240
  86.8 3.1 %collective-permute-done.24.refs_5_ = bf16[32,2048]{1,0:T(8,128)(2,1)S(1)} collective-permute-done((bf16[32,2048]{1,0:T(8,128)(2,1)S(1)}, bf16[32,2048]{1,0:T(8,128)(2,1)S(1)}, u32[]{:S(2)}, u32[]{:S(2)}) %collective-permute-start.24) | collective-permute-done | bytes 131104 | tf_op jit(solution)/shard_map/ppermute | solution.py:264
  89.9 0.9 shard_map.104
  90.8 0.7 collective-permute-done.22.refs_2_
  91.5 0.9 shard_map.102
  (41 shorter events, 0.3 us)
Async XLA Ops:
  0.6 0.7 copy-start.4
  0.6 0.7 copy-start.6
  1.3 6.6 %copy-start.2 = (bf16[1,32,4096]{2,1,0:T(8,128)(2,1)S(1)}, bf16[1,32,4096]{2,1,0:T(8,128)(2,1)}, u32[]{:S(2)}) copy-start(bf16[1,32,4096]{2,1,0:T(8,128)(2,1)} %param.12) | copy-start | bytes 786436
  1.3 6.6 %collective-permute-start = (s32[2,128]{1,0:T(2,128)S(1)}, s32[2,128]{1,0:T(2,128)S(1)}, u32[]{:S(2)}, u32[]{:S(2)}) collective-permute-start(s32[2,128]{1,0:T(2,128)S(1)} %pad_add_fusion), channel_id=1, source_target_pairs={{0,2},{2,0},{4,6},{6,4},{8,10},{10,8},{12,14},{14,12},{1,3},{3,1},... | collective-permute-start | bytes 3080 | tf_op jit(solution)/shard_map/ppermute | solution.py:261
  4.3 35.2 %collective-permute-start.15 = (bf16[128,4096]{1,0:T(8,128)(2,1)}, bf16[128,4096]{1,0:T(8,128)(2,1)S(1)}, u32[]{:S(2)}, u32[]{:S(2)}) collective-permute-start(bf16[128,4096]{1,0:T(8,128)(2,1)} %own_ref.10), channel_id=1, source_target_pairs={{0,2},{2,0},{4,6},{6,4},{8,10},{10,8},{12,14},{14,12},{1,3},{3,1},... | collective-permute-start | bytes 3145736 | tf_op jit(solution)/shard_map/ppermute | solution.py:261
  5.7 18.8 %copy-start.3 = (bf16[1,32,4096]{2,1,0:T(8,128)(2,1)S(1)}, bf16[1,32,4096]{2,1,0:T(8,128)(2,1)}, u32[]{:S(2)}) copy-start(bf16[1,32,4096]{2,1,0:T(8,128)(2,1)} %param.13) | copy-start | bytes 786436
  5.7 39.7 %collective-permute-start.14 = (bf16[128,2048]{1,0:T(8,128)(2,1)S(1)}, bf16[128,2048]{1,0:T(8,128)(2,1)S(1)}, u32[]{:S(2)}, u32[]{:S(2)}) collective-permute-start(bf16[128,2048]{1,0:T(8,128)(2,1)S(1)} %get-tuple-element.45), channel_id=1, source_target_pairs={{0,2},{2,0},{4,6},{6,4},{8,10},{10,8},{12,14},{14,12},{1,3},{3,1},... | collective-permute-start | bytes 1572872 | tf_op jit(solution)/shard_map/ppermute | solution.py:261
  8.6 6.6 %collective-permute-start.1 = (bf16[16,4096]{1,0:T(8,128)(2,1)}, bf16[16,4096]{1,0:T(8,128)(2,1)S(1)}, u32[]{:S(2)}, u32[]{:S(2)}) collective-permute-start(bf16[16,4096]{1,0:T(8,128)(2,1)} %constant_dynamic-slice_fusion.1), channel_id=1, source_target_pairs={{0,4},{2,6},{4,0},{6,2},{8,12},{10,14},{12,8},{14,10},{1,5},{3,7},... | collective-permute-start | bytes 393224 | tf_op jit(solution)/shard_map/ppermute | solution.py:264
  10.1 12.3 %collective-permute-start.9 = (bf16[16,4096]{1,0:T(8,128)(2,1)}, bf16[16,4096]{1,0:T(8,128)(2,1)S(1)}, u32[]{:S(2)}, u32[]{:S(2)}) collective-permute-start(bf16[16,4096]{1,0:T(8,128)(2,1)} %constant_dynamic-slice_fusion.1), channel_id=1, source_target_pairs={{0,8},{2,10},{4,12},{6,14},{8,0},{10,2},{12,4},{14,6},{1,9},{3,11}... | collective-permute-start | bytes 393224 | tf_op jit(solution)/shard_map/ppermute | solution.py:264
  12.7 11.2 %collective-permute-start.10 = (bf16[16,4096]{1,0:T(8,128)(2,1)}, bf16[16,4096]{1,0:T(8,128)(2,1)S(1)}, u32[]{:S(2)}, u32[]{:S(2)}) collective-permute-start(bf16[16,4096]{1,0:T(8,128)(2,1)} %constant_dynamic-slice_fusion.1), channel_id=1, source_target_pairs={{0,12},{2,14},{4,8},{6,10},{8,4},{10,6},{12,0},{14,2},{1,13},{3,15... | collective-permute-start | bytes 393224 | tf_op jit(solution)/shard_map/ppermute | solution.py:264
  15.2 9.3 %collective-permute-start.11 = (bf16[16,4096]{1,0:T(8,128)(2,1)S(1)}, bf16[16,4096]{1,0:T(8,128)(2,1)S(1)}, u32[]{:S(2)}, u32[]{:S(2)}) collective-permute-start(bf16[16,4096]{1,0:T(8,128)(2,1)S(1)} %collective-permute-done.1.refs_0_), channel_id=1, source_target_pairs={{0,16},{16,0},{1,17},{17,1},{2,18},{18,2},{3,19},{19,3},{4,20},{20... | collective-permute-start | bytes 393224 | tf_op jit(solution)/shard_map/ppermute | solution.py:267
  22.5 5.0 %collective-permute-start.12 = (bf16[16,4096]{1,0:T(8,128)(2,1)S(1)}, bf16[16,4096]{1,0:T(8,128)(2,1)S(1)}, u32[]{:S(2)}, u32[]{:S(2)}) collective-permute-start(bf16[16,4096]{1,0:T(8,128)(2,1)S(1)} %collective-permute-done.9.refs_1_), channel_id=1, source_target_pairs={{0,16},{16,0},{1,17},{17,1},{2,18},{18,2},{3,19},{19,3},{4,20},{20... | collective-permute-start | bytes 393224 | tf_op jit(solution)/shard_map/ppermute | solution.py:267
  24.0 5.0 %collective-permute-start.13 = (bf16[16,4096]{1,0:T(8,128)(2,1)S(1)}, bf16[16,4096]{1,0:T(8,128)(2,1)S(1)}, u32[]{:S(2)}, u32[]{:S(2)}) collective-permute-start(bf16[16,4096]{1,0:T(8,128)(2,1)S(1)} %collective-permute-done.10.refs_2_), channel_id=1, source_target_pairs={{0,16},{16,0},{1,17},{17,1},{2,18},{18,2},{3,19},{19,3},{4,20},{20... | collective-permute-start | bytes 393224 | tf_op jit(solution)/shard_map/ppermute | solution.py:267
  24.5 8.1 %collective-permute-start.2 = (bf16[16,4096]{1,0:T(8,128)(2,1)S(1)}, bf16[16,4096]{1,0:T(8,128)(2,1)S(1)}, u32[]{:S(2)}, u32[]{:S(2)}) collective-permute-start(bf16[16,4096]{1,0:T(8,128)(2,1)S(1)} %constant_dynamic-slice_fusion), channel_id=1, source_target_pairs={{0,4},{2,6},{4,0},{6,2},{8,12},{10,14},{12,8},{14,10},{1,5},{3,7},... | collective-permute-start | bytes 393224 | tf_op jit(solution)/shard_map/ppermute | solution.py:264
  27.4 10.1 %collective-permute-start.3 = (bf16[16,4096]{1,0:T(8,128)(2,1)S(1)}, bf16[16,4096]{1,0:T(8,128)(2,1)S(1)}, u32[]{:S(2)}, u32[]{:S(2)}) collective-permute-start(bf16[16,4096]{1,0:T(8,128)(2,1)S(1)} %constant_dynamic-slice_fusion), channel_id=1, source_target_pairs={{0,8},{2,10},{4,12},{6,14},{8,0},{10,2},{12,4},{14,6},{1,9},{3,11}... | collective-permute-start | bytes 393224 | tf_op jit(solution)/shard_map/ppermute | solution.py:264
  28.9 9.4 %collective-permute-start.4 = (bf16[16,4096]{1,0:T(8,128)(2,1)S(1)}, bf16[16,4096]{1,0:T(8,128)(2,1)S(1)}, u32[]{:S(2)}, u32[]{:S(2)}) collective-permute-start(bf16[16,4096]{1,0:T(8,128)(2,1)S(1)} %constant_dynamic-slice_fusion), channel_id=1, source_target_pairs={{0,12},{2,14},{4,8},{6,10},{8,4},{10,6},{12,0},{14,2},{1,13},{3,15... | collective-permute-start | bytes 393224 | tf_op jit(solution)/shard_map/ppermute | solution.py:264
  31.4 9.0 %copy-start.1 = (bf16[128,4096]{1,0:T(8,128)(2,1)S(1)}, bf16[128,4096]{1,0:T(8,128)(2,1)}, u32[]{:S(2)}) copy-start(bf16[128,4096]{1,0:T(8,128)(2,1)} %own_ref.10) | copy-start | bytes 3145732
  31.5 0.7 copy-start.5
  32.6 19.0 %collective-permute-start.8 = (bf16[128,2048]{1,0:T(8,128)(2,1)S(1)}, bf16[128,2048]{1,0:T(8,128)(2,1)S(1)}, u32[]{:S(2)}, u32[]{:S(2)}) collective-permute-start(bf16[128,2048]{1,0:T(8,128)(2,1)S(1)} %get-tuple-element.46), channel_id=1, source_target_pairs={{0,2},{2,0},{4,6},{6,4},{8,10},{10,8},{12,14},{14,12},{1,3},{3,1},... | collective-permute-start | bytes 1572872 | tf_op jit(solution)/shard_map/ppermute | solution.py:261
  37.5 5.0 %collective-permute-start.5 = (bf16[16,4096]{1,0:T(8,128)(2,1)S(1)}, bf16[16,4096]{1,0:T(8,128)(2,1)S(1)}, u32[]{:S(2)}, u32[]{:S(2)}) collective-permute-start(bf16[16,4096]{1,0:T(8,128)(2,1)S(1)} %collective-permute-done.2.refs_0_), channel_id=1, source_target_pairs={{0,16},{16,0},{1,17},{17,1},{2,18},{18,2},{3,19},{19,3},{4,20},{20... | collective-permute-start | bytes 393224 | tf_op jit(solution)/shard_map/ppermute | solution.py:267
  38.4 5.5 %collective-permute-start.6 = (bf16[16,4096]{1,0:T(8,128)(2,1)S(1)}, bf16[16,4096]{1,0:T(8,128)(2,1)S(1)}, u32[]{:S(2)}, u32[]{:S(2)}) collective-permute-start(bf16[16,4096]{1,0:T(8,128)(2,1)S(1)} %collective-permute-done.3.refs_1_), channel_id=1, source_target_pairs={{0,16},{16,0},{1,17},{17,1},{2,18},{18,2},{3,19},{19,3},{4,20},{20... | collective-permute-start | bytes 393224 | tf_op jit(solution)/shard_map/ppermute | solution.py:267
  39.5 5.7 %collective-permute-start.7 = (bf16[16,4096]{1,0:T(8,128)(2,1)S(1)}, bf16[16,4096]{1,0:T(8,128)(2,1)S(1)}, u32[]{:S(2)}, u32[]{:S(2)}) collective-permute-start(bf16[16,4096]{1,0:T(8,128)(2,1)S(1)} %collective-permute-done.4.refs_2_), channel_id=1, source_target_pairs={{0,16},{16,0},{1,17},{17,1},{2,18},{18,2},{3,19},{19,3},{4,20},{20... | collective-permute-start | bytes 393224 | tf_op jit(solution)/shard_map/ppermute | solution.py:267
  42.5 2.9 %collective-permute-start.16 = (f32[32,256]{1,0:T(8,128)S(1)}, f32[32,256]{1,0:T(8,128)S(1)}, u32[]{:S(2)}, u32[]{:S(2)}) collective-permute-start(f32[32,256]{1,0:T(8,128)S(1)} %shard_map.96), channel_id=1, source_target_pairs={{0,1},{1,0},{2,3},{3,2},{4,5},{5,4},{6,7},{7,6},{8,9},{9,8},{10,11... | collective-permute-start | bytes 98312 | tf_op jit(solution)/shard_map/ppermute | solution.py:270
  42.5 2.9 %copy-start = (bf16[128,4096]{1,0:T(8,128)(2,1)S(1)}, bf16[128,4096]{1,0:T(8,128)(2,1)}, u32[]{:S(2)}) copy-start(bf16[128,4096]{1,0:T(8,128)(2,1)} %own_ref.11) | copy-start | bytes 3145732
  45.8 7.5 %collective-permute-start.18 = (bf16[64,2048]{1,0:T(8,128)(2,1)S(1)}, bf16[64,2048]{1,0:T(8,128)(2,1)S(1)}, u32[]{:S(2)}, u32[]{:S(2)}) collective-permute-start(bf16[64,2048]{1,0:T(8,128)(2,1)S(1)} %get-tuple-element.29), channel_id=1, source_target_pairs={{0,4},{2,6},{4,0},{6,2},{8,12},{10,14},{12,8},{14,10},{1,5},{3,7},... | collective-permute-start | bytes 786440 | tf_op jit(solution)/shard_map/ppermute | solution.py:264
  52.1 1.3 %collective-permute-start.17 = (f32[32,256]{1,0:T(8,128)S(1)}, f32[32,256]{1,0:T(8,128)S(1)}, u32[]{:S(2)}, u32[]{:S(2)}) collective-permute-start(f32[32,256]{1,0:T(8,128)S(1)} %shard_map.99), channel_id=1, source_target_pairs={{0,1},{1,0},{2,3},{3,2},{4,5},{5,4},{6,7},{7,6},{8,9},{9,8},{10,11... | collective-permute-start | bytes 98312 | tf_op jit(solution)/shard_map/ppermute | solution.py:270
  54.5 12.0 %collective-permute-start.26 = (bf16[64,2048]{1,0:T(8,128)(2,1)S(1)}, bf16[64,2048]{1,0:T(8,128)(2,1)S(1)}, u32[]{:S(2)}, u32[]{:S(2)}) collective-permute-start(bf16[64,2048]{1,0:T(8,128)(2,1)S(1)} %get-tuple-element.39), channel_id=1, source_target_pairs={{0,4},{2,6},{4,0},{6,2},{8,12},{10,14},{12,8},{14,10},{1,5},{3,7},... | collective-permute-start | bytes 786440 | tf_op jit(solution)/shard_map/ppermute | solution.py:264
  56.2 25.8 %collective-permute-start.21 = (bf16[128,4096]{1,0:T(8,128)(2,1)S(1)}, bf16[128,4096]{1,0:T(8,128)(2,1)S(1)}, u32[]{:S(2)}, u32[]{:S(2)}) collective-permute-start(bf16[128,4096]{1,0:T(8,128)(2,1)S(1)} %shard_map.95.adapter_ref.down_ref), channel_id=1, source_target_pairs={{0,2},{2,0},{4,6},{6,4},{8,10},{10,8},{12,14},{14,12},{1,3},{3,1},... | collective-permute-start | bytes 3145736 | tf_op jit(solution)/shard_map/ppermute | solution.py:261
  56.7 33.2 %collective-permute-start.25 = (bf16[32,2048]{1,0:T(8,128)(2,1)S(1)}, bf16[32,2048]{1,0:T(8,128)(2,1)S(1)}, u32[]{:S(2)}, u32[]{:S(2)}) collective-permute-start(bf16[32,2048]{1,0:T(8,128)(2,1)S(1)} %add_convert_fusion.3), channel_id=1, source_target_pairs={{0,8},{2,10},{4,12},{6,14},{8,0},{10,2},{12,4},{14,6},{1,9},{3,11}... | collective-permute-start | bytes 393224 | tf_op jit(solution)/shard_map/ppermute | solution.py:264
  59.3 15.7 %collective-permute-start.23 = (bf16[64,2048]{1,0:T(8,128)(2,1)S(1)}, bf16[64,2048]{1,0:T(8,128)(2,1)S(1)}, u32[]{:S(2)}, u32[]{:S(2)}) collective-permute-start(bf16[64,2048]{1,0:T(8,128)(2,1)S(1)} %get-tuple-element.35), channel_id=1, source_target_pairs={{0,4},{2,6},{4,0},{6,2},{8,12},{10,14},{12,8},{14,10},{1,5},{3,7},... | collective-permute-start | bytes 786440 | tf_op jit(solution)/shard_map/ppermute | solution.py:264
  59.7 21.7 %collective-permute-start.19 = (bf16[64,2048]{1,0:T(8,128)(2,1)S(1)}, bf16[64,2048]{1,0:T(8,128)(2,1)S(1)}, u32[]{:S(2)}, u32[]{:S(2)}) collective-permute-start(bf16[64,2048]{1,0:T(8,128)(2,1)S(1)} %get-tuple-element.31), channel_id=1, source_target_pairs={{0,4},{2,6},{4,0},{6,2},{8,12},{10,14},{12,8},{14,10},{1,5},{3,7},... | collective-permute-start | bytes 786440 | tf_op jit(solution)/shard_map/ppermute | solution.py:264
  66.6 23.3 %collective-permute-start.27 = (bf16[32,2048]{1,0:T(8,128)(2,1)S(1)}, bf16[32,2048]{1,0:T(8,128)(2,1)S(1)}, u32[]{:S(2)}, u32[]{:S(2)}) collective-permute-start(bf16[32,2048]{1,0:T(8,128)(2,1)S(1)} %add_convert_fusion), channel_id=1, source_target_pairs={{0,8},{2,10},{4,12},{6,14},{8,0},{10,2},{12,4},{14,6},{1,9},{3,11}... | collective-permute-start | bytes 393224 | tf_op jit(solution)/shard_map/ppermute | solution.py:264
  75.0 14.9 %collective-permute-start.24 = (bf16[32,2048]{1,0:T(8,128)(2,1)S(1)}, bf16[32,2048]{1,0:T(8,128)(2,1)S(1)}, u32[]{:S(2)}, u32[]{:S(2)}) collective-permute-start(bf16[32,2048]{1,0:T(8,128)(2,1)S(1)} %add_convert_fusion.1), channel_id=1, source_target_pairs={{0,8},{2,10},{4,12},{6,14},{8,0},{10,2},{12,4},{14,6},{1,9},{3,11}... | collective-permute-start | bytes 393224 | tf_op jit(solution)/shard_map/ppermute | solution.py:264
  81.4 3.7 %collective-permute-start.20 = (bf16[32,128]{1,0:T(8,128)(2,1)S(1)}, bf16[32,128]{1,0:T(8,128)(2,1)S(1)}, u32[]{:S(2)}, u32[]{:S(2)}) collective-permute-start(bf16[32,128]{1,0:T(8,128)(2,1)S(1)} %slice.49), channel_id=1, source_target_pairs={{0,2},{2,0},{4,6},{6,4},{8,10},{10,8},{12,14},{14,12},{1,3},{3,1},... | collective-permute-start | bytes 24584 | tf_op jit(solution)/shard_map/ppermute | solution.py:261
  82.0 9.6 %collective-permute-start.22 = (bf16[32,2048]{1,0:T(8,128)(2,1)S(1)}, bf16[32,2048]{1,0:T(8,128)(2,1)S(1)}, u32[]{:S(2)}, u32[]{:S(2)}) collective-permute-start(bf16[32,2048]{1,0:T(8,128)(2,1)S(1)} %add_convert_fusion.2), channel_id=1, source_target_pairs={{0,8},{2,10},{4,12},{6,14},{8,0},{10,2},{12,4},{14,6},{1,9},{3,11}... | collective-permute-start | bytes 393224 | tf_op jit(solution)/shard_map/ppermute | solution.py:264
